TPU v7x, 128 devices: a whole 4x4x4 slice. The times are simulated.
128 devices in a mesh: dp: 16 (over y_hi, x, core), tensor: 8 (over z, y_lo).
Axes of the slice: x: 4, y: 4 (y_hi: 2, y_lo: 2; y = y_hi * 2 + y_lo), z: 4, core: 2. Of those that a mesh axis runs over, the one named last changes fastest.
Arguments:
- tokens: bfloat16 [16384, 2048], P(('dp', 'tensor')), may hold values from -24 to 24
- segments: int32 [16384], P('dp'), may hold values from 0 to 128, as said below
- cotangent: bfloat16 [16384, 2048], P(('dp', 'tensor')), may hold values from -24 to 24
- attn_gain: float32 [2048], P(('dp', 'tensor')), may hold values from 0.5 to 1.5
- w_query: bfloat16 [2048, 2048], P('dp', 'tensor'), may hold values from -0.125 to 0.125
- w_key: bfloat16 [2048, 2048], P('dp', 'tensor'), may hold values from -0.125 to 0.125
- w_value: bfloat16 [2048, 2048], P('dp', 'tensor'), may hold values from -0.125 to 0.125
- w_beta: bfloat16 [2048, 16], P('dp', 'tensor'), may hold values from -0.125 to 0.125
- conv_weight: bfloat16 [3, 4, 16, 128], P(None, None, 'tensor', 'dp'), may hold values from -3 to 3
- w_out: bfloat16 [2048, 2048], P('tensor', 'dp'), may hold values from -0.25 to 0.25
- ffn_gain: float32 [2048], P(('dp', 'tensor')), may hold values from 0.5 to 1.5
- w_gate: bfloat16 [2048, 5632], P('dp', 'tensor'), may hold values from -0.125 to 0.125
- w_up: bfloat16 [2048, 5632], P('dp', 'tensor'), may hold values from -0.125 to 0.125
- w_down: bfloat16 [5632, 2048], P('tensor', 'dp'), may hold values from -0.078125 to 0.078125
Outputs:
- output: bfloat16 [16384, 2048], P(('dp', 'tensor'))
- tokens_grad: float32 [16384, 2048], P(('dp', 'tensor'))
- attn_gain_grad: float32 [2048], P(('dp', 'tensor'))
- w_query_grad: float32 [2048, 2048], P('dp', 'tensor')
- w_key_grad: float32 [2048, 2048], P('dp', 'tensor')
- w_value_grad: float32 [2048, 2048], P('dp', 'tensor')
- w_beta_grad: float32 [2048, 16], P('dp', 'tensor')
- conv_weight_grad: float32 [3, 4, 16, 128], P(None, None, 'tensor', 'dp')
- w_out_grad: float32 [2048, 2048], P('tensor', 'dp')
- ffn_gain_grad: float32 [2048], P(('dp', 'tensor'))
- w_gate_grad: float32 [2048, 5632], P('dp', 'tensor')
- w_up_grad: float32 [2048, 5632], P('dp', 'tensor')
- w_down_grad: float32 [5632, 2048], P('tensor', 'dp')
Inputs may be any that keep to these rules, and one draw needn't show every extreme that they name: Within each sequence of 1024 consecutive tokens, segments start at 0 and rise by 0 or 1 from one token to the next; a rise marks a document start. Each sequence holds one document of at least 896 tokens.
All inputs are finite; a program needn't handle non-finite values.
Results may differ from a plain program's by a relative error of at most 0.02.
Values may be sent and summed in bfloat16 or wider, within the bound.
No kernel may reach another device: no remote copies, remote signals or barrier semaphores. Data moves between devices by JAX's collectives and lax.ppermute only.
A program may use at most 192 MiB of HBM per device.

v0:
```python
import jax
import jax.numpy as jnp
from jax import lax
from jax.sharding import PartitionSpec as P

SPAN = 64


EPS = 1e-06
PRECISION_FULL = lax.Precision.HIGHEST


def causal_conv(signal, conv_taps, segs):
    length = signal.shape[0]
    summed = conv_taps[0] * signal
    for offset in range(1, conv_taps.shape[0]):
        shifted = jnp.concatenate(
            [jnp.zeros((offset, signal.shape[1]), jnp.float32), signal[: length - offset]], 0
        )
        earlier = jnp.concatenate([jnp.full((offset,), -1, jnp.int32), segs[: length - offset]], 0)
        same_doc = (earlier == segs).astype(jnp.float32)[:, None]
        summed = summed + conv_taps[offset] * shifted * same_doc
    return summed


def delta_rule(queries, keys, values, beta, segs, block):
    length, heads, width = queries.shape
    count = length // block

    def blocked(array):
        return array.reshape(count, block, heads, width).transpose(0, 2, 1, 3)

    beta_blocks = beta.reshape(count, block, heads).transpose(0, 2, 1)
    seg_blocks = segs.reshape(count, block)
    previous = jnp.concatenate(
        [jnp.full((1,), -1, jnp.int32), segs[block - 1 : length - 1 : block]], 0
    )
    strict_lower = jnp.tril(jnp.ones((block, block), jnp.float32), -1)
    with_diag = jnp.tril(jnp.ones((block, block), jnp.float32), 0)
    identity = jnp.eye(block, dtype=jnp.float32)

    def advance(memory_state, items):
        current_query, current_key, v_now, b_now, s_now, prior = items
        same = (s_now[:, None] == s_now[None, :]).astype(jnp.float32)
        carried = (s_now == prior).astype(jnp.float32)
        gram = jnp.einsum("hik,hjk->hij", current_key, current_key, precision=PRECISION_FULL)
        system = identity + b_now[:, :, None] * gram * same * strict_lower
        retrieved_value = jnp.einsum(
            "jyu,jum->jym", current_key, memory_state, precision=PRECISION_FULL
        )
        target = b_now[:, :, None] * (v_now - carried[None, :, None] * retrieved_value)
        stored_value = jax.scipy.linalg.solve_triangular(
            system, target, lower=True, unit_diagonal=True
        )
        scores = (
            jnp.einsum("hik,hjk->hij", current_query, current_key, precision=PRECISION_FULL)
            * same
            * with_diag
        )
        query_output = jnp.einsum(
            "jyu,jum->jym", current_query, memory_state, precision=PRECISION_FULL
        )
        result = carried[None, :, None] * query_output + jnp.einsum(
            "hij,hjv->hiv", scores, stored_value, precision=PRECISION_FULL
        )
        closing_state = (s_now == s_now[block - 1]).astype(jnp.float32)
        state_update = jnp.einsum(
            "myq,myd->mqd",
            current_key * closing_state[None, :, None],
            stored_value,
            precision=PRECISION_FULL,
        )
        return (carried[block - 1] * memory_state + state_update, result)

    start_state = jnp.zeros((heads, width, width), jnp.float32)
    final_state, outputs = lax.scan(
        jax.checkpoint(advance),
        start_state,
        (blocked(queries), blocked(keys), blocked(values), beta_blocks, seg_blocks, previous),
    )
    return outputs.transpose(0, 2, 1, 3).reshape(length, heads * width)


def mixer(query_raw, key_raw, value_raw, beta_raw, conv_taps, segs):
    heads = beta_raw.shape[1]
    width = query_raw.shape[1] // heads
    length = query_raw.shape[0]
    conv_rows = conv_taps.reshape(3, conv_taps.shape[1], heads * width)
    queries = jax.nn.silu(causal_conv(query_raw, conv_rows[0], segs)).reshape(length, heads, width)
    keys = jax.nn.silu(causal_conv(key_raw, conv_rows[1], segs)).reshape(length, heads, width)
    values = jax.nn.silu(causal_conv(value_raw, conv_rows[2], segs)).reshape(length, heads, width)
    queries = queries * lax.rsqrt(jnp.sum(queries * queries, -1, keepdims=True) + EPS)
    keys = keys * lax.rsqrt(jnp.sum(keys * keys, -1, keepdims=True) + EPS)
    beta = jax.nn.sigmoid(beta_raw)
    return delta_rule(queries, keys, values, beta, segs, SPAN)


def inverse_rms(rows):
    return lax.rsqrt(jnp.mean(rows * rows, -1, keepdims=True) + EPS)


def norm_back(rows, scale, gain, grad):
    normed = rows * scale
    scaled = grad * gain
    rows_back = scale * (scaled - normed * jnp.mean(scaled * normed, -1, keepdims=True))
    return (rows_back, jnp.sum(grad * normed, 0))


def matmul(left, right):
    return jnp.dot(left, right, preferred_element_type=jnp.float32)


def left_product(left, right):
    return jnp.einsum("la,lb->ab", left, right, preferred_element_type=jnp.float32)


def right_product(left, right):
    return jnp.einsum("la,ba->lb", left, right, preferred_element_type=jnp.float32)


def spread_rows(rows):
    return lax.all_gather(rows, "tensor", axis=0, tiled=True)


def sum_rows(part):
    return lax.psum_scatter(
        part.astype(jnp.bfloat16), "tensor", scatter_dimension=0, tiled=True
    ).astype(jnp.float32)


def gather_grads(rows):
    return lax.all_gather(rows, "tensor", axis=0, tiled=True)


def sum_grads(part):
    return lax.psum_scatter(
        part.astype(jnp.bfloat16), "tensor", scatter_dimension=0, tiled=True
    ).astype(jnp.float32)


def on_device(
    tokens,
    segments,
    cotangent,
    attn_gain,
    w_query,
    w_key,
    w_value,
    w_beta,
    conv_weight,
    w_out,
    ffn_gain,
    w_gate,
    w_up,
    w_down,
):
    gain_one, gain_two = (
        lax.all_gather(attn_gain, ("dp", "tensor"), axis=0, tiled=True),
        lax.all_gather(ffn_gain, ("dp", "tensor"), axis=0, tiled=True),
    )
    query_w, key_w, value_w, beta_w, conv_taps, out_w = (
        lax.all_gather(w_query, "dp", axis=0, tiled=True),
        lax.all_gather(w_key, "dp", axis=0, tiled=True),
        lax.all_gather(w_value, "dp", axis=0, tiled=True),
        lax.all_gather(w_beta, "dp", axis=0, tiled=True),
        lax.all_gather(conv_weight, "dp", axis=3, tiled=True),
        lax.all_gather(w_out, "dp", axis=1, tiled=True),
    )
    gate_w, up_w, down_w = (
        lax.all_gather(w_gate, "dp", axis=0, tiled=True),
        lax.all_gather(w_up, "dp", axis=0, tiled=True),
        lax.all_gather(w_down, "dp", axis=1, tiled=True),
    )
    rows = tokens.astype(jnp.float32)
    scale_one = inverse_rms(rows)
    seq_normed = spread_rows((rows * scale_one * gain_one).astype(jnp.bfloat16))
    query_raw = matmul(seq_normed, query_w)
    key_raw = matmul(seq_normed, key_w)
    value_raw = matmul(seq_normed, value_w)
    beta_raw = matmul(seq_normed, beta_w)

    def local_mix(query_in, key_in, value_in, beta_in, taps_in):
        return mixer(query_in, key_in, value_in, beta_in, taps_in, segments)

    mixed, mix_back = jax.vjp(
        local_mix, query_raw, key_raw, value_raw, beta_raw, conv_taps.astype(jnp.float32)
    )
    mixed_low = mixed.astype(jnp.bfloat16)
    middle = rows + sum_rows(matmul(mixed_low, out_w))
    scale_two = inverse_rms(middle)
    seq_second = spread_rows((middle * scale_two * gain_two).astype(jnp.bfloat16))
    gate = matmul(seq_second, gate_w)
    up_part = matmul(seq_second, up_w)
    sigma = jax.nn.sigmoid(gate)
    swish = gate * sigma
    active = (swish * up_part).astype(jnp.bfloat16)
    result = middle + sum_rows(matmul(active, down_w))
    seq_grad = gather_grads(cotangent)
    gate_w, up_w, down_w = (
        lax.all_gather(w_gate, "dp", axis=0, tiled=True),
        lax.all_gather(w_up, "dp", axis=0, tiled=True),
        lax.all_gather(w_down, "dp", axis=1, tiled=True),
    )
    grad_down = left_product(active, seq_grad)
    grad_active = right_product(seq_grad, down_w)
    slope = sigma * (1.0 + gate * (1.0 - sigma))
    gate_back = (grad_active * up_part * slope).astype(jnp.bfloat16)
    up_back = (grad_active * swish).astype(jnp.bfloat16)
    grad_gate = left_product(seq_second, gate_back)
    grad_up = left_product(seq_second, up_back)
    seq_back = right_product(gate_back, gate_w) + right_product(up_back, up_w)
    middle_back, gain_two_grad = norm_back(middle, scale_two, gain_two, sum_grads(seq_back))
    middle_grad = cotangent.astype(jnp.float32) + middle_back
    middle_low = middle_grad.astype(jnp.bfloat16)
    query_w, key_w, value_w, beta_w, out_w = (
        lax.all_gather(w_query, "dp", axis=0, tiled=True),
        lax.all_gather(w_key, "dp", axis=0, tiled=True),
        lax.all_gather(w_value, "dp", axis=0, tiled=True),
        lax.all_gather(w_beta, "dp", axis=0, tiled=True),
        lax.all_gather(w_out, "dp", axis=1, tiled=True),
    )
    seq_middle = gather_grads(middle_low)
    grad_out = left_product(mixed_low, seq_middle)
    mixed_back = right_product(seq_middle, out_w)
    query_back, key_back, value_back, beta_back, taps_grad = mix_back(mixed_back)
    query_low = query_back.astype(jnp.bfloat16)
    key_low = key_back.astype(jnp.bfloat16)
    value_low = value_back.astype(jnp.bfloat16)
    beta_low = beta_back.astype(jnp.bfloat16)
    grad_query = left_product(seq_normed, query_low)
    grad_key = left_product(seq_normed, key_low)
    grad_value = left_product(seq_normed, value_low)
    grad_beta = left_product(seq_normed, beta_low)
    seq_first = (
        right_product(query_low, query_w)
        + right_product(key_low, key_w)
        + right_product(value_low, value_w)
        + right_product(beta_low, beta_w)
    )
    rows_back, gain_one_grad = norm_back(rows, scale_one, gain_one, sum_grads(seq_first))
    tokens_grad = middle_grad + rows_back
    final = tuple(
        (
            lax.psum_scatter(
                grad_query.astype(jnp.bfloat16), "dp", scatter_dimension=0, tiled=True
            ).astype(jnp.float32),
            lax.psum_scatter(
                grad_key.astype(jnp.bfloat16), "dp", scatter_dimension=0, tiled=True
            ).astype(jnp.float32),
            lax.psum_scatter(
                grad_value.astype(jnp.bfloat16), "dp", scatter_dimension=0, tiled=True
            ).astype(jnp.float32),
            lax.psum_scatter(
                grad_beta.astype(jnp.bfloat16), "dp", scatter_dimension=0, tiled=True
            ).astype(jnp.float32),
            lax.psum_scatter(
                taps_grad.astype(jnp.bfloat16), "dp", scatter_dimension=3, tiled=True
            ).astype(jnp.float32),
            lax.psum_scatter(
                grad_out.astype(jnp.bfloat16), "dp", scatter_dimension=1, tiled=True
            ).astype(jnp.float32),
            lax.psum_scatter(
                grad_gate.astype(jnp.bfloat16), "dp", scatter_dimension=0, tiled=True
            ).astype(jnp.float32),
            lax.psum_scatter(
                grad_up.astype(jnp.bfloat16), "dp", scatter_dimension=0, tiled=True
            ).astype(jnp.float32),
            lax.psum_scatter(
                grad_down.astype(jnp.bfloat16), "dp", scatter_dimension=1, tiled=True
            ).astype(jnp.float32),
        )
    )
    gain_sums = (
        lax.psum_scatter(gain_one_grad, ("dp", "tensor"), scatter_dimension=0, tiled=True),
        lax.psum_scatter(gain_two_grad, ("dp", "tensor"), scatter_dimension=0, tiled=True),
    )
    return (
        result.astype(jnp.bfloat16),
        tokens_grad,
        gain_sums[0],
        final[0],
        final[1],
        final[2],
        final[3],
        final[4],
        final[5],
        gain_sums[1],
        final[6],
        final[7],
        final[8],
    )


def solution(mesh):
    placed = (
        P(("dp", "tensor"), None),
        P("dp"),
        P(("dp", "tensor"), None),
        P(("dp", "tensor")),
        P("dp", "tensor"),
        P("dp", "tensor"),
        P("dp", "tensor"),
        P("dp", "tensor"),
        P(None, None, "tensor", "dp"),
        P("tensor", "dp"),
        P(("dp", "tensor")),
        P("dp", "tensor"),
        P("dp", "tensor"),
        P("tensor", "dp"),
    )
    return jax.shard_map(
        on_device,
        mesh=mesh,
        in_specs=placed,
        out_specs=(
            P(("dp", "tensor"), None),
            P(("dp", "tensor"), None),
            P(("dp", "tensor")),
            P("dp", "tensor"),
            P("dp", "tensor"),
            P("dp", "tensor"),
            P("dp", "tensor"),
            P(None, None, "tensor", "dp"),
            P("tensor", "dp"),
            P(("dp", "tensor")),
            P("dp", "tensor"),
            P("dp", "tensor"),
            P("tensor", "dp"),
        ),
        check_vma=False,
    )
```

profile of v0, /device:TPU:1, one launch (start us, length us, event | category | flops | bytes accessed | tf_op | source)
XLA Modules:
  0.0 2575.2 jit_solution(8765984202993269479)
XLA Ops:
  10.2 68.8 %all-reduce.41 = (f32[2048]{0:T(1024)S(1)}, f32[2048]{0:T(1024)S(1)}) all-reduce(f32[2048]{0:T(1024)S(1)} %dynamic-update-slice, f32[2048]{0:T(1024)S(1)} %dynamic-update-slice.1), channel_id=1, replica_groups=mesh['dp'=16,'tensor'=8] {'dp','tensor'}, use_global_device_ids=true, to_apply=%add.35 | all-reduce | flops 4096 | bytes 32768
  87.5 22.0 all_gather.57
  109.7 20.1 all_gather.53
  132.3 37.1 %all-gather.12.cloned.1.call-done = bf16[1024,2048]{1,0:T(8,128)(2,1)} async-done(((bf16[128,2048]{1,0:T(8,128)(2,1)}), bf16[1024,2048]{1,0:T(8,128)(2,1)}) %all-gather.12.cloned.1.call-update) | async-done | bytes 4194320 | tf_op jit(solution)/shard_map/all_gather | solution.py:122
  173.6 43.2 %all-gather.16.cloned.1.call-done = bf16[2048,256]{1,0:T(8,128)(2,1)} async-done(((bf16[128,256]{1,0:T(8,128)(2,1)}), bf16[2048,256]{1,0:T(8,128)(2,1)}) %all-gather.16.cloned.1.call-update) | async-done | bytes 1048592 | tf_op jit(solution)/shard_map/all_gather | solution.py:164
  224.7 38.4 %all-gather.18.cloned.1.call-done = bf16[2048,256]{1,0:T(8,128)(2,1)} async-done(((bf16[128,256]{1,0:T(8,128)(2,1)}), bf16[2048,256]{1,0:T(8,128)(2,1)}) %all-gather.18.cloned.1.call-update) | async-done | bytes 1048592 | tf_op jit(solution)/shard_map/all_gather | solution.py:162
  266.9 42.3 %all-gather.14.cloned.1.call-done = bf16[2048,256]{1,0:T(8,128)(2,1)} async-done(((bf16[128,256]{1,0:T(8,128)(2,1)}), bf16[2048,256]{1,0:T(8,128)(2,1)}) %all-gather.14.cloned.1.call-update) | async-done | bytes 1048592 | tf_op jit(solution)/shard_map/all_gather | solution.py:163
  340.4 385.6 %while.38 = (s32[]{:T(128)}, f32[2,128,128]{2,1,0:T(8,128)S(1)}, bf16[16,2,64,128]{3,2,1,0:T(8,128)(2,1)}, f32[16,2,128,128]{3,2,1,0:T(8,128)}, s32[16,64]{1,0:T...) while((s32[]{:T(128)}, f32[2,128,128]{2,1,0:T(8,128)S(1)}, ...), condition=%wide.region_4.6_spmd.clone, body=%wide.region_3.5_spmd.clone.sunk | while | flops 126234944 | bytes 2097361 | solution.py:76
  733.8 89.0 %reduce-scatter.24.cloned.1.call-done = bf16[128,2048]{1,0:T(8,128)(2,1)} async-done(((bf16[1024,2048]{1,0:T(8,128)(2,1)}), bf16[128,2048]{1,0:T(8,128)(2,1)}) %reduce-scatter.24.cloned.1.call-update) | async-done | bytes 524304 | tf_op jit(solution)/shard_map/reduce_scatter | solution.py:126
  828.8 49.6 %all-gather.26.cloned.1.call-done = bf16[2048,704]{0,1:T(8,128)(2,1)} async-done(((bf16[128,704]{0,1:T(8,128)(2,1)}), bf16[2048,704]{0,1:T(8,128)(2,1)}) %all-gather.26.cloned.1.call-update) | async-done | bytes 2883600 | tf_op jit(solution)/shard_map/all_gather | solution.py:171
  878.5 90.7 %all-gather.22.cloned.1.call-done = bf16[1024,2048]{1,0:T(8,128)(2,1)} async-done(((bf16[128,2048]{1,0:T(8,128)(2,1)}), bf16[1024,2048]{1,0:T(8,128)(2,1)}) %all-gather.22.cloned.1.call-update) | async-done | bytes 4194320 | tf_op jit(solution)/shard_map/all_gather | solution.py:122
  977.1 47.8 %all-gather.24.cloned.1.call-done = bf16[2048,704]{0,1:T(8,128)(2,1)} async-done(((bf16[128,704]{0,1:T(8,128)(2,1)}), bf16[2048,704]{0,1:T(8,128)(2,1)}) %all-gather.24.cloned.1.call-update) | async-done | bytes 2883600 | tf_op jit(solution)/shard_map/all_gather | solution.py:170
  1032.7 46.0 %all-gather.28.cloned.1.call-done = bf16[704,2048]{1,0:T(8,128)(2,1)} async-done(((bf16[704,128]{1,0:T(8,128)(2,1)}), bf16[704,2048]{1,0:T(8,128)(2,1)}) %all-gather.28.cloned.1.call-update) | async-done | bytes 2883600 | tf_op jit(solution)/shard_map/all_gather | solution.py:172
  1078.7 90.7 %all-gather.30.cloned.1.call-done = bf16[1024,2048]{1,0:T(8,128)(2,1)} async-done(((bf16[128,2048]{1,0:T(8,128)(2,1)}), bf16[1024,2048]{1,0:T(8,128)(2,1)}) %all-gather.30.cloned.1.call-update) | async-done | bytes 4194320 | tf_op jit(solution)/shard_map/all_gather | solution.py:132
  1188.8 91.4 %reduce-scatter.28.cloned.1.call-done = bf16[128,2048]{1,0:T(8,128)(2,1)} async-done(((bf16[1024,2048]{1,0:T(8,128)(2,1)}), bf16[128,2048]{1,0:T(8,128)(2,1)}) %reduce-scatter.28.cloned.1.call-update) | async-done | bytes 524304 | tf_op jit(solution)/shard_map/reduce_scatter | solution.py:136
  1327.1 49.2 %all-gather.32.cloned.1.call-done = bf16[1024,2048]{1,0:T(8,128)(2,1)} async-done(((bf16[128,2048]{1,0:T(8,128)(2,1)}), bf16[1024,2048]{1,0:T(8,128)(2,1)}) %all-gather.32.cloned.1.call-update) | async-done | bytes 4194320 | tf_op jit(solution)/shard_map/all_gather | solution.py:132
  1390.0 633.0 %while.39 = (s32[]{:T(128)}, f32[2,128,128]{2,1,0:T(8,128)S(1)}, f32[16,2,64,128]{3,2,1,0:T(8,128)}, f32[16,2,64,128]{3,2,1,0:T(8,128)}, f32[16,2,64,128]{3,2,1,...) while((s32[]{:T(128)}, f32[2,128,128]{2,1,0:T(8,128)S(1)}, ...), condition=%wide.region_13.15_spmd.clone, body=%wide.region_10.14_spmd.clone.sunk | while | flops 321548480 | bytes 6659995 | solution.py:76
  2122.4 34.0 %all-reduce.38 = bf16[3,4,2,128]{3,2,1,0:T(2,128)(2,1)S(1)} all-reduce(bf16[3,4,2,128]{3,2,1,0:T(2,128)(2,1)S(1)} %convert_element_type.250), channel_id=11, replica_groups=mesh['dp'=16,'tensor'=8] {'dp'}, use_global_device_ids=true, to_apply=%region_36.38.clone | all-reduce | flops 3072 | bytes 12288
  2167.0 68.0 %reduce-scatter.32.cloned.1.call-done = bf16[128,256]{1,0:T(8,128)(2,1)} async-done(((bf16[2048,256]{1,0:T(8,128)(2,1)}), bf16[128,256]{1,0:T(8,128)(2,1)}) %reduce-scatter.32.cloned.1.call-update) | async-done | bytes 65552 | tf_op jit(solution)/shard_map/reduce_scatter | solution.py:244
  2236.5 69.1 %reduce-scatter.34.cloned.1.call-done = bf16[128,256]{1,0:T(8,128)(2,1)} async-done(((bf16[2048,256]{1,0:T(8,128)(2,1)}), bf16[128,256]{1,0:T(8,128)(2,1)}) %reduce-scatter.34.cloned.1.call-update) | async-done | bytes 65552 | tf_op jit(solution)/shard_map/reduce_scatter | solution.py:247
  2307.1 68.2 %reduce-scatter.36.cloned.1.call-done = bf16[128,256]{1,0:T(8,128)(2,1)} async-done(((bf16[2048,256]{1,0:T(8,128)(2,1)}), bf16[128,256]{1,0:T(8,128)(2,1)}) %reduce-scatter.36.cloned.1.call-update) | async-done | bytes 65552 | tf_op jit(solution)/shard_map/reduce_scatter | solution.py:250
  2376.8 93.4 %reduce-scatter.30.cloned.1.call-done = bf16[128,2048]{1,0:T(8,128)(2,1)} async-done(((bf16[1024,2048]{1,0:T(8,128)(2,1)}), bf16[128,2048]{1,0:T(8,128)(2,1)}) %reduce-scatter.30.cloned.1.call-update) | async-done | bytes 524304 | tf_op jit(solution)/shard_map/reduce_scatter | solution.py:136
  2471.7 66.5 %all-reduce.40 = (f32[2048]{0:T(1024)S(1)}, f32[2048]{0:T(1024)S(1)}) all-reduce(f32[2048]{0:T(1024)S(1)} %get-tuple-element.624, f32[2048]{0:T(1024)S(1)} %copy-done.49), channel_id=6, replica_groups=mesh['dp'=16,'tensor'=8] {'dp','tensor'}, use_global_device_ids=true, to_apply=%region_19.21.clone | all-reduce | flops 4096 | bytes 32768
  2539.4 25.7 reduce-scatter.26.cloned.1.call-done
  (1468 shorter events, 1303.5 us)
Async XLA Ops:
  7.2 162.3 %all-gather.12.cloned.1.call-start = ((), (), s32[]{:S(2)}) async-start(), calls=%async_computation.12 | async-start | bytes 4718592 | tf_op jit(solution)/shard_map/all_gather | solution.py:122
  79.1 1203.6 %copy-start.28 = (f32[2048]{0:T(1024)}, f32[2048]{0:T(1024)S(1)}, u32[]{:S(2)}) copy-start(f32[2048]{0:T(1024)S(1)} %get-tuple-element.681) | copy-start | bytes 24580
  81.1 135.7 %all-gather.16.cloned.1.call-start = ((), (), s32[]{:S(2)}) async-start(), calls=%async_computation.14 | async-start | bytes 1114112 | tf_op jit(solution)/shard_map/all_gather | solution.py:164
  81.9 181.2 %all-gather.18.cloned.1.call-start = ((), (), s32[]{:S(2)}) async-start(), calls=%async_computation.15 | async-start | bytes 1114112 | tf_op jit(solution)/shard_map/all_gather | solution.py:162
  82.6 226.6 %all-gather.14.cloned.1.call-start = ((), (), s32[]{:S(2)}) async-start(), calls=%async_computation.13 | async-start | bytes 1114112 | tf_op jit(solution)/shard_map/all_gather | solution.py:163
  83.2 645.1 %all-gather.20.cloned.1.call-start = ((), (), s32[]{:S(2)}) async-start(), calls=%async_computation.16 | async-start | bytes 1114112 | tf_op jit(solution)/shard_map/all_gather | solution.py:167
  83.8 739.0 %reduce-scatter.24.cloned.1.call-start = ((), (), s32[]{:S(2)}) async-start(), calls=%async_computation.17 | async-start | bytes 4718592 | tf_op jit(solution)/shard_map/reduce_scatter | solution.py:126
  733.0 145.4 %all-gather.26.cloned.1.call-start = ((), (), s32[]{:S(2)}) async-start(), calls=%async_computation.20 | async-start | bytes 3063808 | tf_op jit(solution)/shard_map/all_gather | solution.py:171
  733.8 235.4 %all-gather.22.cloned.1.call-start = ((), (), s32[]{:S(2)}) async-start(), calls=%async_computation.18 | async-start | bytes 4718592 | tf_op jit(solution)/shard_map/all_gather | solution.py:122
  826.6 198.3 %all-gather.24.cloned.1.call-start = ((), (), s32[]{:S(2)}) async-start(), calls=%async_computation.19 | async-start | bytes 3063808 | tf_op jit(solution)/shard_map/all_gather | solution.py:170
  827.3 251.4 %all-gather.28.cloned.1.call-start = ((), (), s32[]{:S(2)}) async-start(), calls=%async_computation.21 | async-start | bytes 3063808 | tf_op jit(solution)/shard_map/all_gather | solution.py:172
  827.9 341.6 %all-gather.30.cloned.1.call-start = ((), (), s32[]{:S(2)}) async-start(), calls=%async_computation.23 | async-start | bytes 4718592 | tf_op jit(solution)/shard_map/all_gather | solution.py:132
  828.6 451.6 %reduce-scatter.28.cloned.1.call-start = ((), (), s32[]{:S(2)}) async-start(), calls=%async_computation.24 | async-start | bytes 4718592 | tf_op jit(solution)/shard_map/reduce_scatter | solution.py:136
  1188.8 187.6 %all-gather.32.cloned.1.call-start = ((), (), s32[]{:S(2)}) async-start(), calls=%async_computation.25 | async-start | bytes 4718592 | tf_op jit(solution)/shard_map/all_gather | solution.py:132
  1285.5 831.3 %reduce-scatter.46.cloned.1.call-start = ((), (), s32[]{:S(2)}) async-start(), calls=%async_computation.34 | async-start | bytes 3342336
  1297.5 821.1 %reduce-scatter.42.cloned.1.call-start = ((), (), s32[]{:S(2)}) async-start(), calls=%async_computation.32 | async-start | bytes 3342336
  1309.5 810.9 %reduce-scatter.44.cloned.1.call-start = ((), (), s32[]{:S(2)}) async-start(), calls=%async_computation.33 | async-start | bytes 3342336
  1326.7 830.4 %reduce-scatter.38.cloned.1.call-start = ((), (), s32[]{:S(2)}) async-start(), calls=%async_computation.30 | async-start | bytes 557056
  2031.8 133.5 %reduce-scatter.40.cloned.1.call-start = ((), (), s32[]{:S(2)}) async-start(), calls=%async_computation.31 | async-start | bytes 1114112
  2059.2 175.8 %reduce-scatter.32.cloned.1.call-start = ((), (), s32[]{:S(2)}) async-start(), calls=%async_computation.27 | async-start | bytes 1114112 | tf_op jit(solution)/shard_map/reduce_scatter | solution.py:244
  2074.6 231.0 %reduce-scatter.34.cloned.1.call-start = ((), (), s32[]{:S(2)}) async-start(), calls=%async_computation.28 | async-start | bytes 1114112 | tf_op jit(solution)/shard_map/reduce_scatter | solution.py:247
  2084.6 290.7 %reduce-scatter.36.cloned.1.call-start = ((), (), s32[]{:S(2)}) async-start(), calls=%async_computation.29 | async-start | bytes 1114112 | tf_op jit(solution)/shard_map/reduce_scatter | solution.py:250
  2091.8 378.3 %reduce-scatter.30.cloned.1.call-start = ((), (), s32[]{:S(2)}) async-start(), calls=%async_computation.26 | async-start | bytes 4718592 | tf_op jit(solution)/shard_map/reduce_scatter | solution.py:136
  2106.6 458.5 %reduce-scatter.26.cloned.1.call-start = ((), (), s32[]{:S(2)}) async-start(), calls=%async_computation.22 | async-start | bytes 4718592 | tf_op jit(solution)/shard_map/reduce_scatter | solution.py:126
  (162 other events, 8137.3 us)
Sparse Core Ops, SparseCore 0:
  81.3 88.1 all-gather.11
  171.9 44.8 all-gather.15
  219.3 43.7 all-gather.17
  265.4 43.7 all-gather.13
  311.3 45.0 all-gather.19
  733.2 89.6 reduce-scatter.23
  825.1 53.3 all-gather.25
  880.1 89.0 all-gather.21
  971.5 53.3 all-gather.23
  1027.0 51.6 all-gather.27
  1080.3 89.0 all-gather.29
  1188.9 91.2 reduce-scatter.27
  1285.6 90.7 all-gather.31
  1380.2 74.3 reduce-scatter.45
  1458.5 74.3 reduce-scatter.41
  1536.7 74.3 reduce-scatter.43
  2032.0 63.3 reduce-scatter.37
  2099.5 65.8 reduce-scatter.39
  2169.2 65.7 reduce-scatter.31
  2239.8 65.7 reduce-scatter.33
  2309.4 65.8 reduce-scatter.35
  2377.8 92.2 reduce-scatter.29
  2472.7 92.3 reduce-scatter.25
where the time goes:
time: 2600 us; the launch traced here: 2580 us
  waiting for transfers between devices  1050 us (40%)
  other arithmetic  533 us (20%)
  matrix products  482 us (19%)
  local copies, waits for them, and re-layouts  274 us (11%)
  blocking collectives  211 us (8%)
    another operation x112, other arithmetic, advance(): jax.scipy.linalg.solve_triangular(system, target, lower=True, unit_diagon...  351 us
    reduce_scatter x2, waiting for transfers between devices, sum_grads(): lax.psum_scatter(part.astype(jnp.bfloat16), 'tensor', scatter_dimension=0...  185 us
    unnamed x3, blocking collectives  169 us
    all_gather x2, waiting for transfers between devices, gather_grads(): return lax.all_gather(rows, 'tensor', axis=0, tiled=True)  140 us
    all_gather x2, waiting for transfers between devices, spread_rows(): return lax.all_gather(rows, 'tensor', axis=0, tiled=True)  128 us
    reduce_scatter x2, waiting for transfers between devices, sum_rows(): lax.psum_scatter(part.astype(jnp.bfloat16), 'tensor', scatter_dimension=0...  115 us
    squeeze x80, local copies, waits for them, and re-layouts, delta_rule(): lax.scan(jax.checkpoint(advance), start_state, (blocked(queries), blocked...  75 us
    reduce_scatter x1, waiting for transfers between devices, on_device(): lax.psum_scatter(grad_key.astype(jnp.bfloat16), 'dp', scatter_dimension=0...  69.1 us
  transfers between devices with their start and end apart: 23, of which 18 were waited for; matrix products, arithmetic and copies ran while one was open for 48% of the time, Pallas kernels for 0%

commit v1 on v0

v1 whole, which is shorter than its diff:
```python
import functools
import jax
import jax.numpy as jnp
from jax import lax
from jax.experimental import pallas as pl
from jax.experimental.pallas import tpu as pltpu
from jax.sharding import PartitionSpec as P

C = 128
EPS = 1e-06
F32 = jnp.float32
BF16 = jnp.bfloat16
NN = (((1,), (0,)), ((), ()))
NT = (((1,), (1,)), ((), ()))
TN = (((0,), (0,)), ((), ()))


def dot(left, right, dims):
    return lax.dot_general(left, right, dims, preferred_element_type=F32)


def once(left, right, dims):
    return dot(left.astype(BF16), right.astype(BF16), dims)


def halves(value):
    high = value.astype(BF16)
    return high, (value - high.astype(F32)).astype(BF16)


def fine(left, right, dims):
    left_high, left_low = halves(left)
    right_high, right_low = halves(right)
    return (
        dot(left_high, right_high, dims)
        + dot(left_high, right_low, dims)
        + dot(left_low, right_high, dims)
    )


def sigmoid(v):
    return 1.0 / (1.0 + jnp.exp(-v))


def masks():
    row = lax.broadcasted_iota(jnp.int32, (C, C), 0)
    col = lax.broadcasted_iota(jnp.int32, (C, C), 1)
    return row, col


def shifted(rows, before, offset):
    joined = jnp.concatenate([before, rows], 0)
    return pltpu.roll(joined, offset, 0)[8:]


def convolved(rows, before, taps, base, marks):
    total = taps[base : base + 1] * rows
    moved = []
    for offset in range(1, 4):
        term = shifted(rows, before, offset) * marks[offset - 1]
        moved.append(term)
        total = total + taps[base + offset : base + offset + 1] * term
    return total, moved


def inverses(systems):
    row, col = masks()
    eye = jnp.where(row == col, 1.0, 0.0)
    solved = []
    near = (row == col + 1) & ((row & 1) == 1)
    solved = [eye - jnp.where(near, a, 0.0) for a in systems]
    for level in range(1, 7):
        odd = ((row >> level) & 1) == 1
        off = odd & ((row >> level) == (col >> level) + 1)
        parts = [fine(x, jnp.where(off, a, 0.0), NN) for x, a in zip(solved, systems)]
        solved = [x - fine(p, x, NN) for x, p in zip(solved, parts)]
    return solved


def forward_kernel(chunks, mm, raw, taps, aux, segs, mixed, t_out, u_out, s_out, m_out, q_out, before, state):
    step = pl.program_id(0)

    @pl.when(step == 0)
    def _():
        before[...] = jnp.zeros_like(before)
        state[...] = jnp.zeros_like(state)

    row, col = masks()
    eye = jnp.where(row == col, 1.0, 0.0)
    taps_now = taps[...]
    items = []
    for c in range(chunks):
        rows = pl.ds(c * C, C)
        prev = before[...] if c == 0 else raw[pl.ds(c * C - 8, 8), :768]
        marks = [aux[rows, j : j + 1] for j in range(3)]
        carried, closing, seg = aux[rows, 3:4], aux[rows, 4:5], aux[rows, 5:6]
        same = seg == segs[0, c : c + 1, :]
        gamma = carried[C - 1 : C]
        acts = []
        for part in range(3):
            cols = slice(part * 256, part * 256 + 256)
            conv, _ = convolved(raw[rows, cols], prev[:, cols], taps_now, part * 4, marks)
            acts.append(conv * sigmoid(conv))
        for h in range(2):
            hc = slice(h * 128, h * 128 + 128)
            q, k, v = acts[0][:, hc], acts[1][:, hc], acts[2][:, hc]
            q = q * lax.rsqrt(jnp.sum(q * q, -1, keepdims=True) + EPS)
            k = k * lax.rsqrt(jnp.sum(k * k, -1, keepdims=True) + EPS)
            b = sigmoid(raw[rows, 768 + h : 769 + h])
            items.append((q, k, v, b, carried, closing, same, gamma))
    before[...] = raw[pl.ds(chunks * C - 8, 8), :768]
    systems, scores = [], []
    for q, k, v, b, carried, closing, same, gamma in items:
        gram = mm(k, k, NT)
        systems.append(jnp.where(same & (row > col), b * gram, 0.0))
        scores.append(jnp.where(same & (row >= col), mm(q, k, NT), 0.0))
    solved = inverses(systems)
    wus = [
        mm(t, jnp.concatenate([(i[4] * i[3]) * i[1], i[3] * i[2]], 1), NN)
        for t, i in zip(solved, items)
    ]
    mns = [mm(i[5] * i[1], wu, TN) for wu, i in zip(wus, items)]
    qos = [mm(p, wu, NN) for p, wu in zip(scores, wus)]
    for n, i in enumerate(items):
        t_out[n] = solved[n]
        c, h = n // 2, n % 2
        now = state[h]
        s_out[n] = now
        move = i[7] * eye - mns[n][:, :128]
        query = i[4] * i[0] - qos[n][:, :128]
        m_out[n] = move
        q_out[n] = query
        state[h] = mm(move, now, NN) + mns[n][:, 128:]
        u_out[n] = wus[n][:, 128:] - mm(wus[n][:, :128], now, NN)
        mixed[pl.ds(c * C, C), h * 128 : h * 128 + 128] = (mm(query, now, NN) + qos[n][:, 128:]).astype(BF16)


def mix_forward(raw, taps, aux, segs, chunks=2, mm=once):
    steps = 8 // chunks
    saved = jax.ShapeDtypeStruct((16, C, C), F32)
    block = pl.BlockSpec((2 * chunks, C, C), lambda i: (i, 0, 0))
    return pl.pallas_call(
        functools.partial(forward_kernel, chunks, mm),
        grid=(steps,),
        in_specs=[
            pl.BlockSpec((chunks * C, 896), lambda i: (i, 0)),
            pl.BlockSpec((12, 256), lambda i: (0, 0)),
            pl.BlockSpec((chunks * C, 128), lambda i: (i, 0)),
            pl.BlockSpec((1, chunks, 128), lambda i: (i, 0, 0)),
        ],
        out_specs=[pl.BlockSpec((chunks * C, 256), lambda i: (i, 0))] + [block] * 5,
        out_shape=[jax.ShapeDtypeStruct((1024, 256), BF16)] + [saved] * 5,
        scratch_shapes=[pltpu.VMEM((8, 768), F32), pltpu.VMEM((2, C, C), F32)],
        compiler_params=pltpu.CompilerParams(vmem_limit_bytes=48 * 1024 * 1024),
        name="mix_forward",
    )(raw, taps, aux, segs.reshape(steps, chunks, 128))


def backward_kernel(chunks, mm, raw, prior, taps, aux, segs, grad, t_in, u_in, s_in, m_in, q_in, back, taps_grad, after, adjoint):
    step = pl.program_id(0)
    last = pl.num_programs(0) - 1
    back[:, 768:] = jnp.zeros_like(back[:, 768:])

    @pl.when(step == 0)
    def _():
        after[...] = jnp.zeros_like(after)
        adjoint[...] = jnp.zeros_like(adjoint)
        taps_grad[...] = jnp.zeros_like(taps_grad)

    row, col = masks()
    taps_now = taps[...]
    taps_sum = [[jnp.zeros((1, 256), F32) for _ in range(4)] for _ in range(3)]
    items = []
    for c in range(chunks):
        rows = pl.ds(c * C, C)
        if c == 0:
            prev = jnp.where(step == last, 0.0, prior[:, :768])
        else:
            prev = raw[pl.ds(c * C - 8, 8), :768]
        marks = [aux[rows, j : j + 1] for j in range(3)]
        carried, closing, seg = aux[rows, 3:4], aux[rows, 4:5], aux[rows, 5:6]
        same = seg == segs[0, c : c + 1, :]
        acts, slopes, moved = [], [], []
        for part in range(3):
            cols = slice(part * 256, part * 256 + 256)
            now = raw[rows, cols]
            conv, terms = convolved(now, prev[:, cols], taps_now, part * 4, marks)
            s = sigmoid(conv)
            acts.append(conv * s)
            slopes.append(s * (1.0 + conv * (1.0 - s)))
            moved.append([now] + terms)
        heads = []
        for h in range(2):
            hc = slice(h * 128, h * 128 + 128)
            q, k, v = acts[0][:, hc], acts[1][:, hc], acts[2][:, hc]
            rq = lax.rsqrt(jnp.sum(q * q, -1, keepdims=True) + EPS)
            rk = lax.rsqrt(jnp.sum(k * k, -1, keepdims=True) + EPS)
            b = sigmoid(raw[rows, 768 + h : 769 + h])
            heads.append((q * rq, k * rk, v, b, rq, rk, grad[rows, hc]))
        items.append((marks, carried, closing, same, slopes, moved, heads))
    for c in reversed(range(chunks)):
        marks, carried, closing, same, slopes, moved, heads = items[c]
        back_q, back_k, back_v = [], [], []
        for h in range(2):
            n = 2 * c + h
            q, k, v, b, rq, rk, do = heads[h]
            t, u, s, m, qe = t_in[n], u_in[n], s_in[n], m_in[n], q_in[n]
            g = adjoint[h]
            adjoint[h] = mm(m, g, TN) + mm(qe, do, TN)
            gram = mm(k, k, NT)
            score = jnp.where(same & (row >= col), mm(q, k, NT), 0.0)
            du = mm(score, do, TN) + mm(closing * k, g, NN)
            dr = mm(t, du, TN)
            dps = mm(jnp.concatenate([do, dr], 0), u, NT)
            dp = jnp.where(same & (row >= col), dps[:C], 0.0)
            da = jnp.where(same & (row > col), -dps[C:], 0.0)
            e = b * da
            sides = mm(jnp.concatenate([carried * do, (carried * b) * dr], 0), s, NT)
            inner = mm(jnp.concatenate([dp, e], 0), k, NN)
            dq = sides[:C] + inner[:C]
            dk = (
                inner[C:]
                - sides[C:]
                + mm(jnp.concatenate([dp, e], 0), jnp.concatenate([q, k], 0), TN)
                + closing * mm(u, g, NT)
            )
            ks = mm(k, s, NN)
            db = jnp.sum(dr * (v - carried * ks) + da * gram, -1, keepdims=True)
            back_q.append(rq * (dq - q * jnp.sum(dq * q, -1, keepdims=True)))
            back_k.append(rk * (dk - k * jnp.sum(dk * k, -1, keepdims=True)))
            back_v.append(b * dr)
            back[pl.ds(c * C, C), 768 + h : 769 + h] = (db * b * (1.0 - b)).astype(BF16)
        for part, pair in enumerate((back_q, back_k, back_v)):
            d = jnp.concatenate(pair, 1) * slopes[part]
            total = taps_now[part * 4 : part * 4 + 1] * d
            taps_sum[part][0] += jnp.sum(d * moved[part][0], 0, keepdims=True)
            cols = slice(part * 256, part * 256 + 256)
            for offset in range(1, 4):
                taps_sum[part][offset] += jnp.sum(d * moved[part][offset], 0, keepdims=True)
                marked = d * marks[offset - 1]
                joined = jnp.concatenate([marked, after[offset - 1, :, cols]], 0)
                after[offset - 1, :, cols] = marked[:8]
                up = pltpu.roll(joined, C + 8 - offset, 0)[:C]
                total = total + taps_now[part * 4 + offset : part * 4 + offset + 1] * up
            back[pl.ds(c * C, C), cols] = total.astype(BF16)
    for part in range(3):
        for offset in range(4):
            r = part * 4 + offset
            taps_grad[r : r + 1, :] += taps_sum[part][offset]


def mix_backward(raw, taps, aux, segs, grad, saved, chunks=2, mm=once):
    steps = 8 // chunks
    block = pl.BlockSpec((2 * chunks, C, C), lambda i: (steps - 1 - i, 0, 0))
    rows = lambda width: pl.BlockSpec((chunks * C, width), lambda i: (steps - 1 - i, 0))
    return pl.pallas_call(
        functools.partial(backward_kernel, chunks, mm),
        grid=(steps,),
        in_specs=[
            rows(896),
            pl.BlockSpec((8, 896), lambda i: (jnp.maximum((steps - 1 - i) * chunks * 16 - 1, 0), 0)),
            pl.BlockSpec((12, 256), lambda i: (0, 0)),
            rows(128),
            pl.BlockSpec((1, chunks, 128), lambda i: (steps - 1 - i, 0, 0)),
            rows(256),
        ]
        + [block] * 5,
        out_specs=[rows(896), pl.BlockSpec((12, 256), lambda i: (0, 0))],
        out_shape=[
            jax.ShapeDtypeStruct((1024, 896), BF16),
            jax.ShapeDtypeStruct((12, 256), F32),
        ],
        scratch_shapes=[pltpu.VMEM((3, 8, 768), F32), pltpu.VMEM((2, C, C), F32)],
        compiler_params=pltpu.CompilerParams(vmem_limit_bytes=48 * 1024 * 1024),
        name="mix_backward",
    )(raw, raw, taps, aux, segs.reshape(steps, chunks, 128), grad, *saved)


def mix_marks(segs):
    marks = [
        jnp.concatenate([jnp.zeros((o,), F32), (segs[o:] == segs[:-o]).astype(F32)])
        for o in range(1, 4)
    ]
    blocks = segs.reshape(8, C)
    prior = jnp.concatenate([jnp.full((1,), -1, jnp.int32), blocks[:-1, -1]])
    carried = (blocks == prior[:, None]).astype(F32).reshape(1024)
    closing = (blocks == blocks[:, -1:]).astype(F32).reshape(1024)
    columns = jnp.stack(marks + [carried, closing, segs.astype(F32)], 1)
    return jnp.pad(columns, ((0, 0), (0, 122))), blocks.astype(F32)


AXES = ("yh", "x", "c", "z", "yl")
TEAM = ("z", "c")
RING = ("yh", "yl", "x")
PAD = 768
HID = 704


def trade(value):
    return lax.ppermute(value, ("c", "yl"), [(0, 0), (1, 2), (2, 1), (3, 3)])


def mate(value):
    return lax.ppermute(value, "c", [(0, 1), (1, 0)])


def ordered(rows):
    count = rows.shape[0]
    return rows.reshape(count, 2, 4, 2, 128).transpose(0, 1, 3, 2, 4).reshape(count, 2048)


def restored(rows):
    count = rows.shape[0]
    return rows.reshape(count, 2, 2, 4, 128).transpose(0, 1, 3, 2, 4).reshape(count, 2048)


def gather_team(rows):
    return lax.all_gather(rows, TEAM, axis=0, tiled=True)


def sum_team(part):
    return lax.psum_scatter(part, TEAM, scatter_dimension=0, tiled=True).astype(F32)


def gather_ring(rows):
    return lax.all_gather(rows, RING, axis=0, tiled=True)


def sum_ring(part):
    return lax.psum_scatter(part, RING, scatter_dimension=0, tiled=True)


def matmul(left, right, dims, kind=F32):
    return lax.dot_general(left, right, dims, preferred_element_type=F32).astype(kind)


def inverse_rms(rows):
    return lax.rsqrt(jnp.mean(rows * rows, -1, keepdims=True) + EPS)


def norm_back(normed, scale, scaled):
    return scale * (scaled - normed * jnp.mean(scaled * normed, -1, keepdims=True))


def on_device(
    tokens,
    segments,
    cotangent,
    attn_gain,
    w_query,
    w_key,
    w_value,
    w_beta,
    conv_weight,
    w_out,
    ffn_gain,
    w_gate,
    w_up,
    w_down,
):
    gains = jnp.broadcast_to(jnp.stack([attn_gain, ffn_gain])[None], (8, 2, 16))
    gains = lax.all_to_all(gains, ("z", "yl"), 0, 0, tiled=True).transpose(1, 0, 2).reshape(2, 128, 1)
    gain_one, gain_two = gains[0], gains[1]

    rows = ordered(trade(tokens)).astype(F32)
    scale_one = inverse_rms(rows)
    normed_one = rows * scale_one
    seq_one = gather_team(normed_one.astype(BF16))

    def scaled(weight, gain):
        return (weight.astype(F32) * gain).astype(BF16)

    taps_block = jnp.pad(conv_weight.reshape(24, 8), ((0, 104), (0, 112)))
    small = jnp.concatenate([jnp.pad(scaled(w_beta, gain_one), ((0, 0), (0, 6))), taps_block], 1)
    mix_pack = jnp.concatenate(
        [scaled(w, gain_one) for w in (w_query, w_key, w_value)] + [small, w_out.T], 1
    )
    wide = ((0, 0), (0, PAD - HID))
    ffn_pack = jnp.concatenate(
        [jnp.pad(scaled(w, gain_two), wide) for w in (w_gate, w_up)] + [jnp.pad(w_down.T, wide)], 1
    )
    mix_w = gather_ring(trade(mix_pack))
    in_w, out_w = mix_w[:, :896], mix_w[:, 896:]
    ffn_w = gather_ring(trade(ffn_pack))
    gate_up_w, down_w = ffn_w[:, : 2 * PAD], ffn_w[:, 2 * PAD :]
    taps = in_w[:, 768:].reshape(2, 2, 4, 128, 128)[:, :, :, :24, 8:16]
    taps = taps.transpose(3, 0, 2, 1, 4).reshape(12, 256).astype(F32)
    own = lax.axis_index("c") == lax.axis_index("yl")
    segs = jnp.where(own, segments, mate(segments))
    marks, seg_rows = mix_marks(segs)

    raw = matmul(seq_one, in_w, NN)
    mixed, *saved = mix_forward(raw, taps, marks, seg_rows, chunks=4, mm=fine)
    middle = rows + sum_team(matmul(mixed, out_w, NT, BF16))
    scale_two = inverse_rms(middle)
    normed_two = middle * scale_two
    seq_two = gather_team(normed_two.astype(BF16))
    grad_rows = ordered(trade(cotangent))
    seq_grad = gather_team(grad_rows)
    grad_active = matmul(seq_grad, down_w, NN)
    gate_up = matmul(seq_two, gate_up_w, NN)
    gate, up_part = gate_up[:, :PAD], gate_up[:, PAD:]
    sigma = sigmoid(gate)
    swish = gate * sigma
    active = (swish * up_part).astype(BF16)
    slope = sigma * (1.0 + gate * (1.0 - sigma))
    both_back = jnp.concatenate([grad_active * up_part * slope, grad_active * swish], 1).astype(BF16)
    second = sum_team(matmul(both_back, gate_up_w, NT, BF16))
    middle_grad = grad_rows.astype(F32) + norm_back(normed_two, scale_two, second)
    seq_middle = gather_team(middle_grad.astype(BF16))
    result = middle + sum_team(matmul(active, down_w, NT, BF16))
    output = trade(restored(result.astype(BF16)))
    ffn_grad = jnp.concatenate([matmul(seq_two, both_back, TN, BF16), matmul(seq_grad, active, TN, BF16)], 1)
    ffn_grad = trade(sum_ring(ffn_grad)).astype(F32)

    mixed_back = matmul(seq_middle, out_w, NN)
    back, taps_grad = mix_backward(raw, taps, marks, seg_rows, mixed_back, saved, chunks=2, mm=fine)
    first = sum_team(matmul(back, in_w, NT, BF16))
    tokens_grad = middle_grad + norm_back(normed_one, scale_one, first)
    tokens_grad = trade(restored(tokens_grad.astype(BF16))).astype(F32)
    taps_grad = taps_grad.reshape(24, 2, 4, 2, 8).transpose(1, 3, 2, 0, 4).reshape(16, 24, 8).astype(BF16)
    taps_grad = jnp.pad(taps_grad, ((0, 0), (0, 104), (8, 112))).reshape(2048, 128)
    in_grad = matmul(seq_one, back, TN, BF16)
    mix_grad = jnp.concatenate(
        [in_grad[:, :768], in_grad[:, 768:] + taps_grad, matmul(seq_middle, mixed, TN, BF16)], 1
    )
    mix_grad = trade(sum_ring(mix_grad)).astype(F32)

    grad_query, grad_key, grad_value = (mix_grad[:, n * 256 : n * 256 + 256] for n in range(3))
    grad_beta, grad_taps, grad_out = mix_grad[:, 768:770], mix_grad[:24, 776:784], mix_grad[:, 896:]
    grad_gate, grad_up, grad_down = (ffn_grad[:, n * PAD : n * PAD + HID] for n in range(3))

    def dotted(pairs):
        return sum(jnp.sum(grad * weight.astype(F32), 1) for grad, weight in pairs)

    gain_parts = jnp.stack(
        [
            dotted([(grad_query, w_query), (grad_key, w_key), (grad_value, w_value), (grad_beta, w_beta)]),
            dotted([(grad_gate, w_gate), (grad_up, w_up)]),
        ]
    )
    gain_parts = gain_parts.reshape(2, 8, 16).transpose(1, 0, 2)
    gain_sums = jnp.sum(lax.all_to_all(gain_parts, ("z", "yl"), 0, 0, tiled=True), 0)
    return (
        output,
        tokens_grad,
        gain_sums[0],
        grad_query * gain_one,
        grad_key * gain_one,
        grad_value * gain_one,
        grad_beta * gain_one,
        grad_taps.reshape(3, 4, 2, 8),
        grad_out.T,
        gain_sums[1],
        grad_gate * gain_two,
        grad_up * gain_two,
        grad_down.T,
    )


def solution(mesh):
    dp, tensor = ("yh", "x", "c"), ("z", "yl")
    every = dp + tensor
    split = jax.sharding.Mesh(mesh.devices.reshape(2, 4, 2, 4, 2), AXES)
    placed = (
        P(every, None),
        P(dp),
        P(every, None),
        P(every),
        P(dp, tensor),
        P(dp, tensor),
        P(dp, tensor),
        P(dp, tensor),
        P(None, None, tensor, dp),
        P(tensor, dp),
        P(every),
        P(dp, tensor),
        P(dp, tensor),
        P(tensor, dp),
    )
    return jax.shard_map(
        on_device,
        mesh=split,
        in_specs=placed,
        out_specs=(
            P(every, None),
            P(every, None),
            P(every),
            P(dp, tensor),
            P(dp, tensor),
            P(dp, tensor),
            P(dp, tensor),
            P(None, None, tensor, dp),
            P(tensor, dp),
            P(every),
            P(dp, tensor),
            P(dp, tensor),
            P(tensor, dp),
        ),
        check_vma=False,
    )
```

time: 2600 us -> 738 us (0.28)
  waiting for transfers between devices: 1050 us -> 449 us
  other arithmetic: 533 us -> 34.3 us
  matrix products: 482 us -> 85.1 us
  local copies, waits for them, and re-layouts: 274 us -> 57.6 us
  blocking collectives: 211 us -> 0 us
  starting transfers between devices: 2.14 us -> 47.3 us
  Pallas kernels: 0 us -> 41.9 us
    reduce_scatter x7 -> x4, waiting for transfers between devices: 505 us -> 111 us  [sum_team(): lax.psum_scatter(part, TEAM, scatter_dimension=0, tiled=True).astype(F32)]
    another operation x128 -> x4, other arithmetic: 351 us -> 0.92 us  [the longest x1 0.68 us: on_device(): gains = jnp.broadcast_to(jnp.stack([attn_gain, ffn_gain])[None], (8, 2, 16))]
    all_gather x11 -> x6, waiting for transfers between devices: 535 us -> 193 us  [the longest x2 103 us: gather_ring(): return lax.all_gather(rows, RING, axis=0, tiled=True)]
    dot_general x376 -> x12, matrix products: 425 us -> 85.1 us  [matmul(): lax.dot_general(left, right, dims, preferred_element_type=F32).astype(kind)]
    unnamed x3 -> x0, blocking collectives: 169 us -> none
    unnamed x28 -> x14, waiting for transfers between devices: 12.2 us -> 103 us
    squeeze x80 -> x1, local copies, waits for them, and re-layouts: 75 us -> 0.52 us  [on_device(): gain_sums[1]]
    convert_element_type x110 -> x13, other arithmetic: 80.3 us -> 10.8 us  [the longest x2 3.73 us: on_device(): tokens_grad = trade(restored(tokens_grad.astype(BF16))).astype(F32)]
  transfers between devices with their start and end apart: 23 -> 23, of which waited for: 18 -> 19; matrix products, arithmetic and copies ran while one was open for 48% -> 17% of each run, Pallas kernels for 0% -> 4%
where the time goes in v1:
time: 738 us; the launch traced here: 730 us
  waiting for transfers between devices  449 us (61%)
  matrix products  85.1 us (12%)
  local copies, waits for them, and re-layouts  57.6 us (8%)
  starting transfers between devices  47.3 us (6%)
  Pallas kernels  41.9 us (6%)
  other arithmetic  34.3 us (5%)
  between operations  15.1 us (2%)
    reduce_scatter x4, waiting for transfers between devices, sum_team(): lax.psum_scatter(part, TEAM, scatter_dimension=0, tiled=True).astype(F32)  111 us
    unnamed x14, waiting for transfers between devices  103 us
    all_gather x2, waiting for transfers between devices, gather_ring(): return lax.all_gather(rows, RING, axis=0, tiled=True)  103 us
    all_gather x4, waiting for transfers between devices, gather_team(): return lax.all_gather(rows, TEAM, axis=0, tiled=True)  90.4 us
    dot_general x12, matrix products, matmul(): lax.dot_general(left, right, dims, preferred_element_type=F32).astype(kind)  85.1 us
    ppermute x8, waiting for transfers between devices, trade(): return lax.ppermute(value, ('c', 'yl'), [(0, 0), (1, 2), (2, 1), (3, 3)])  40.2 us
    unnamed x83, local copies, waits for them, and re-layouts  38.2 us
    ppermute x8, starting transfers between devices, trade(): return lax.ppermute(value, ('c', 'yl'), [(0, 0), (1, 2), (2, 1), (3, 3)])  35.7 us
  transfers between devices with their start and end apart: 23, of which 19 were waited for; matrix products, arithmetic and copies ran while one was open for 17% of the time, Pallas kernels for 4%

profile of v1, /device:TPU:1, one launch (start us, length us, event | category | flops | bytes accessed | tf_op | source)
XLA Modules:
  0.0 730.1 jit_solution(15948603333427986178)
XLA Ops:
  47.8 42.9 %all-gather.9.cloned.1.call-done = bf16[2048,1152]{0,1:T(8,128)(2,1)} async-done(((bf16[128,1152]{0,1:T(8,128)(2,1)}), bf16[2048,1152]{0,1:T(8,128)(2,1)}) %all-gather.9.cloned.1.call-update) | async-done | bytes 4718608 | tf_op jit(solution)/shard_map/all_gather | solution.py:326
  92.7 33.4 %all-gather.7.cloned.1.call-done = bf16[1024,2048]{1,0:T(8,128)(2,1)} async-done(((bf16[128,2048]{1,0:T(8,128)(2,1)}), bf16[1024,2048]{1,0:T(8,128)(2,1)}) %all-gather.7.cloned.1.call-update) | async-done | bytes 4194320 | tf_op jit(solution)/shard_map/all_gather | solution.py:318
  126.1 9.6 %fusion.8.raw.prior = f32[1024,896]{1,0:T(8,128)} fusion(bf16[1024,2048]{1,0:T(8,128)(2,1)} %all-gather.7.cloned.1.call-done, bf16[2048,1152]{0,1:T(8,128)(2,1)} %all-gather.9.cloned.1.call-done), kind=kOutput, calls=%fused_computation.14 | convolution fusion | flops 3758096384 | bytes 11534336 | tf_op jit(solution)/shard_map/dot_general | solution.py:334
  135.7 16.3 %mix_forward.1 = (bf16[1024,256]{1,0:T(8,128)(2,1)S(1)}, f32[16,128,128]{2,1,0:T(8,128)S(1)}, f32[16,128,128]{2,1,0:T(8,128)S(1)}, f32[16,128,128]{2,1,0:T(8,128...) custom-call(f32[1024,896]{1,0:T(8,128)} %fusion.8.raw.prior, f32[12,256]{1,0:T(8,128)S(1)} %reshape.208.taps, ...), custom_call_target="tpu_custom_call" | custom-call | tf_op jit(solution)/shard_map/mix_forward/pallas_call | solution.py:142
  163.1 8.3 %collective-permute-done.3 = bf16[128,2304]{0,1:T(8,128)(2,1)} collective-permute-done((bf16[128,2304]{0,1:T(8,128)(2,1)S(1)}, bf16[128,2304]{0,1:T(8,128)(2,1)}, u32[]{:S(2)}, u32[]{:S(2)}) %collective-permute-start.3) | collective-permute-done | bytes 589856 | tf_op jit(solution)/shard_map/ppermute | solution.py:300
  171.5 21.9 %reduce-scatter.11.cloned.1.call-done = bf16[128,2048]{1,0:T(8,128)(2,1)} async-done(((bf16[1024,2048]{1,0:T(8,128)(2,1)}), bf16[128,2048]{1,0:T(8,128)(2,1)}) %reduce-scatter.11.cloned.1.call-update) | async-done | bytes 524304 | tf_op jit(solution)/shard_map/reduce_scatter | solution.py:322
  204.0 9.6 %collective-permute-done.5 = bf16[128,2048]{1,0:T(8,128)(2,1)} collective-permute-done((bf16[128,2048]{1,0:T(8,128)(2,1)}, bf16[128,2048]{1,0:T(8,128)(2,1)}, u32[]{:S(2)}, u32[]{:S(2)}) %collective-permute-start.5) | collective-permute-done | bytes 524320 | tf_op jit(solution)/shard_map/ppermute | solution.py:300
  220.2 59.6 %all-gather.13.cloned.1.call-done = bf16[2048,2304]{0,1:T(8,128)(2,1)} async-done(((bf16[128,2304]{0,1:T(8,128)(2,1)}), bf16[2048,2304]{0,1:T(8,128)(2,1)}) %all-gather.13.cloned.1.call-update) | async-done | bytes 9437200 | tf_op jit(solution)/shard_map/all_gather | solution.py:326
  279.8 35.2 %all-gather.11.cloned.1.call-done = bf16[1024,2048]{1,0:T(8,128)(2,1)} async-done(((bf16[128,2048]{1,0:T(8,128)(2,1)}), bf16[1024,2048]{1,0:T(8,128)(2,1)}) %all-gather.11.cloned.1.call-update) | async-done | bytes 4194320 | tf_op jit(solution)/shard_map/all_gather | solution.py:318
  315.0 11.9 %fusion.2 = f32[1024,1536]{1,0:T(8,128)} fusion(bf16[1024,2048]{1,0:T(8,128)(2,1)} %all-gather.11.cloned.1.call-done, bf16[2048,2304]{0,1:T(8,128)(2,1)} %all-gather.13.cloned.1.call-done), kind=kOutput, calls=%fused_computation.4 | convolution fusion | flops 6442450944 | bytes 16777216 | tf_op jit(solution)/shard_map/dot_general | solution.py:334
  326.9 21.8 %all-gather.15.cloned.1.call-done = bf16[1024,2048]{1,0:T(8,128)(2,1)} async-done(((bf16[128,2048]{1,0:T(8,128)(2,1)}), bf16[1024,2048]{1,0:T(8,128)(2,1)}) %all-gather.15.cloned.1.call-update) | async-done | bytes 4194320 | tf_op jit(solution)/shard_map/all_gather | solution.py:318
  348.7 10.7 %fusion.11 = (bf16[1024,768]{1,0:T(8,128)(2,1)S(1)}, bf16[1024,768]{1,0:T(8,128)(2,1)S(1)}, bf16[1024,768]{1,0:T(8,128)(2,1)}) fusion(f32[1024,1536]{1,0:T(8,128)} %fusion.2, bf16[1024,2048]{1,0:T(8,128)(2,1)} %all-gather.15.cloned.1.call-done, bf16[2048,2304]{0,1:T(8,128)(2,1)} %all-gather.13.cloned.1.call-done), kind=kOutput, calls=%fused_computation.20 | convolution fusion | flops 3233021952 | bytes 18350080 | tf_op jit(solution)/shard_map/dot_general | solution.py:334
  361.1 8.2 %fusion.4 = bf16[1024,2048]{1,0:T(8,128)(2,1)} fusion(bf16[2048,2304]{0,1:T(8,128)(2,1)S(1)} %copy-done.23, bf16[1024,768]{1,0:T(8,128)(2,1)S(1)} %get-tuple-element.104, bf16[1024,768]{1,0:T(8,128)(2,1)S(1)} %get-tuple-element.103), kind=kOutput, calls=%fused_computation.7 | convolution fusion | flops 6450839552 | bytes 13631488 | tf_op jit(solution)/shard_map/dot_general | solution.py:334
  369.4 34.5 %reduce-scatter.15.cloned.1.call-done = bf16[128,2048]{1,0:T(8,128)(2,1)} async-done(((bf16[1024,2048]{1,0:T(8,128)(2,1)}), bf16[128,2048]{1,0:T(8,128)(2,1)}) %reduce-scatter.15.cloned.1.call-update) | async-done | bytes 524304 | tf_op jit(solution)/shard_map/reduce_scatter | solution.py:322
  415.3 7.8 %convolution_convert_fusion = bf16[2048,1536]{0,1:T(8,128)(2,1)S(1)} fusion(bf16[1024,2048]{1,0:T(8,128)(2,1)S(1)} %copy-done.24, bf16[1024,768]{1,0:T(8,128)(2,1)S(1)} %copy-done.31, bf16[1024,768]{1,0:T(8,128)(2,1)S(1)} %copy-done.29), kind=kOutput, calls=%fused_computation.1 | convolution fusion | flops 6451888128 | bytes 13631488 | tf_op jit(solution)/shard_map/dot_general | solution.py:334
  423.1 11.3 %pad_maximum_fusion = bf16[2048,2304]{0,1:T(8,128)(2,1)} fusion(bf16[2048,768]{0,1:T(8,128)(2,1)S(1)} %fusion.14, bf16[2048,1536]{0,1:T(8,128)(2,1)S(1)} %convolution_convert_fusion), kind=kLoop, calls=%fused_computation | loop fusion | flops 18874368 | bytes 18874368 | tf_op jit(solution)/shard_map/concatenate | solution.py:413
  434.4 12.7 %copy.123 = bf16[2048,2304]{1,0:T(8,128)(2,1)} copy(bf16[2048,2304]{0,1:T(8,128)(2,1)} %pad_maximum_fusion) | data formatting | bytes 18874368
  451.5 25.6 %mix_backward.1 = (bf16[1024,896]{1,0:T(8,128)(2,1)}, f32[12,256]{1,0:T(8,128)S(1)}) custom-call(f32[1024,896]{1,0:T(8,128)} %fusion.8.raw.prior, f32[1024,896]{1,0:T(8,128)} %fusion.8.raw.prior, f32[12,256]{1,0:T(8,128)S(1)} %reshape.208.taps, f32[1024,128]{1,0:T(8,128)S(1)} %pad.32.aux, f32[4,2,128]{2,1,0:T(2,128)S(1)} %bitcast.82, ...), custom_call_target="tpu_custom_call" | custom-call | tf_op jit(solution)/shard_map/mix_backward/pallas_call | solution.py:256
  477.1 7.6 %convolution_convert_fusion.3 = bf16[1024,2048]{1,0:T(8,128)(2,1)} fusion(bf16[1024,896]{1,0:T(8,128)(2,1)} %get-tuple-element.27, bf16[2048,1152]{0,1:T(8,128)(2,1)S(1)} %bitcast.90), kind=kOutput, calls=%fused_computation.10 | convolution fusion | flops 3760193536 | bytes 9699328 | tf_op jit(solution)/shard_map/dot_general | solution.py:334
  514.0 21.5 %reduce-scatter.21.cloned.1.call-done = bf16[128,2304]{1,0:T(8,128)(2,1)} async-done(((bf16[2048,2304]{1,0:T(8,128)(2,1)}), bf16[128,2304]{1,0:T(8,128)(2,1)}) %reduce-scatter.21.cloned.1.call-update) | async-done | bytes 589840
  541.9 7.8 %collective-permute-done.8 = bf16[128,2304]{0,1:T(8,128)(2,1)S(1)} collective-permute-done((bf16[128,2304]{0,1:T(8,128)(2,1)}, bf16[128,2304]{0,1:T(8,128)(2,1)S(1)}, u32[]{:S(2)}, u32[]{:S(2)}) %collective-permute-start.8) | collective-permute-done | bytes 589856 | tf_op jit(solution)/shard_map/ppermute | solution.py:300
  550.9 22.5 %reduce-scatter.17.cloned.1.call-done = bf16[128,2048]{1,0:T(8,128)(2,1)} async-done(((bf16[1024,2048]{1,0:T(8,128)(2,1)}), bf16[128,2048]{1,0:T(8,128)(2,1)}) %reduce-scatter.17.cloned.1.call-update) | async-done | bytes 524304 | tf_op jit(solution)/shard_map/reduce_scatter | solution.py:322
  574.7 80.9 %reduce-scatter.19.cloned.1.call-done = bf16[128,1152]{1,0:T(8,128)(2,1)} async-done(((bf16[2048,1152]{1,0:T(8,128)(2,1)}), bf16[128,1152]{1,0:T(8,128)(2,1)}) %reduce-scatter.19.cloned.1.call-update) | async-done | bytes 294928
  662.5 31.8 %reduce-scatter.13.cloned.1.call-done = bf16[128,2048]{1,0:T(8,128)(2,1)} async-done(((bf16[1024,2048]{1,0:T(8,128)(2,1)}), bf16[128,2048]{1,0:T(8,128)(2,1)}) %reduce-scatter.13.cloned.1.call-update) | async-done | bytes 524304 | tf_op jit(solution)/shard_map/reduce_scatter | solution.py:322
  (211 shorter events, 161.7 us)
Async XLA Ops:
  8.5 11.9 %all-to-all-start = ((f32[8,2,16]{2,1,0:T(2,128)}), f32[8,2,16]{2,1,0:T(2,128)S(1)}, u32[]{:S(2)}, u32[]{:S(2)}) async-start(f32[8,2,16]{2,1,0:T(2,128)} %broadcast_in_dim.2), calls=%async_computation | async-start | bytes 16384 | tf_op jit(solution)/shard_map/all_to_all | solution.py:362
  15.3 75.4 %all-gather.9.cloned.1.call-start = ((), (), s32[]{:S(2)}) async-start(), calls=%async_computation.9 | async-start | bytes 5013504 | tf_op jit(solution)/shard_map/all_gather | solution.py:326
  22.1 8.6 %collective-permute-start.1 = (bf16[128,1152]{0,1:T(8,128)(2,1)S(1)}, bf16[128,1152]{0,1:T(8,128)(2,1)S(1)}, u32[]{:S(2)}, u32[]{:S(2)}) collective-permute-start(bf16[128,1152]{0,1:T(8,128)(2,1)S(1)} %bitcast_dynamic-update-slice_fusion), channel_id=1, source_target_pairs={{0,0},{1,8},{8,1},{9,9},{2,2},{3,10},{10,3},{11,11},{4,4},{5,12},{... | collective-permute-start | bytes 884744 | tf_op jit(solution)/shard_map/ppermute | solution.py:300
  31.5 94.6 %all-gather.7.cloned.1.call-start = ((), (), s32[]{:S(2)}) async-start(), calls=%async_computation.8 | async-start | bytes 4718592 | tf_op jit(solution)/shard_map/all_gather | solution.py:318
  31.5 10.7 %collective-permute-start = (bf16[128,2048]{1,0:T(8,128)(2,1)}, bf16[128,2048]{1,0:T(8,128)(2,1)S(1)}, u32[]{:S(2)}, u32[]{:S(2)}) collective-permute-start(bf16[128,2048]{1,0:T(8,128)(2,1)} %param.14), channel_id=1, source_target_pairs={{0,0},{1,8},{8,1},{9,9},{2,2},{3,10},{10,3},{11,11},{4,4},{5,12},{... | collective-permute-start | bytes 1572872 | tf_op jit(solution)/shard_map/ppermute | solution.py:300
  45.2 148.2 %reduce-scatter.11.cloned.1.call-start = ((), (), s32[]{:S(2)}) async-start(), calls=%async_computation.10 | async-start | bytes 4718592 | tf_op jit(solution)/shard_map/reduce_scatter | solution.py:322
  45.2 1.2 collective-permute-start.2
  158.6 121.2 %all-gather.13.cloned.1.call-start = ((), (), s32[]{:S(2)}) async-start(), calls=%async_computation.12 | async-start | bytes 10027008 | tf_op jit(solution)/shard_map/all_gather | solution.py:326
  159.8 11.6 %collective-permute-start.3 = (bf16[128,2304]{0,1:T(8,128)(2,1)S(1)}, bf16[128,2304]{0,1:T(8,128)(2,1)}, u32[]{:S(2)}, u32[]{:S(2)}) collective-permute-start(bf16[128,2304]{0,1:T(8,128)(2,1)S(1)} %fusion.33), channel_id=1, source_target_pairs={{0,0},{1,8},{8,1},{9,9},{2,2},{3,10},{10,3},{11,11},{4,4},{5,12},{... | collective-permute-start | bytes 1769480 | tf_op jit(solution)/shard_map/ppermute | solution.py:300
  171.4 143.6 %all-gather.11.cloned.1.call-start = ((), (), s32[]{:S(2)}) async-start(), calls=%async_computation.11 | async-start | bytes 4718592 | tf_op jit(solution)/shard_map/all_gather | solution.py:318
  197.3 151.4 %all-gather.15.cloned.1.call-start = ((), (), s32[]{:S(2)}) async-start(), calls=%async_computation.14 | async-start | bytes 4718592 | tf_op jit(solution)/shard_map/all_gather | solution.py:318
  197.3 16.3 %collective-permute-start.5 = (bf16[128,2048]{1,0:T(8,128)(2,1)}, bf16[128,2048]{1,0:T(8,128)(2,1)}, u32[]{:S(2)}, u32[]{:S(2)}) collective-permute-start(bf16[128,2048]{1,0:T(8,128)(2,1)} %param.16), channel_id=1, source_target_pairs={{0,0},{1,8},{8,1},{9,9},{2,2},{3,10},{10,3},{11,11},{4,4},{5,12},{... | collective-permute-start | bytes 1572872 | tf_op jit(solution)/shard_map/ppermute | solution.py:300
  220.1 183.8 %reduce-scatter.15.cloned.1.call-start = ((), (), s32[]{:S(2)}) async-start(), calls=%async_computation.15 | async-start | bytes 4718592 | tf_op jit(solution)/shard_map/reduce_scatter | solution.py:322
  369.3 78.2 %all-gather.17.cloned.1.call-start = ((), (), s32[]{:S(2)}) async-start(), calls=%async_computation.16 | async-start | bytes 4718592 | tf_op jit(solution)/shard_map/all_gather | solution.py:318
  408.6 126.8 %reduce-scatter.21.cloned.1.call-start = ((), (), s32[]{:S(2)}) async-start(), calls=%async_computation.19 | async-start | bytes 10027008
  447.1 126.3 %reduce-scatter.17.cloned.1.call-start = ((), (), s32[]{:S(2)}) async-start(), calls=%async_computation.17 | async-start | bytes 4718592 | tf_op jit(solution)/shard_map/reduce_scatter | solution.py:322
  484.8 170.8 %reduce-scatter.19.cloned.1.call-start = ((), (), s32[]{:S(2)}) async-start(), calls=%async_computation.18 | async-start | bytes 5013504
  505.7 188.5 %reduce-scatter.13.cloned.1.call-start = ((), (), s32[]{:S(2)}) async-start(), calls=%async_computation.13 | async-start | bytes 4718592 | tf_op jit(solution)/shard_map/reduce_scatter | solution.py:322
  513.9 180.3 %copy-start.6 = (bf16[128,2048]{1,0:T(8,128)(2,1)S(1)}, bf16[128,2048]{1,0:T(8,128)(2,1)}, u32[]{:S(2)}) copy-start(bf16[128,2048]{1,0:T(8,128)(2,1)} %reduce-scatter.11.cloned.1.call-done) | copy-start | bytes 1572868
  537.6 12.1 %collective-permute-start.8 = (bf16[128,2304]{0,1:T(8,128)(2,1)}, bf16[128,2304]{0,1:T(8,128)(2,1)S(1)}, u32[]{:S(2)}, u32[]{:S(2)}) collective-permute-start(bf16[128,2304]{0,1:T(8,128)(2,1)} %copy.124), channel_id=1, source_target_pairs={{0,0},{1,8},{8,1},{9,9},{2,2},{3,10},{10,3},{11,11},{4,4},{5,12},{... | collective-permute-start | bytes 1769480 | tf_op jit(solution)/shard_map/ppermute | solution.py:300
  657.4 51.8 %collective-permute-start.7 = (bf16[128,1152]{0,1:T(8,128)(2,1)}, bf16[128,1152]{0,1:T(8,128)(2,1)S(1)}, u32[]{:S(2)}, u32[]{:S(2)}) collective-permute-start(bf16[128,1152]{0,1:T(8,128)(2,1)} %copy.122), channel_id=1, source_target_pairs={{0,0},{1,8},{8,1},{9,9},{2,2},{3,10},{10,3},{11,11},{4,4},{5,12},{... | collective-permute-start | bytes 884744 | tf_op jit(solution)/shard_map/ppermute | solution.py:300
  699.3 15.3 %collective-permute-start.6 = (bf16[128,2048]{1,0:T(8,128)(2,1)S(1)}, bf16[128,2048]{1,0:T(8,128)(2,1)S(1)}, u32[]{:S(2)}, u32[]{:S(2)}) collective-permute-start(bf16[128,2048]{1,0:T(8,128)(2,1)S(1)} %reshape.204), channel_id=1, source_target_pairs={{0,0},{1,8},{8,1},{9,9},{2,2},{3,10},{10,3},{11,11},{4,4},{5,12},{... | collective-permute-start | bytes 1572872 | tf_op jit(solution)/shard_map/ppermute | solution.py:300
  707.3 11.5 %collective-permute-start.4 = (bf16[128,2048]{1,0:T(8,128)(2,1)S(1)}, bf16[128,2048]{1,0:T(8,128)(2,1)S(1)}, u32[]{:S(2)}, u32[]{:S(2)}) collective-permute-start(bf16[128,2048]{1,0:T(8,128)(2,1)S(1)} %reshape.200), channel_id=1, source_target_pairs={{0,0},{1,8},{8,1},{9,9},{2,2},{3,10},{10,3},{11,11},{4,4},{5,12},{... | collective-permute-start | bytes 1572872 | tf_op jit(solution)/shard_map/ppermute | solution.py:300
  711.3 10.4 %all-to-all-start.1 = ((f32[8,2,16]{2,1,0:T(2,128)}), f32[8,2,16]{2,1,0:T(2,128)S(1)}, u32[]{:S(2)}, u32[]{:S(2)}) async-start(f32[8,2,16]{2,1,0:T(2,128)} %copy.115), calls=%async_computation.5 | async-start | bytes 16384 | tf_op jit(solution)/shard_map/all_to_all | solution.py:443
  (33 other events, 733.7 us)
Sparse Core Ops, SparseCore 0:
  31.6 59.0 all-gather.8
  93.0 33.0 all-gather.6
  158.7 34.6 reduce-scatter.10
  195.4 84.3 all-gather.12
  281.9 33.0 all-gather.10
  316.6 32.1 all-gather.14
  369.4 34.4 reduce-scatter.14
  408.8 34.6 all-gather.16
  447.2 88.1 reduce-scatter.20
  537.8 35.5 reduce-scatter.16
  577.1 78.4 reduce-scatter.18
  658.0 36.1 reduce-scatter.12

commit v2 on v1

v2 whole, which is shorter than its diff:
```python
import functools
import jax
import jax.numpy as jnp
from jax import lax
from jax.experimental import pallas as pl
from jax.experimental.pallas import tpu as pltpu
from jax.sharding import PartitionSpec as P

C = 128
D = 2048
PARTS = (512, 512)
EPS = 1e-06
F32 = jnp.float32
BF16 = jnp.bfloat16
NN = (((1,), (0,)), ((), ()))
NT = (((1,), (1,)), ((), ()))
TN = (((0,), (0,)), ((), ()))


def dot(left, right, dims):
    return lax.dot_general(left, right, dims, preferred_element_type=F32)


def once(left, right, dims):
    return dot(left.astype(BF16), right.astype(BF16), dims)


def halves(value):
    high = value.astype(BF16)
    return high, (value - high.astype(F32)).astype(BF16)


def fine(left, right, dims):
    left_high, left_low = halves(left)
    right_high, right_low = halves(right)
    (over,), (under,) = dims[0]
    first = dot(
        jnp.concatenate([left_high, left_low], over), jnp.concatenate([right_high, right_high], under), dims
    )
    return first + dot(left_high, right_low, dims)


def sigmoid(v):
    return 1.0 / (1.0 + jnp.exp(-v))


def masks():
    row = lax.broadcasted_iota(jnp.int32, (C, C), 0)
    col = lax.broadcasted_iota(jnp.int32, (C, C), 1)
    return row, col


def shifted(rows, before, offset):
    joined = jnp.concatenate([before, rows], 0)
    return pltpu.roll(joined, offset, 0)[8:]


def convolved(rows, before, taps, marks):
    total = taps[0:1] * rows
    moved = []
    for offset in range(1, 4):
        term = shifted(rows, before, offset) * marks[offset - 1]
        moved.append(term)
        total = total + taps[offset : offset + 1] * term
    return total, moved


def inverses(systems):
    row, col = masks()
    eye = jnp.where(row == col, 1.0, 0.0)
    solved = []
    near = (row == col + 1) & ((row & 1) == 1)
    solved = [eye - jnp.where(near, a, 0.0) for a in systems]
    for level in range(1, 7):
        odd = ((row >> level) & 1) == 1
        off = odd & ((row >> level) == (col >> level) + 1)
        parts = [fine(x, jnp.where(off, a, 0.0), NN) for x, a in zip(solved, systems)]
        solved = [x - fine(p, x, NN) for x, p in zip(solved, parts)]
    return solved


def forward_kernel(chunks, mm, place, same, other, weights, out_w, out_w_next, taps, aux, segs, wait, wait_next, mixed, raw, part_same, part_other, t_out, u_out, s_out, m_out, q_out, before, state):
    step = pl.program_id(0)

    @pl.when(step == 0)
    def _():
        raw[:512, :] = dot(same[...], weights[...], NN)
        raw[512:, :] = dot(other[...], weights[...], NN)
        before[...] = jnp.zeros_like(before)
        state[...] = jnp.zeros_like(state)

    row, col = masks()
    eye = jnp.where(row == col, 1.0, 0.0)
    taps_now = taps[...]
    items = []
    for c in range(chunks):
        rows, fixed = spot(place, chunks * step + c), pl.ds(c * C, C)
        prev = before[...] if c == 0 else raw[spot(place, chunks * step + c - 1, 120, 8), :768]
        marks = [aux[fixed, j : j + 1] for j in range(3)]
        carried, closing, seg = aux[fixed, 3:4], aux[fixed, 4:5], aux[fixed, 5:6]
        same_doc = seg == segs[0, c : c + 1, :]
        gamma = carried[C - 1 : C]
        for h in range(2):
            acts = []
            for part in range(3):
                cols = slice(384 * h + 128 * part, 384 * h + 128 * part + 128)
                conv, _ = convolved(raw[rows, cols], prev[:, cols], taps_now[:, cols], marks)
                acts.append(conv * sigmoid(conv))
            q, k, v = acts
            q = q * lax.rsqrt(jnp.sum(q * q, -1, keepdims=True) + EPS)
            k = k * lax.rsqrt(jnp.sum(k * k, -1, keepdims=True) + EPS)
            b = sigmoid(raw[rows, 768 + h : 769 + h])
            items.append((q, k, v, b, carried, closing, same_doc, gamma))
    before[...] = raw[spot(place, chunks * step + chunks - 1, 120, 8), :768]
    systems, scores = [], []
    for q, k, v, b, carried, closing, same_doc, gamma in items:
        gram = mm(k, k, NT)
        systems.append(jnp.where(same_doc & (row > col), b * gram, 0.0))
        scores.append(jnp.where(same_doc & (row >= col), mm(q, k, NT), 0.0))
    solved = inverses(systems)
    wus = [
        mm(t, jnp.concatenate([(i[4] * i[3]) * i[1], i[3] * i[2]], 1), NN)
        for t, i in zip(solved, items)
    ]
    mns = [mm(i[5] * i[1], wu, TN) for wu, i in zip(wus, items)]
    qos = [mm(p, wu, NN) for p, wu in zip(scores, wus)]
    for n, i in enumerate(items):
        c, h = n // 2, n % 2
        t_out[h, c] = solved[n]
        now = state[h]
        s_out[h, c] = now
        move = i[7] * eye - mns[n][:, :128]
        query = i[4] * i[0] - qos[n][:, :128]
        m_out[h, c] = move
        q_out[h, c] = query
        state[h] = mm(move, now, NN) + mns[n][:, 128:]
        u_out[h, c] = wus[n][:, 128:] - mm(wus[n][:, :128], now, NN)
        result = (mm(query, now, NN) + qos[n][:, 128:]).astype(BF16)
        mixed[spot(place, chunks * step + c), h * 128 : h * 128 + 128] = result

    @pl.when(step == pl.num_programs(0) - 1)
    def _():
        project = jnp.concatenate([out_w[...], out_w_next[...]], 1)
        at = 0
        for ref in (part_same, part_other):
            count = ref.shape[0]
            ref[...] = dot(mixed[at : at + count, :], project, NT).astype(BF16)
            at += count


def spot(place, block, start=0, count=C):
    return pl.ds(pl.multiple_of(place[block] * C + start, 8), count)


def mix_forward(place, parts, weights, taps, aux, segs, waits, mm=fine):
    chunks, steps = 4, 2
    saved = jax.ShapeDtypeStruct((2, 8, C, C), F32)
    block = pl.BlockSpec((2, chunks, C, C), lambda i, place: (0, i, 0, 0))
    rows = lambda width: pl.BlockSpec((1024, width), lambda i, place: (0, 0))
    return pl.pallas_call(
        functools.partial(forward_kernel, chunks, mm),
        grid_spec=pltpu.PrefetchScalarGridSpec(
            num_scalar_prefetch=1,
            grid=(steps,),
            in_specs=[
                *[pl.BlockSpec((part.shape[0], D), lambda i, place: (0, 0)) for part in parts],
                pl.BlockSpec((D, 896), lambda i, place: (0, 0)),
                *[pl.BlockSpec((D, 128), lambda i, place, n=n: (0, 7 + n)) for n in range(2)],
                pl.BlockSpec((4, 768), lambda i, place: (0, 0)),
                pl.BlockSpec((chunks * C, 128), lambda i, place: (i, 0)),
                pl.BlockSpec((1, chunks, 128), lambda i, place: (i, 0, 0)),
                *[pl.BlockSpec(memory_space=pl.ANY) for _ in waits],
            ],
            out_specs=[rows(256), rows(896)]
            + [pl.BlockSpec((count, D), lambda i, place: (0, 0)) for count in PARTS]
            + [block] * 5,
            scratch_shapes=[pltpu.VMEM((8, 768), F32), pltpu.VMEM((2, C, C), F32)],
        ),
        out_shape=[jax.ShapeDtypeStruct((1024, 256), BF16)]
        + [jax.ShapeDtypeStruct((1024, 896), F32)]
        + [jax.ShapeDtypeStruct((count, D), BF16) for count in PARTS]
        + [saved] * 5,
        compiler_params=pltpu.CompilerParams(vmem_limit_bytes=48 * 1024 * 1024),
        cost_estimate=pl.CostEstimate(flops=20 << 30, bytes_accessed=20 << 20, transcendentals=0),
        name="mix_forward",
    )(place, *parts, weights, weights, weights, taps, aux, segs.reshape(steps, chunks, 128), *waits)


def backward_kernel(chunks, mm, place, near, other, out_w, out_w_next, raw, taps, aux, segs, t_in, u_in, s_in, m_in, q_in, back, taps_grad, after, adjoint, grad):
    step = pl.program_id(0)
    last = pl.num_programs(0) - 1
    start = chunks * (last - step)

    @pl.when(step == 0)
    def _():
        weights = jnp.concatenate([out_w[...], out_w_next[...]], 1)
        at = 0
        for ref in (near, other):
            grad[at : at + ref.shape[0], :] = dot(ref[...], weights, NN)
            at += ref.shape[0]
        after[...] = jnp.zeros_like(after)
        adjoint[...] = jnp.zeros_like(adjoint)
        taps_grad[...] = jnp.zeros_like(taps_grad)
        back[:, 768:] = jnp.zeros_like(back[:, 768:])

    row, col = masks()
    taps_sum = [[jnp.zeros((1, 128), F32) for _ in range(4)] for _ in range(6)]
    items = []
    for c in range(chunks):
        rows, fixed = spot(place, start + c), pl.ds(c * C, C)
        if c == 0:
            prev = jnp.where(step == last, 0.0, raw[spot(place, jnp.maximum(start - 1, 0), 120, 8), :768])
        else:
            prev = raw[spot(place, start + c - 1, 120, 8), :768]
        marks = [aux[fixed, j : j + 1] for j in range(3)]
        carried, closing, seg = aux[fixed, 3:4], aux[fixed, 4:5], aux[fixed, 5:6]
        same = seg == segs[0, c : c + 1, :]
        for h in range(2):
            acts, slopes, moved = [], [], []
            for part in range(3):
                cols = slice(384 * h + 128 * part, 384 * h + 128 * part + 128)
                now = raw[rows, cols]
                conv, terms = convolved(now, prev[:, cols], taps[:, cols], marks)
                s = sigmoid(conv)
                acts.append(conv * s)
                slopes.append(s * (1.0 + conv * (1.0 - s)))
                moved.append([now] + terms)
            q, k, v = acts
            rq = lax.rsqrt(jnp.sum(q * q, -1, keepdims=True) + EPS)
            rk = lax.rsqrt(jnp.sum(k * k, -1, keepdims=True) + EPS)
            b = sigmoid(raw[rows, 768 + h : 769 + h])
            do = grad[rows, 128 * h : 128 * h + 128]
            items.append((c, h, marks, carried, closing, same, slopes, moved, q * rq, k * rk, v, b, rq, rk, do))
    for item in sorted(items, key=lambda item: (-item[0], item[1])):
        c, h, marks, carried, closing, same, slopes, moved, q, k, v, b, rq, rk, do = item
        t, u, s, m, qe = t_in[h, c], u_in[h, c], s_in[h, c], m_in[h, c], q_in[h, c]
        g = adjoint[h]
        adjoint[h] = mm(m, g, TN) + mm(qe, do, TN)
        gram = mm(k, k, NT)
        score = jnp.where(same & (row >= col), mm(q, k, NT), 0.0)
        du = mm(score, do, TN) + mm(closing * k, g, NN)
        dr = mm(t, du, TN)
        dps = mm(jnp.concatenate([do, dr], 0), u, NT)
        dp = jnp.where(same & (row >= col), dps[:C], 0.0)
        da = jnp.where(same & (row > col), -dps[C:], 0.0)
        e = b * da
        sides = mm(jnp.concatenate([carried * do, (carried * b) * dr], 0), s, NT)
        inner = mm(jnp.concatenate([dp, e], 0), k, NN)
        dq = sides[:C] + inner[:C]
        dk = (
            inner[C:]
            - sides[C:]
            + mm(jnp.concatenate([dp, e], 0), jnp.concatenate([q, k], 0), TN)
            + closing * mm(u, g, NT)
        )
        ks = mm(k, s, NN)
        db = jnp.sum(dr * (v - carried * ks) + da * gram, -1, keepdims=True)
        backs = (
            rq * (dq - q * jnp.sum(dq * q, -1, keepdims=True)),
            rk * (dk - k * jnp.sum(dk * k, -1, keepdims=True)),
            b * dr,
        )
        rows = spot(place, start + c)
        back[rows, 768 + h : 769 + h] = (db * b * (1.0 - b)).astype(BF16)
        for part in range(3):
            d = backs[part] * slopes[part]
            cols = slice(384 * h + part * 128, 384 * h + part * 128 + 128)
            sums = taps_sum[3 * h + part]
            total = taps[0:1, cols] * d
            sums[0] += jnp.sum(d * moved[part][0], 0, keepdims=True)
            for offset in range(1, 4):
                sums[offset] += jnp.sum(d * moved[part][offset], 0, keepdims=True)
                marked = d * marks[offset - 1]
                joined = jnp.concatenate([marked, after[offset - 1, :, cols]], 0)
                after[offset - 1, :, cols] = marked[:8]
                up = pltpu.roll(joined, C + 8 - offset, 0)[:C]
                total = total + taps[offset : offset + 1, cols] * up
            back[rows, cols] = total.astype(BF16)
    for part in range(6):
        for offset in range(4):
            taps_grad[offset : offset + 1, part * 128 : part * 128 + 128] += taps_sum[part][offset]


def mix_backward(place, three, weights, raw, taps, aux, segs, saved, mm=fine):
    chunks, steps = 2, 4
    block = pl.BlockSpec((2, chunks, C, C), lambda i, place: (0, steps - 1 - i, 0, 0))
    rows = lambda width: pl.BlockSpec((1024, width), lambda i, place: (0, 0))
    return pl.pallas_call(
        functools.partial(backward_kernel, chunks, mm),
        grid_spec=pltpu.PrefetchScalarGridSpec(
            num_scalar_prefetch=1,
            grid=(steps,),
            in_specs=[pl.BlockSpec(part.shape, lambda i, place: (0, 0)) for part in three]
            + [pl.BlockSpec((D, 128), lambda i, place, n=n: (0, 7 + n)) for n in range(2)]
            + [
                rows(896),
                pl.BlockSpec((4, 768), lambda i, place: (0, 0)),
                pl.BlockSpec((chunks * C, 128), lambda i, place: (steps - 1 - i, 0)),
                pl.BlockSpec((1, chunks, 128), lambda i, place: (steps - 1 - i, 0, 0)),
            ]
            + [block] * 5,
            out_specs=[rows(896), pl.BlockSpec((4, 768), lambda i, place: (0, 0))],
            scratch_shapes=[
                pltpu.VMEM((3, 8, 768), F32),
                pltpu.VMEM((2, C, C), F32),
                pltpu.VMEM((1024, 256), F32),
            ],
        ),
        out_shape=[jax.ShapeDtypeStruct((1024, 896), BF16), jax.ShapeDtypeStruct((4, 768), F32)],
        compiler_params=pltpu.CompilerParams(vmem_limit_bytes=60 * 1024 * 1024),
        cost_estimate=pl.CostEstimate(flops=25 << 30, bytes_accessed=20 << 20, transcendentals=0),
        name="mix_backward",
    )(place, *three, weights, weights, raw, taps, aux, segs.reshape(steps, chunks, 128), *saved)


def marks_kernel(pack, aux, rows):
    segs = pack[:, 784:792].astype(F32)
    rows[...] = segs.T
    aux[...] = jnp.zeros_like(aux)
    for c in range(8):
        now = jnp.broadcast_to(segs[:, c : c + 1], (C, C))
        prior = jnp.broadcast_to(segs[:, c - 1 : c], (C, C)) if c else jnp.full((C, C), -1.0, F32)
        joined = jnp.concatenate([prior[120:], now], 0)
        columns = [pltpu.roll(joined, offset, 0)[8:] == now for offset in range(1, 4)]
        columns += [now == prior[C - 1 : C], now == now[C - 1 : C]]
        here = pl.ds(c * C, C)
        for n, column in enumerate(columns):
            aux[here, n : n + 1] = jnp.where(column, 1.0, 0.0)[:, :1]
        aux[here, 5:6] = now[:, :1]


AXES = ("yh", "x", "c", "z", "yl")
TEAM = ("z", "c")
RING = ("yh", "yl", "x")
PAD = 768
HID = 704
FORTH = [(a * 4 + x) * 2 + p for a in range(2) for p in range(2) for x in range(4)]
HOME = [(a * 2 + p) * 4 + x for a in range(2) for x in range(4) for p in range(2)]


def trade(value):
    return lax.ppermute(value, ("c", "yl"), [(0, 0), (1, 2), (2, 1), (3, 3)])


def mate(value):
    return lax.ppermute(value, "c", [(0, 1), (1, 0)])


def ahead(value):
    return lax.ppermute(value, "z", [(n, (n + 1) % 4) for n in range(4)])


def behind(value):
    return lax.ppermute(value, "z", [(n, (n - 1) % 4) for n in range(4)])


def local_call(kernel, name, outs, *operands, waits=(), limit=48):
    count = len(operands)

    def body(*refs):
        kernel(*refs[:count], *refs[count + len(waits) :])

    def whole(shape):
        return pl.BlockSpec(shape, lambda i: (0,) * len(shape))

    return pl.pallas_call(
        body,
        grid=(1,),
        in_specs=[whole(part.shape) for part in operands] + [pl.BlockSpec(memory_space=pl.ANY)] * len(waits),
        out_specs=[whole(shape) for shape, _ in outs],
        out_shape=[jax.ShapeDtypeStruct(shape, kind) for shape, kind in outs],
        compiler_params=pltpu.CompilerParams(vmem_limit_bytes=limit * 1024 * 1024),
        name=name,
    )(*operands, *waits)


def inverse_rms(rows):
    return lax.rsqrt(jnp.mean(rows * rows, -1, keepdims=True) + EPS)


def norm_back(normed, scale, scaled):
    return scale * (scaled - normed * jnp.mean(scaled * normed, -1, keepdims=True))


def put(out, value, blocks, at=0):
    for n, block in enumerate(blocks):
        out[:, at + n * 128 : at + n * 128 + 128] = value[:, block * 128 : block * 128 + 128].astype(out.dtype)


def norm_kernel(pack, rows, out):
    value = pack[:, 1152:].astype(F32)
    put(rows, value, FORTH)
    put(out, value * inverse_rms(value), FORTH)


def order_kernel(rows, out):
    put(out, rows[...], FORTH)


def ends_kernel(before, after, high, low):
    high[...] = before[:64]
    low[...] = after[64:]


def turn_kernel(*refs):
    at = 0
    for ref in refs[:2]:
        refs[-1][:, at : at + ref.shape[0]] = ref[...].T
        at += ref.shape[0]


def turned(parts, wait):
    block = 512
    return pl.pallas_call(
        turn_kernel,
        grid=(D // block,),
        in_specs=[pl.BlockSpec((part.shape[0], block), lambda i: (0, i)) for part in parts]
        + [pl.BlockSpec(memory_space=pl.ANY)],
        out_specs=pl.BlockSpec((block, 1024), lambda i: (i, 0)),
        out_shape=jax.ShapeDtypeStruct((D, 1024), BF16),
        compiler_params=pltpu.CompilerParams(vmem_limit_bytes=60 * 1024 * 1024),
        name="turned",
    )(*parts, wait)


def landed(own, up_high, up_low, down_high, down_low):
    high = up_high[...].astype(F32) + down_high[...].astype(F32)
    low = up_low[...].astype(F32) + down_low[...].astype(F32)
    return own[...] + jnp.concatenate([high, low], 0)


def middle_kernel(rows, own, up_high, up_low, down_high, down_low, middle, normed):
    value = rows[...].astype(F32) + landed(own, up_high, up_low, down_high, down_low)
    middle[...] = value
    normed[...] = (value * inverse_rms(value)).astype(BF16)


def second_kernel(middle, grad, scaled, out, low):
    value = middle[...]
    scale = inverse_rms(value)
    total = grad[...].astype(F32) + norm_back(value * scale, scale, scaled[...].astype(F32))
    out[...] = total
    low[...] = total.astype(BF16)


def first_kernel(rows, grad, own, up_high, up_low, down_high, down_low, out):
    value = rows[...].astype(F32)
    scale = inverse_rms(value)
    scaled = landed(own, up_high, up_low, down_high, down_low)
    put(out, grad[...] + norm_back(value * scale, scale, scaled), HOME)


def result_kernel(middle, own, up_high, up_low, down_high, down_low, out):
    put(out, middle[...] + landed(own, up_high, up_low, down_high, down_low), HOME)


def mix_pack_kernel(query, key, value, beta, taps, segs, out_w, gain_one, gain_two, tokens, out, gains):
    for n, ref in enumerate((query, key, value)):
        for h in range(2):
            out[:, h * 384 + n * 128 : h * 384 + n * 128 + 128] = ref[:, h * 128 : h * 128 + 128]
    out[:, 768:896] = jnp.zeros((128, 128), BF16)
    out[:, 768:776] = jnp.concatenate([beta[...].astype(F32), jnp.zeros((6, 128), F32)], 0).T.astype(BF16)
    out[:24, 776:784] = taps[...]
    out[:, 784:792] = segs[...].astype(F32).T.astype(BF16)
    out[:, 896:1152] = out_w[...].astype(F32).T.astype(BF16)
    gains[...] = jnp.concatenate([gain_one[...], gain_two[...]], 0)
    out[:, 1152:] = tokens[...]


def mix_scale_kernel(pack, gain, out):
    out[:, :768] = (pack[:, :768].astype(F32) * gain[...]).astype(BF16)
    small = pack[:, 768:896].astype(F32)
    lane = lax.broadcasted_iota(jnp.int32, small.shape, 1)
    out[:, 768:896] = jnp.where(lane < 2, small * gain[...], small).astype(BF16)
    out[:, 896:] = pack[:, 896:1152]


def ffn_pack_kernel(gate, up, down, out):
    for n, ref in enumerate((gate, up, down)):
        for j in range(3):
            count = min(256, HID - 256 * j)
            at = 768 * j + 256 * n
            out[:, at : at + count] = ref[256 * j : 256 * j + count, :].astype(F32).T.astype(BF16)
            if count < 256:
                out[:, at + count : at + 256] = jnp.zeros((128, 256 - count), BF16)


def ffn_scale_kernel(pack, gain, out):
    for j in range(3):
        at = 768 * j
        out[:, at : at + 512] = (pack[:, at : at + 512].astype(F32) * gain[...]).astype(BF16)
        out[:, at + 512 : at + 768] = pack[:, at + 512 : at + 768]


def ffn_sums_kernel(grads, weights, out, copy):
    copy[...] = grads[...]
    total = jnp.zeros((128, 1), F32)
    for j in range(3):
        here = slice(768 * j, 768 * j + 512)
        total = total + jnp.sum(grads[:, here].astype(F32) * weights[:, here].astype(F32), 1, keepdims=True)
    out[...] = total.reshape(1, 128)


def ffn_unpack_kernel(pack, gain, gate, up, down):
    for n, ref in enumerate((gate, up, down)):
        for j in range(3):
            count = min(256, HID - 256 * j)
            at = 768 * j + 256 * n
            value = pack[:, at : at + 256].astype(F32).T[:count]
            ref[256 * j : 256 * j + count, :] = value if n == 2 else value * gain[...]


def mix_unpack_kernel(pack, gain, query, key, value, beta, taps, out):
    for h in range(2):
        for n, ref in enumerate((query, key, value)):
            at = 384 * h + 128 * n
            ref[:, h * 128 : h * 128 + 128] = pack[at : at + 128, :].astype(F32) * gain[...]
    beta[...] = pack[768:770, :].astype(F32) * gain[...].reshape(1, 128)
    taps[...] = pack[770:772, :].astype(F32)
    out[...] = pack[784:, :].astype(F32)


def cross_kernel(same, other, own, up, down, after_high, after_low, before_high, before_low):
    total = same[...].astype(F32) + other[...].astype(F32)
    own[...] = total[:128]
    after_high[...] = total[128:192]
    after_low[...] = total[192:256].astype(BF16)
    before_high[...] = total[256:320].astype(BF16)
    before_low[...] = total[320:384]
    up[...] = total[384:448].astype(BF16)
    down[...] = total[448:].astype(BF16)


def pass_kernel(high, up, low, down, after, before):
    after[...] = (high[...] + up[...].astype(F32)).astype(BF16)
    before[...] = (low[...] + down[...].astype(F32)).astype(BF16)


def join_kernel(*refs):
    refs[-1][...] = jnp.concatenate([ref[...] for ref in refs[:-1]], 0)


def join(*parts):
    count = sum(part.shape[0] for part in parts)
    return local_call(join_kernel, "join", [((count, parts[0].shape[1]), BF16)], *parts)[0]


def gather_team(rows):
    before, after = ahead(rows), behind(rows)
    high, low = local_call(ends_kernel, "ends", [((64, D), BF16)] * 2, before, after)
    same = join(rows, after, before, ahead(high), behind(low))
    return same, mate(same)


def sum_team(same, other, waits=()):
    own, up, down, after_high, after_low, before_high, before_low = local_call(
        cross_kernel,
        "cross",
        [((128, D), F32)] + [((64, D), kind) for kind in (BF16, BF16, F32, BF16, BF16, F32)],
        same,
        mate(other),
        waits=waits,
        limit=60,
    )
    up, down = ahead(up), behind(down)
    after_low, before_high = ahead(after_low), behind(before_high)
    passed, before_low = local_call(
        pass_kernel, "pass_sum", [((64, D), BF16)] * 2, after_high, up, before_low, down
    )
    return (own, ahead(passed), after_low, before_high, behind(before_low)), passed


def gather_rows(rows):
    return lax.all_gather(rows, TEAM, axis=0, tiled=True)


def sum_rows(part):
    return lax.psum_scatter(part, TEAM, scatter_dimension=0, tiled=True)


def gather_ring(rows):
    return lax.all_gather(rows, RING, axis=0, tiled=True)


def swap_ring(part):
    return lax.all_to_all(part, RING, 0, 0, tiled=True)


def total_kernel(parts, pack, out, sums):
    total = parts[0].astype(F32)
    for n in range(1, 16):
        total = total + parts[n].astype(F32)
    out[...] = total.astype(BF16)
    small = pack[:, 768:896].astype(F32).T
    across = jnp.sum(total[768:770, :] * small[:2], 0, keepdims=True)
    rows = jnp.zeros((128, 1), F32)
    for n in range(6):
        here = slice(128 * n, 128 * n + 128)
        rows = rows + jnp.sum(total[here, :] * pack[:, here].astype(F32), 1, keepdims=True)
    sums[...] = across + rows.reshape(1, 128)


def matmul(left, right, dims, kind=F32):
    return lax.dot_general(left, right, dims, preferred_element_type=F32).astype(kind)


def ffn_kernel(source, *refs):
    parts, grads, (weights, active, back, second, total) = refs[:2], refs[2:4], refs[4:]
    step = pl.program_id(0)
    row = 0
    for part, grad in zip(parts, grads):
        count = part.shape[0]
        here = slice(row, row + count)
        both = dot(part[...], weights[:, :512], NN)
        grad_active = dot(grad[...], weights[:, 512:], NN)
        gate, up = both[:, :256], both[:, 256:]
        sigma = sigmoid(gate)
        swish = gate * sigma
        active[here, :] = (swish * up).astype(BF16)
        slope = sigma * (1.0 + gate * (1.0 - sigma))
        backs = jnp.concatenate([grad_active * up * slope, grad_active * swish], 1).astype(BF16)
        back[here, :] = backs
        piece = dot(backs, weights[:, :512], NT)

        @pl.when(step == 0)
        def _():
            total[here, :] = piece

        @pl.when(step == 1)
        def _():
            total[here, :] = total[here, :] + piece

        @pl.when(step == 2)
        def _():
            done = (total[here, :] + piece).astype(BF16)
            for n in range(count // C):
                second[spot(source, row // C + n), :] = done[n * C : n * C + C]

        row += count


def ffn(source, parts, grads, weights):
    whole = [pl.BlockSpec(part.shape, lambda j, source: (0, 0)) for part in parts]
    return pl.pallas_call(
        ffn_kernel,
        grid_spec=pltpu.PrefetchScalarGridSpec(
            num_scalar_prefetch=1,
            grid=(3,),
            in_specs=whole + whole + [pl.BlockSpec((D, 768), lambda j, source: (0, j))],
            out_specs=[
                pl.BlockSpec((1024, 256), lambda j, source: (0, j)),
                pl.BlockSpec((1024, 512), lambda j, source: (0, j)),
                pl.BlockSpec((1024, D), lambda j, source: (0, 0)),
            ],
            scratch_shapes=[pltpu.VMEM((1024, D), F32)],
        ),
        out_shape=[
            jax.ShapeDtypeStruct((1024, 768), BF16),
            jax.ShapeDtypeStruct((1024, 1536), BF16),
            jax.ShapeDtypeStruct((1024, D), BF16),
        ],
        compiler_params=pltpu.CompilerParams(vmem_limit_bytes=60 * 1024 * 1024),
        cost_estimate=pl.CostEstimate(flops=2 * 1024 * D * 1280 * 3, bytes_accessed=30 << 20, transcendentals=0),
        name="ffn",
    )(source, *parts, *grads, weights)


def ffn_grad_kernel(*refs):
    parts, grads, (back, active, out) = refs[:2], refs[2:4], refs[4:]
    seq = jnp.concatenate([ref[...].T for ref in parts], 1)
    dy = jnp.concatenate([ref[...].T for ref in grads], 1)
    for j in range(3):
        at = j * 768
        out[:, at : at + 512] = dot(seq, back[:, j * 512 : j * 512 + 512], NN).astype(BF16)
        out[:, at + 512 : at + 768] = dot(dy, active[:, j * 256 : j * 256 + 256], NN).astype(BF16)


def ffn_grad(parts, grads, back, active):
    block = 512
    return pl.pallas_call(
        ffn_grad_kernel,
        grid=(D // block,),
        in_specs=[pl.BlockSpec((part.shape[0], block), lambda i: (0, i)) for part in (*parts, *grads)]
        + [pl.BlockSpec(part.shape, lambda i: (0, 0)) for part in (back, active)],
        out_specs=pl.BlockSpec((block, 2304), lambda i: (i, 0)),
        out_shape=jax.ShapeDtypeStruct((D, 2304), BF16),
        compiler_params=pltpu.CompilerParams(vmem_limit_bytes=60 * 1024 * 1024),
        cost_estimate=pl.CostEstimate(flops=2 * 1024 * D * 2304, bytes_accessed=20 << 20, transcendentals=0),
        name="ffn_grad",
    )(*parts, *grads, back, active)


def in_grad_kernel(one, back, taps, near, other, mixed, out):
    total = dot(one[...], back[...], NN)
    outer = 0.0
    at = 0
    for ref in (near, other):
        outer = outer + dot(mixed[at : at + ref.shape[0], :].T, ref[...], NN)
        at += ref.shape[0]
    small = total[:, 768:].T
    for r in range(4):
        rows = slice(r * 128, r * 128 + 128)
        for n in range(6):
            out[r, n * 128 : n * 128 + 128, :] = total[rows, n * 128 : n * 128 + 128].astype(BF16)
        tail = jnp.concatenate([small[:2, rows], taps[r], jnp.zeros((12, 128), F32)], 0)
        out[r, 768:784, :] = tail.astype(BF16)
        out[r, 784:, :] = outer[:, rows].astype(BF16)


def in_grad(one, back, taps, three, mixed):
    block = 512
    return pl.pallas_call(
        in_grad_kernel,
        grid=(D // block,),
        in_specs=[
            pl.BlockSpec((block, 1024), lambda i: (i, 0)),
            pl.BlockSpec(back.shape, lambda i: (0, 0)),
            pl.BlockSpec((4, 2, 128), lambda i: (i, 0, 0)),
            *[pl.BlockSpec((part.shape[0], block), lambda i: (0, i)) for part in three],
            pl.BlockSpec(mixed.shape, lambda i: (0, 0)),
        ],
        out_specs=pl.BlockSpec((4, 1040, 128), lambda i: (i, 0, 0)),
        out_shape=jax.ShapeDtypeStruct((16, 1040, 128), BF16),
        compiler_params=pltpu.CompilerParams(vmem_limit_bytes=60 * 1024 * 1024),
        cost_estimate=pl.CostEstimate(flops=2 * 1024 * D * 1152, bytes_accessed=8 << 20, transcendentals=0),
        name="in_grad",
    )(one, back, taps, *three, mixed)


def first_kernel_parts(back, weights, *outs):
    at = 0
    for out in outs:
        count = out.shape[0]
        out[...] = dot(back[at : at + count, :], weights[...], NT).astype(BF16)
        at += count


def first_parts(back, weights):
    block = 512
    return pl.pallas_call(
        first_kernel_parts,
        grid=(D // block,),
        in_specs=[pl.BlockSpec((1024, 896), lambda i: (0, 0)), pl.BlockSpec((block, 896), lambda i: (i, 0))],
        out_specs=[pl.BlockSpec((count, block), lambda i: (0, i)) for count in PARTS],
        out_shape=[jax.ShapeDtypeStruct((count, D), BF16) for count in PARTS],
        compiler_params=pltpu.CompilerParams(vmem_limit_bytes=60 * 1024 * 1024),
        cost_estimate=pl.CostEstimate(flops=2 * 1024 * D * 896, bytes_accessed=8 << 20, transcendentals=0),
        name="first_parts",
    )(back, weights)


def down_kernel(active, first, second, third, wait, *outs):
    right = jnp.concatenate([first[...], second[...], third[...]], 1)
    at = 0
    for out in outs:
        out[...] = dot(active[at : at + out.shape[0], :], right, NT).astype(BF16)
        at += out.shape[0]


def down_product(active, weights, wait):
    block = 512
    return pl.pallas_call(
        down_kernel,
        grid=(D // block,),
        in_specs=[pl.BlockSpec((1024, PAD), lambda i: (0, 0))]
        + [pl.BlockSpec((block, 256), lambda i, j=j: (i, 3 * j + 2)) for j in range(3)]
        + [pl.BlockSpec(memory_space=pl.ANY)],
        out_specs=[pl.BlockSpec((count, block), lambda i: (0, i)) for count in PARTS],
        out_shape=[jax.ShapeDtypeStruct((count, D), BF16) for count in PARTS],
        compiler_params=pltpu.CompilerParams(vmem_limit_bytes=60 * 1024 * 1024),
        cost_estimate=pl.CostEstimate(flops=2 * 1024 * D * 768, bytes_accessed=8 << 20, transcendentals=0),
        name="down_product",
    )(active, weights, weights, weights, wait)


def team_total(values, pair):
    values = values.reshape(4, 2, 16)
    here = lax.axis_index(pair)
    mine = lax.dynamic_index_in_dim(values, here, 1, False)
    other = lax.dynamic_index_in_dim(values, 1 - here, 1, False)
    mine = mine + lax.ppermute(other, pair, [(0, 1), (1, 0)])
    place = lax.axis_index("z")

    def block(distance):
        return lax.dynamic_index_in_dim(mine, (place + distance) & 3, 0, False)

    total = block(0)
    for distance in range(1, 4):
        total = total + lax.ppermute(block(distance), "z", [(n, (n + distance) % 4) for n in range(4)])
    return total


def on_device(
    tokens,
    segments,
    cotangent,
    attn_gain,
    w_query,
    w_key,
    w_value,
    w_beta,
    conv_weight,
    w_out,
    ffn_gain,
    w_gate,
    w_up,
    w_down,
):
    core, z = lax.axis_index("c"), lax.axis_index("z")
    true = jnp.arange(8, dtype=jnp.int32)
    distance, other = (true // 2 - z) & 3, (true % 2) ^ core
    place = (jnp.where(distance > 1, 5 - distance, distance) + 4 * other).astype(jnp.int32)

    source = jnp.sum(jnp.where(place[:, None] == true[None, :], true[:, None], 0), 0).astype(jnp.int32)

    mix_pack, gains = local_call(
        mix_pack_kernel,
        "mix_pack",
        [((128, 1152 + D), BF16), ((2, 16), F32)],
        w_query,
        w_key,
        w_value,
        w_beta.T,
        conv_weight.reshape(24, 8),
        segments.reshape(8, 128),
        w_out,
        attn_gain.reshape(1, 16),
        ffn_gain.reshape(1, 16),
        tokens,
        limit=60,
    )
    mix_pack = trade(mix_pack)
    rows, one = local_call(norm_kernel, "norm_one", [((128, D), BF16)] * 2, mix_pack)
    (grad_rows,) = local_call(order_kernel, "order_grad", [((128, D), BF16)], cotangent, limit=60)
    grad_rows = trade(grad_rows)
    (ffn_pack,) = local_call(ffn_pack_kernel, "ffn_pack", [((128, 2304), BF16)], w_gate.T, w_up.T, w_down, limit=60)
    ffn_pack = trade(ffn_pack)

    gains = jnp.broadcast_to(jnp.concatenate([gains, mate(gains)], 0)[None], (8, 4, 16))
    gains = lax.all_to_all(gains, ("z", "yl"), 0, 0, tiled=True).transpose(1, 0, 2).reshape(4, 128)
    home = gains[:2]
    away = jnp.where(core == lax.axis_index("yl"), gains[:2], gains[2:])
    (scaled_pack,) = local_call(mix_scale_kernel, "mix_scale", [((128, 1152), BF16)], mix_pack, away[0][:, None])
    mix_w = gather_ring(scaled_pack)

    one = gather_team(one)
    grads = gather_team(grad_rows)
    (scaled_ffn,) = local_call(
        ffn_scale_kernel, "ffn_scale", [((128, 2304), BF16)], ffn_pack, away[1][:, None]
    )
    ffn_w = gather_ring(scaled_ffn)

    taps = mix_w[:, 768:896].reshape(2, 2, 4, 128, 128)[:, :, :, :24, 8:16].reshape(2, 2, 4, 3, 4, 2, 8)
    taps = taps.transpose(4, 5, 3, 0, 2, 1, 6).reshape(4, 768).astype(F32)
    marks, seg_rows = local_call(marks_kernel, "marks", [((1024, 128), F32), ((8, 128), F32)], mix_pack)
    mixed, raw, *saved = mix_forward(place, one, mix_w, taps, marks, seg_rows, (scaled_ffn, grads[1]))
    middle, two = local_call(
        middle_kernel, "middle", [((128, D), F32), ((128, D), BF16)], rows, *sum_team(*saved[:2])[0]
    )
    one_turned = turned(one, saved[0])
    two = gather_team(two)
    active, ffn_back, second = ffn(source, two, grads, ffn_w)
    ffn_grads = ffn_grad(two, grads, ffn_back, active)
    result = down_product(active, ffn_w, second)
    middle_grad, three = local_call(
        second_kernel,
        "second",
        [((128, D), F32), ((128, D), BF16)],
        middle,
        grad_rows,
        sum_rows(second),
        waits=(ffn_grads, one_turned, result[0]),
    )
    ring_grads = lax.psum_scatter(ffn_grads, RING, scatter_dimension=0, tiled=True)
    three = gather_team(three)
    back, taps_grad = mix_backward(place, three, mix_w, raw, taps, marks, seg_rows, saved[2:])
    taps_grad = taps_grad.reshape(4, 2, 3, 2, 4, 2, 8).transpose(3, 5, 4, 1, 2, 0, 6).reshape(16, 2, 96)
    taps_grad = jnp.pad(taps_grad, ((0, 0), (0, 0), (0, 32)))
    ring_parts = lax.all_to_all(in_grad(one_turned, back, taps_grad, three, mixed), RING, 0, 0, tiled=True)
    terms, _ = sum_team(*first_parts(back, mix_w))
    (tokens_grad,) = local_call(first_kernel, "first", [((128, D), BF16)], rows, middle_grad, *terms)
    terms, passed = sum_team(*result, waits=terms[:1])
    (output,) = local_call(result_kernel, "result", [((128, D), BF16)], middle, *terms)
    ffn_sum, ring_grads = local_call(
        ffn_sums_kernel,
        "ffn_sums",
        [((1, 128), F32), ((128, 2304), BF16)],
        ring_grads,
        scaled_ffn,
        waits=(passed, tokens_grad),
    )
    grad_gate, grad_up, grad_down = local_call(
        ffn_unpack_kernel, "ffn_unpack", [((HID, 128), F32)] * 3, trade(ring_grads), home[1][None]
    )
    mix_grad, sums = local_call(
        total_kernel,
        "ring_total",
        [((1040, 128), BF16), ((1, 128), F32)],
        ring_parts,
        scaled_pack,
        waits=(tokens_grad, ffn_sum),
    )
    tokens_grad = trade(tokens_grad).astype(F32)
    output = trade(output)
    grad_query, grad_key, grad_value, grad_beta, grad_taps, grad_out = local_call(
        mix_unpack_kernel,
        "mix_unpack",
        [((128, 256), F32)] * 3 + [((2, 128), F32), ((2, 128), F32), ((256, 128), F32)],
        trade(mix_grad),
        home[0][:, None],
    )
    grad_taps = grad_taps[:, :96].reshape(2, 3, 4, 8).transpose(1, 2, 0, 3)
    return (
        output,
        tokens_grad,
        trade(team_total(sums, "c")) / attn_gain,
        grad_query,
        grad_key,
        grad_value,
        grad_beta.T,
        grad_taps,
        grad_out,
        trade(team_total(ffn_sum, "c")) / ffn_gain,
        grad_gate.T,
        grad_up.T,
        grad_down,
    )


def solution(mesh):
    dp, tensor = ("yh", "x", "c"), ("z", "yl")
    every = dp + tensor
    split = jax.sharding.Mesh(mesh.devices.reshape(2, 4, 2, 4, 2), AXES)
    placed = (
        P(every, None),
        P(dp),
        P(every, None),
        P(every),
        P(dp, tensor),
        P(dp, tensor),
        P(dp, tensor),
        P(dp, tensor),
        P(None, None, tensor, dp),
        P(tensor, dp),
        P(every),
        P(dp, tensor),
        P(dp, tensor),
        P(tensor, dp),
    )
    return jax.shard_map(
        on_device,
        mesh=split,
        in_specs=placed,
        out_specs=(
            P(every, None),
            P(every, None),
            P(every),
            P(dp, tensor),
            P(dp, tensor),
            P(dp, tensor),
            P(dp, tensor),
            P(None, None, tensor, dp),
            P(tensor, dp),
            P(every),
            P(dp, tensor),
            P(dp, tensor),
            P(tensor, dp),
        ),
        check_vma=False,
    )
```

time: 738 us -> 449 us (0.61)
  waiting for transfers between devices: 449 us -> 115 us
  Pallas kernels: 41.9 us -> 165 us
  matrix products: 85.1 us -> 0 us
  starting transfers between devices: 47.3 us -> 116 us
  local copies, waits for them, and re-layouts: 57.6 us -> 26.6 us
  other arithmetic: 34.3 us -> 5.91 us
    pallas_call x2 -> x37, Pallas kernels: 41.9 us -> 165 us  [the longest x1 33.7 us: ffn(): pl.pallas_call(ffn_kernel, grid_spec=pltpu.PrefetchScalarGridSpec(num_sca...]
    unnamed x14 -> x4, waiting for transfers between devices: 103 us -> 0.07 us
    all_gather x2, waiting for transfers between devices: 103 us -> 0.48 us  [gather_ring(): return lax.all_gather(rows, RING, axis=0, tiled=True)]
    reduce_scatter x4 -> x2, waiting for transfers between devices: 111 us -> 10.4 us  [the longest x1 10.4 us: sum_rows(): return lax.psum_scatter(part, TEAM, scatter_dimension=0, tiled=True)]
    all_gather x4 -> x0, waiting for transfers between devices: 90.4 us -> none  [gather_team(): return lax.all_gather(rows, TEAM, axis=0, tiled=True)]
    dot_general x12 -> x0, matrix products: 85.1 us -> none  [matmul(): lax.dot_general(left, right, dims, preferred_element_type=F32).astype(kind)]
    ppermute x0 -> x42, waiting for transfers between devices: none -> 56.1 us  [the longest x17 52.3 us: ahead(): return lax.ppermute(value, 'z', [(n, (n + 1) % 4) for n in range(4)])]
    ppermute x0 -> x42, starting transfers between devices: none -> 55.9 us  [the longest x17 35.1 us: behind(): return lax.ppermute(value, 'z', [(n, (n - 1) % 4) for n in range(4)])]
  transfers between devices with their start and end apart: 23 -> 65, of which waited for: 19 -> 30; matrix products, arithmetic and copies ran while one was open for 17% -> 2% of each run, Pallas kernels for 4% -> 28%
where the time goes in v2:
time: 449 us; the launch traced here: 443 us
  Pallas kernels  165 us (37%)
  starting transfers between devices  116 us (26%)
  waiting for transfers between devices  115 us (26%)
  local copies, waits for them, and re-layouts  26.6 us (6%)
  between operations  14.7 us (3%)
  other arithmetic  5.91 us (1%)
    ppermute x17, waiting for transfers between devices, ahead(): return lax.ppermute(value, 'z', [(n, (n + 1) % 4) for n in range(4)])  52.3 us
    ppermute x9, starting transfers between devices, trade(): return lax.ppermute(value, ('c', 'yl'), [(0, 0), (1, 2), (2, 1), (3, 3)])  39.7 us
    ppermute x17, starting transfers between devices, behind(): return lax.ppermute(value, 'z', [(n, (n - 1) % 4) for n in range(4)])  35.1 us
    pallas_call x1, Pallas kernels, ffn(): pl.pallas_call(ffn_kernel, grid_spec=pltpu.PrefetchScalarGridSpec(num_sca...  33.7 us
    pallas_call x29, Pallas kernels, local_call(): pl.pallas_call(body, grid=(1,), in_specs=[whole(part.shape) for part in o...  32 us
    pallas_call x1, Pallas kernels, mix_backward(): pl.pallas_call(functools.partial(backward_kernel, chunks, mm), grid_spec=...  27.7 us
    ppermute x9, waiting for transfers between devices, trade(): return lax.ppermute(value, ('c', 'yl'), [(0, 0), (1, 2), (2, 1), (3, 3)])  25.9 us
    pallas_call x1, Pallas kernels, mix_forward(): pl.pallas_call(functools.partial(forward_kernel, chunks, mm), grid_spec=p...  25.8 us
  transfers between devices with their start and end apart: 65, of which 30 were waited for; matrix products, arithmetic and copies ran while one was open for 2% of the time, Pallas kernels for 28%

profile of v2, /device:TPU:1, one launch (start us, length us, event | category | flops | bytes accessed | tf_op | source)
XLA Modules:
  0.0 443.0 jit_solution(16960464749722990589)
XLA Ops:
  9.6 4.6 %collective-permute-start = (bf16[128,3200]{1,0:T(8,128)(2,1)}, bf16[128,3200]{1,0:T(8,128)(2,1)S(1)}, u32[]{:S(2)}, u32[]{:S(2)}) collective-permute-start(bf16[128,3200]{1,0:T(8,128)(2,1)} %get-tuple-element.89), channel_id=1, source_target_pairs={{0,0},{1,8},{8,1},{9,9},{2,2},{3,10},{10,3},{11,11},{4,4},{5,12},{... | collective-permute-start | bytes 2457608 | tf_op jit(solution)/shard_map/ppermute | solution.py:342
  16.9 5.0 %all-to-all-start = ((f32[8,4,16]{2,1,0:T(4,128)}), f32[8,4,16]{2,1,0:T(4,128)S(1)}, u32[]{:S(2)}, u32[]{:S(2)}) async-start(f32[8,4,16]{2,1,0:T(4,128)} %broadcast_in_dim.14), calls=%async_computation | async-start | bytes 32768 | tf_op jit(solution)/shard_map/all_to_all | solution.py:840
  22.0 5.1 %all-to-all-done = f32[8,4,16]{2,1,0:T(4,128)S(1)} async-done(((f32[8,4,16]{2,1,0:T(4,128)}), f32[8,4,16]{2,1,0:T(4,128)S(1)}, u32[]{:S(2)}, u32[]{:S(2)}) %all-to-all-start) | async-done | bytes 2080 | tf_op jit(solution)/shard_map/all_to_all | solution.py:840
  34.1 8.6 %collective-permute-done.7.refs_0_ = bf16[128,2304]{1,0:T(8,128)(2,1)S(1)} collective-permute-done((bf16[128,2304]{1,0:T(8,128)(2,1)}, bf16[128,2304]{1,0:T(8,128)(2,1)S(1)}, u32[]{:S(2)}, u32[]{:S(2)}) %collective-permute-start.7) | collective-permute-done | bytes 589856 | tf_op jit(solution)/shard_map/ppermute | solution.py:342
  50.0 7.1 %collective-permute-done.8.refs_0_.refs_1_ = bf16[128,2048]{1,0:T(8,128)(2,1)S(1)} collective-permute-done((bf16[128,2048]{1,0:T(8,128)(2,1)}, bf16[128,2048]{1,0:T(8,128)(2,1)S(1)}, u32[]{:S(2)}, u32[]{:S(2)}) %collective-permute-start.8) | collective-permute-done | bytes 524320 | tf_op jit(solution)/shard_map/ppermute | solution.py:342
  62.9 4.5 %collective-permute-done.10.refs_0_.refs_2_ = bf16[128,2048]{1,0:T(8,128)(2,1)S(1)} collective-permute-done((bf16[128,2048]{1,0:T(8,128)(2,1)S(1)}, bf16[128,2048]{1,0:T(8,128)(2,1)S(1)}, u32[]{:S(2)}, u32[]{:S(2)}) %collective-permute-start.10) | collective-permute-done | bytes 524320 | tf_op jit(solution)/shard_map/ppermute | solution.py:350
  86.1 25.8 %mix_forward.1 = (bf16[1024,256]{1,0:T(8,128)(2,1)S(1)}, f32[1024,896]{1,0:T(8,128)}, bf16[512,2048]{1,0:T(8,128)(2,1)}, bf16[512,2048]{1,0:T(8,128)(2,1)}, f32[...) custom-call(s32[8]{0:T(128)S(1)} %fusion.2.place, ...), custom_call_target="tpu_custom_call" | custom-call | flops 21474836480 | bytes 20971520 | tf_op jit(solution)/shard_map/mix_forward/pallas_call | solution.py:160
  148.5 9.2 %collective-permute-done.22.refs_0_.refs_2_ = bf16[128,2048]{1,0:T(8,128)(2,1)S(1)} collective-permute-done((bf16[128,2048]{1,0:T(8,128)(2,1)S(1)}, bf16[128,2048]{1,0:T(8,128)(2,1)S(1)}, u32[]{:S(2)}, u32[]{:S(2)}) %collective-permute-start.22) | collective-permute-done | bytes 524320 | tf_op jit(solution)/shard_map/ppermute | solution.py:350
  165.7 4.9 %collective-permute-start.25 = (bf16[512,2048]{1,0:T(8,128)(2,1)S(1)}, bf16[512,2048]{1,0:T(8,128)(2,1)}, u32[]{:S(2)}, u32[]{:S(2)}) collective-permute-start(bf16[512,2048]{1,0:T(8,128)(2,1)S(1)} %join.6.refs_0_), channel_id=1, source_target_pairs={{0,8},{8,0},{1,9},{9,1},{2,10},{10,2},{3,11},{11,3},{4,12},{12,4},... | collective-permute-start | bytes 6291464 | tf_op jit(solution)/shard_map/ppermute | solution.py:346
  174.4 33.7 %ffn.1 = (bf16[1024,768]{1,0:T(8,128)(2,1)}, bf16[1024,1536]{1,0:T(8,128)(2,1)}, bf16[1024,2048]{1,0:T(8,128)(2,1)}) custom-call(s32[8]{0:T(128)} %select_reduce_fusion.source, bf16[512,2048]{1,0:T(8,128)(2,1)} %copy-done.4, bf16[512,2048]{1,0:T(8,128)(2,1)} %collective-permute-done.25.refs_1_, bf16[512,2048]{1,0:T(8,128)(2,1)} %join.5.refs_2_, ...), custom_call_target="tpu_custom_call" | custom-call | flops 16106127360 | bytes 31457280 | tf_op jit(solution)/shard_map/ffn/pallas_call | solution.py:644
  208.2 15.3 %ffn_grad.1.refs_3_ = bf16[2048,2304]{1,0:T(8,128)(2,1)} custom-call(bf16[512,2048]{1,0:T(8,128)(2,1)} %copy-done.4, bf16[512,2048]{1,0:T(8,128)(2,1)} %collective-permute-done.25.refs_1_, bf16[512,2048]{1,0:T(8,128)(2,1)} %join.5.refs_2_, bf16[512,2048]{1,0:T(8,128)(2,1)} %collective-permute-done.13.wait_next.refs_3_, ...), custom_call_target="tpu_custom_call" | custom-call | flops 9663676416 | bytes 20971520 | tf_op jit(solution)/shard_map/ffn_grad/pallas_call | solution.py:680
  223.6 5.3 %turned.1.refs_4_.one = bf16[2048,1024]{1,0:T(8,128)(2,1)} custom-call(bf16[512,2048]{1,0:T(8,128)(2,1)} %copy-done, bf16[512,2048]{1,0:T(8,128)(2,1)} %collective-permute-done.5.other.refs_1_, bf16[512,2048]{1,0:T(8,128)(2,1)} %get-tuple-element.99.refs_0_.refs_2_), custom_call_target="tpu_custom_call" | custom-call | tf_op jit(solution)/shard_map/turned/pallas_call | solution.py:414
  228.9 7.2 %down_product.1 = (bf16[512,2048]{1,0:T(8,128)(2,1)}, bf16[512,2048]{1,0:T(8,128)(2,1)}) custom-call(bf16[1024,768]{1,0:T(8,128)(2,1)} %get-tuple-element.114.active.refs_5_, bf16[2048,2304]{1,0:T(8,128)(2,1)} %all-gather.5.cloned.1.call-done.refs_4_.first.second.third, bf16[2048,2304]{1,0:T(8,128)(2,1)} %all-gather.5.cloned.1.call-done.refs_4_.first.second.third, ...), custom_call_target="tpu_custom_call" | custom-call | flops 3221225472 | bytes 8388608 | tf_op jit(solution)/shard_map/down_product/pallas_call | solution.py:762
  236.0 10.4 %reduce-scatter.3.cloned.1.call-done.refs_2_ = bf16[128,2048]{1,0:T(8,128)(2,1)} async-done(((bf16[1024,2048]{1,0:T(8,128)(2,1)}), bf16[128,2048]{1,0:T(8,128)(2,1)}) %reduce-scatter.3.cloned.1.call-update) | async-done | bytes 524304 | tf_op jit(solution)/shard_map/reduce_scatter | solution.py:578
  253.8 9.2 %collective-permute-done.28.refs_0_.refs_2_ = bf16[128,2048]{1,0:T(8,128)(2,1)S(1)} collective-permute-done((bf16[128,2048]{1,0:T(8,128)(2,1)S(1)}, bf16[128,2048]{1,0:T(8,128)(2,1)S(1)}, u32[]{:S(2)}, u32[]{:S(2)}) %collective-permute-start.28) | collective-permute-done | bytes 524320 | tf_op jit(solution)/shard_map/ppermute | solution.py:350
  266.9 5.3 %collective-permute-done.29.refs_3_ = bf16[64,2048]{1,0:T(8,128)(2,1)S(1)} collective-permute-done((bf16[64,2048]{1,0:T(8,128)(2,1)S(1)}, bf16[64,2048]{1,0:T(8,128)(2,1)S(1)}, u32[]{:S(2)}, u32[]{:S(2)}) %collective-permute-start.29) | collective-permute-done | bytes 262176 | tf_op jit(solution)/shard_map/ppermute | solution.py:350
  281.8 27.7 %mix_backward.1 = (bf16[1024,896]{1,0:T(8,128)(2,1)}, f32[4,768]{1,0:T(4,128)}) custom-call(s32[8]{0:T(128)} %copy-done.25, bf16[512,2048]{1,0:T(8,128)(2,1)} %copy-done.3, bf16[512,2048]{1,0:T(8,128)(2,1)} %copy-done.34, bf16[2048,1152]{1,0:T(8,128)(2,1)} %all-gather.3.cloned.1.call-done.weights.out_w.out_w_next, ...), custom_call_target="tpu_custom_call" | custom-call | flops 26843545600 | bytes 20971520 | tf_op jit(solution)/shard_map/mix_backward/pallas_call | solution.py:288
  311.4 9.9 %in_grad.1 = bf16[16,1040,128]{2,1,0:T(8,128)(2,1)} custom-call(bf16[2048,1024]{1,0:T(8,128)(2,1)} %turned.1.refs_4_.one, bf16[1024,896]{1,0:T(8,128)(2,1)} %get-tuple-element.128.back, f32[16,2,128]{2,1,0:T(2,128)} %pad.4.taps, bf16[512,2048]{1,0:T(8,128)(2,1)} %copy-done.3, bf16[512,2048]{1,0:T(8,128)(2,1)} %copy-done.34, bf16[1024,256]{1,0:T(8,128)(2,1)} %copy-done.26), custom_call_target="tpu_custom_call" | custom-call | flops 4831838208 | bytes 8388608 | tf_op jit(solution)/shard_map/in_grad/pallas_call | solution.py:712
  321.3 6.6 %all-to-all-start.1 = ((bf16[16,1040,128]{2,1,0:T(8,128)(2,1)}), bf16[16,1040,128]{2,1,0:T(8,128)(2,1)}, u32[]{:S(2)}, u32[]{:S(2)}) async-start(bf16[16,1040,128]{2,1,0:T(8,128)(2,1)} %in_grad.1), calls=%async_computation.2 | async-start | bytes 8519680 | tf_op jit(solution)/shard_map/all_to_all | solution.py:879
  327.9 8.0 %first_parts.1 = (bf16[512,2048]{1,0:T(8,128)(2,1)}, bf16[512,2048]{1,0:T(8,128)(2,1)}) custom-call(bf16[1024,896]{1,0:T(8,128)(2,1)} %get-tuple-element.128.back, bf16[2048,1152]{1,0:T(8,128)(2,1)} %all-gather.3.cloned.1.call-done.weights.out_w.out_w_next), custom_call_target="tpu_custom_call" | custom-call | flops 3758096384 | bytes 8388608 | tf_op jit(solution)/shard_map/first_parts/pallas_call | solution.py:740
  371.7 6.7 %collective-permute-start.46 = (bf16[128,2048]{1,0:T(8,128)(2,1)S(1)}, bf16[128,2048]{1,0:T(8,128)(2,1)}, u32[]{:S(2)}, u32[]{:S(2)}) collective-permute-start(bf16[128,2048]{1,0:T(8,128)(2,1)S(1)} %first.1.refs_3_.refs_2_), channel_id=1, source_target_pairs={{0,0},{1,8},{8,1},{9,9},{2,2},{3,10},{10,3},{11,11},{4,4},{5,12},{... | collective-permute-start | bytes 1572872 | tf_op jit(solution)/shard_map/ppermute | solution.py:342
  382.5 5.2 %collective-permute-start.39 = (bf16[128,2048]{1,0:T(8,128)(2,1)S(1)}, bf16[128,2048]{1,0:T(8,128)(2,1)S(1)}, u32[]{:S(2)}, u32[]{:S(2)}) collective-permute-start(bf16[128,2048]{1,0:T(8,128)(2,1)S(1)} %result.1), channel_id=1, source_target_pairs={{0,0},{1,8},{8,1},{9,9},{2,2},{3,10},{10,3},{11,11},{4,4},{5,12},{... | collective-permute-start | bytes 1572872 | tf_op jit(solution)/shard_map/ppermute | solution.py:342
  391.2 8.3 %collective-permute-done.39 = bf16[128,2048]{1,0:T(8,128)(2,1)S(1)} collective-permute-done((bf16[128,2048]{1,0:T(8,128)(2,1)S(1)}, bf16[128,2048]{1,0:T(8,128)(2,1)S(1)}, u32[]{:S(2)}, u32[]{:S(2)}) %collective-permute-start.39) | collective-permute-done | bytes 524320 | tf_op jit(solution)/shard_map/ppermute | solution.py:342
  421.9 5.4 %collective-permute-start.51 = (f32[16]{0:T(128)S(1)}, f32[16]{0:T(128)S(1)}, u32[]{:S(2)}, u32[]{:S(2)}) collective-permute-start(f32[16]{0:T(128)S(1)} %fusion.8), channel_id=1, source_target_pairs={{0,0},{1,8},{8,1},{9,9},{2,2},{3,10},{10,3},{11,11},{4,4},{5,12},{... | collective-permute-start | bytes 200 | tf_op jit(solution)/shard_map/ppermute | solution.py:342
  (258 shorter events, 189.4 us)
Async XLA Ops:
  9.6 17.7 %collective-permute-start = (bf16[128,3200]{1,0:T(8,128)(2,1)}, bf16[128,3200]{1,0:T(8,128)(2,1)S(1)}, u32[]{:S(2)}, u32[]{:S(2)}) collective-permute-start(bf16[128,3200]{1,0:T(8,128)(2,1)} %get-tuple-element.89), channel_id=1, source_target_pairs={{0,0},{1,8},{8,1},{9,9},{2,2},{3,10},{10,3},{11,11},{4,4},{5,12},{... | collective-permute-start | bytes 2457608 | tf_op jit(solution)/shard_map/ppermute | solution.py:342
  21.9 61.2 %all-gather.3.cloned.1.call-start = ((), (), s32[]{:S(2)}) async-start(), calls=%async_computation.4 | async-start | bytes 5013504 | tf_op jit(solution)/shard_map/all_gather | solution.py:582
  28.1 146.4 %all-gather.5.cloned.1.call-start = ((), (), s32[]{:S(2)}) async-start(), calls=%async_computation.5 | async-start | bytes 10027008 | tf_op jit(solution)/shard_map/all_gather | solution.py:582
  30.3 12.4 %collective-permute-start.7 = (bf16[128,2304]{1,0:T(8,128)(2,1)}, bf16[128,2304]{1,0:T(8,128)(2,1)S(1)}, u32[]{:S(2)}, u32[]{:S(2)}) collective-permute-start(bf16[128,2304]{1,0:T(8,128)(2,1)} %ffn_pack.1), channel_id=1, source_target_pairs={{0,0},{1,8},{8,1},{9,9},{2,2},{3,10},{10,3},{11,11},{4,4},{5,12},{... | collective-permute-start | bytes 1769480 | tf_op jit(solution)/shard_map/ppermute | solution.py:342
  43.7 202.7 %reduce-scatter.3.cloned.1.call-start = ((), (), s32[]{:S(2)}) async-start(), calls=%async_computation.6 | async-start | bytes 4718592 | tf_op jit(solution)/shard_map/reduce_scatter | solution.py:578
  45.7 11.4 %collective-permute-start.8 = (bf16[128,2048]{1,0:T(8,128)(2,1)}, bf16[128,2048]{1,0:T(8,128)(2,1)S(1)}, u32[]{:S(2)}, u32[]{:S(2)}) collective-permute-start(bf16[128,2048]{1,0:T(8,128)(2,1)} %order_grad.1), channel_id=1, source_target_pairs={{0,0},{1,8},{8,1},{9,9},{2,2},{3,10},{10,3},{11,11},{4,4},{5,12},{... | collective-permute-start | bytes 1572872 | tf_op jit(solution)/shard_map/ppermute | solution.py:342
  60.2 12.9 %collective-permute-start.2 = (bf16[128,2048]{1,0:T(8,128)(2,1)S(1)}, bf16[128,2048]{1,0:T(8,128)(2,1)S(1)}, u32[]{:S(2)}, u32[]{:S(2)}) collective-permute-start(bf16[128,2048]{1,0:T(8,128)(2,1)S(1)} %get-tuple-element.91.refs_0_), channel_id=1, source_target_pairs={{0,2},{2,4},{4,6},{6,0},{1,3},{3,5},{5,7},{7,1},{8,10},{10,12},{12... | collective-permute-start | bytes 1572872 | tf_op jit(solution)/shard_map/ppermute | solution.py:350
  60.2 12.8 %collective-permute-start.1 = (bf16[128,2048]{1,0:T(8,128)(2,1)S(1)}, bf16[128,2048]{1,0:T(8,128)(2,1)S(1)}, u32[]{:S(2)}, u32[]{:S(2)}) collective-permute-start(bf16[128,2048]{1,0:T(8,128)(2,1)S(1)} %get-tuple-element.91.refs_0_), channel_id=1, source_target_pairs={{0,6},{2,0},{4,2},{6,4},{1,7},{3,1},{5,3},{7,5},{8,14},{10,8},{12,... | collective-permute-start | bytes 1572872 | tf_op jit(solution)/shard_map/ppermute | solution.py:354
  129.5 12.0 %collective-permute-start.18 = (bf16[64,2048]{1,0:T(8,128)(2,1)}, bf16[64,2048]{1,0:T(8,128)(2,1)S(1)}, u32[]{:S(2)}, u32[]{:S(2)}) collective-permute-start(bf16[64,2048]{1,0:T(8,128)(2,1)} %get-tuple-element.107), channel_id=1, source_target_pairs={{0,2},{2,4},{4,6},{6,0},{1,3},{3,5},{5,7},{7,1},{8,10},{10,12},{12... | collective-permute-start | bytes 786440 | tf_op jit(solution)/shard_map/ppermute | solution.py:350
  129.5 12.0 %collective-permute-start.19 = (bf16[64,2048]{1,0:T(8,128)(2,1)}, bf16[64,2048]{1,0:T(8,128)(2,1)S(1)}, u32[]{:S(2)}, u32[]{:S(2)}) collective-permute-start(bf16[64,2048]{1,0:T(8,128)(2,1)} %get-tuple-element.108), channel_id=1, source_target_pairs={{0,6},{2,0},{4,2},{6,4},{1,7},{3,1},{5,3},{7,5},{8,14},{10,8},{12,... | collective-permute-start | bytes 786440 | tf_op jit(solution)/shard_map/ppermute | solution.py:354
  145.7 11.9 %collective-permute-start.22 = (bf16[128,2048]{1,0:T(8,128)(2,1)S(1)}, bf16[128,2048]{1,0:T(8,128)(2,1)S(1)}, u32[]{:S(2)}, u32[]{:S(2)}) collective-permute-start(bf16[128,2048]{1,0:T(8,128)(2,1)S(1)} %get-tuple-element.111.refs_0_), channel_id=1, source_target_pairs={{0,2},{2,4},{4,6},{6,0},{1,3},{3,5},{5,7},{7,1},{8,10},{10,12},{12... | collective-permute-start | bytes 1572872 | tf_op jit(solution)/shard_map/ppermute | solution.py:350
  208.2 191.3 %reduce-scatter.5.cloned.1.call-start = ((), (), s32[]{:S(2)}) async-start(), calls=%async_computation.7 | async-start | bytes 10027008 | tf_op jit(solution)/shard_map/reduce_scatter | solution.py:874
  249.6 13.4 %collective-permute-start.28 = (bf16[128,2048]{1,0:T(8,128)(2,1)S(1)}, bf16[128,2048]{1,0:T(8,128)(2,1)S(1)}, u32[]{:S(2)}, u32[]{:S(2)}) collective-permute-start(bf16[128,2048]{1,0:T(8,128)(2,1)S(1)} %get-tuple-element.119.refs_0_), channel_id=1, source_target_pairs={{0,2},{2,4},{4,6},{6,0},{1,3},{3,5},{5,7},{7,1},{8,10},{10,12},{12... | collective-permute-start | bytes 1572872 | tf_op jit(solution)/shard_map/ppermute | solution.py:350
  250.4 12.6 %collective-permute-start.27 = (bf16[128,2048]{1,0:T(8,128)(2,1)S(1)}, bf16[128,2048]{1,0:T(8,128)(2,1)S(1)}, u32[]{:S(2)}, u32[]{:S(2)}) collective-permute-start(bf16[128,2048]{1,0:T(8,128)(2,1)S(1)} %get-tuple-element.119.refs_0_), channel_id=1, source_target_pairs={{0,6},{2,0},{4,2},{6,4},{1,7},{3,1},{5,3},{7,5},{8,14},{10,8},{12,... | collective-permute-start | bytes 1572872 | tf_op jit(solution)/shard_map/ppermute | solution.py:354
  321.3 81.7 %all-to-all-start.1 = ((bf16[16,1040,128]{2,1,0:T(8,128)(2,1)}), bf16[16,1040,128]{2,1,0:T(8,128)(2,1)}, u32[]{:S(2)}, u32[]{:S(2)}) async-start(bf16[16,1040,128]{2,1,0:T(8,128)(2,1)} %in_grad.1), calls=%async_computation.2 | async-start | bytes 8519680 | tf_op jit(solution)/shard_map/all_to_all | solution.py:879
  345.3 11.7 %collective-permute-start.41 = (bf16[64,2048]{1,0:T(8,128)(2,1)}, bf16[64,2048]{1,0:T(8,128)(2,1)S(1)}, u32[]{:S(2)}, u32[]{:S(2)}) collective-permute-start(bf16[64,2048]{1,0:T(8,128)(2,1)} %get-tuple-element.145), channel_id=1, source_target_pairs={{0,6},{2,0},{4,2},{6,4},{1,7},{3,1},{5,3},{7,5},{8,14},{10,8},{12,... | collective-permute-start | bytes 786440 | tf_op jit(solution)/shard_map/ppermute | solution.py:354
  357.1 13.9 %collective-permute-start.42 = (bf16[64,2048]{1,0:T(8,128)(2,1)S(1)}, bf16[64,2048]{1,0:T(8,128)(2,1)S(1)}, u32[]{:S(2)}, u32[]{:S(2)}) collective-permute-start(bf16[64,2048]{1,0:T(8,128)(2,1)S(1)} %get-tuple-element.146), channel_id=1, source_target_pairs={{0,2},{2,4},{4,6},{6,0},{1,3},{3,5},{5,7},{7,1},{8,10},{10,12},{12... | collective-permute-start | bytes 786440 | tf_op jit(solution)/shard_map/ppermute | solution.py:350
  359.7 18.7 %collective-permute-start.36 = (bf16[64,2048]{1,0:T(8,128)(2,1)}, bf16[64,2048]{1,0:T(8,128)(2,1)S(1)}, u32[]{:S(2)}, u32[]{:S(2)}) collective-permute-start(bf16[64,2048]{1,0:T(8,128)(2,1)} %get-tuple-element.138), channel_id=1, source_target_pairs={{0,2},{2,4},{4,6},{6,0},{1,3},{3,5},{5,7},{7,1},{8,10},{10,12},{12... | collective-permute-start | bytes 786440 | tf_op jit(solution)/shard_map/ppermute | solution.py:350
  365.3 13.1 %collective-permute-start.37 = (bf16[64,2048]{1,0:T(8,128)(2,1)}, bf16[64,2048]{1,0:T(8,128)(2,1)S(1)}, u32[]{:S(2)}, u32[]{:S(2)}) collective-permute-start(bf16[64,2048]{1,0:T(8,128)(2,1)} %get-tuple-element.139), channel_id=1, source_target_pairs={{0,6},{2,0},{4,2},{6,4},{1,7},{3,1},{5,3},{7,5},{8,14},{10,8},{12,... | collective-permute-start | bytes 786440 | tf_op jit(solution)/shard_map/ppermute | solution.py:354
  365.3 16.0 %collective-permute-start.38 = (bf16[64,2048]{1,0:T(8,128)(2,1)S(1)}, bf16[64,2048]{1,0:T(8,128)(2,1)S(1)}, u32[]{:S(2)}, u32[]{:S(2)}) collective-permute-start(bf16[64,2048]{1,0:T(8,128)(2,1)S(1)} %get-tuple-element.140), channel_id=1, source_target_pairs={{0,6},{2,0},{4,2},{6,4},{1,7},{3,1},{5,3},{7,5},{8,14},{10,8},{12,... | collective-permute-start | bytes 786440 | tf_op jit(solution)/shard_map/ppermute | solution.py:354
  371.7 17.4 %collective-permute-start.46 = (bf16[128,2048]{1,0:T(8,128)(2,1)S(1)}, bf16[128,2048]{1,0:T(8,128)(2,1)}, u32[]{:S(2)}, u32[]{:S(2)}) collective-permute-start(bf16[128,2048]{1,0:T(8,128)(2,1)S(1)} %first.1.refs_3_.refs_2_), channel_id=1, source_target_pairs={{0,0},{1,8},{8,1},{9,9},{2,2},{3,10},{10,3},{11,11},{4,4},{5,12},{... | collective-permute-start | bytes 1572872 | tf_op jit(solution)/shard_map/ppermute | solution.py:342
  382.5 17.0 %collective-permute-start.39 = (bf16[128,2048]{1,0:T(8,128)(2,1)S(1)}, bf16[128,2048]{1,0:T(8,128)(2,1)S(1)}, u32[]{:S(2)}, u32[]{:S(2)}) collective-permute-start(bf16[128,2048]{1,0:T(8,128)(2,1)S(1)} %result.1), channel_id=1, source_target_pairs={{0,0},{1,8},{8,1},{9,9},{2,2},{3,10},{10,3},{11,11},{4,4},{5,12},{... | collective-permute-start | bytes 1572872 | tf_op jit(solution)/shard_map/ppermute | solution.py:342
  407.4 25.2 %collective-permute-start.52 = (bf16[1040,128]{1,0:T(8,128)(2,1)S(1)}, bf16[1040,128]{1,0:T(8,128)(2,1)S(1)}, u32[]{:S(2)}, u32[]{:S(2)}) collective-permute-start(bf16[1040,128]{1,0:T(8,128)(2,1)S(1)} %get-tuple-element.154), channel_id=1, source_target_pairs={{0,0},{1,8},{8,1},{9,9},{2,2},{3,10},{10,3},{11,11},{4,4},{5,12},{... | collective-permute-start | bytes 798728 | tf_op jit(solution)/shard_map/ppermute | solution.py:342
  411.8 22.5 %collective-permute-start.58 = (bf16[128,2304]{1,0:T(8,128)(2,1)S(1)}, bf16[128,2304]{1,0:T(8,128)(2,1)S(1)}, u32[]{:S(2)}, u32[]{:S(2)}) collective-permute-start(bf16[128,2304]{1,0:T(8,128)(2,1)S(1)} %get-tuple-element.161), channel_id=1, source_target_pairs={{0,0},{1,8},{8,1},{9,9},{2,2},{3,10},{10,3},{11,11},{4,4},{5,12},{... | collective-permute-start | bytes 1769480 | tf_op jit(solution)/shard_map/ppermute | solution.py:342
  (78 other events, 728.1 us)
Sparse Core Ops, SparseCore 0:
  28.2 54.8 all-gather.2
  85.2 75.1 all-gather.4
  208.3 38.1 reduce-scatter.2
  249.8 110.2 reduce-scatter.4

commit v3 on v2

--- a/solution.py
+++ b/solution.py
@@ -21,10 +21,6 @@
     return lax.dot_general(left, right, dims, preferred_element_type=F32)
 
 
-def once(left, right, dims):
-    return dot(left.astype(BF16), right.astype(BF16), dims)
-
-
 def halves(value):
     high = value.astype(BF16)
     return high, (value - high.astype(F32)).astype(BF16)
@@ -56,12 +52,12 @@
 
 
 def convolved(rows, before, taps, marks):
-    total = taps[0:1] * rows
+    total = taps[0] * rows
     moved = []
     for offset in range(1, 4):
         term = shifted(rows, before, offset) * marks[offset - 1]
         moved.append(term)
-        total = total + taps[offset : offset + 1] * term
+        total = total + taps[offset] * term
     return total, moved
 
 
@@ -79,13 +75,33 @@
     return solved
 
 
-def forward_kernel(chunks, mm, place, same, other, weights, out_w, out_w_next, taps, aux, segs, wait, wait_next, mixed, raw, part_same, part_other, t_out, u_out, s_out, m_out, q_out, before, state):
+def taps_of(taps, part, h):
+    return [taps[row : row + 1] for row in range(part * 8 + h, part * 8 + 8, 2)]
+
+
+def place_of(member):
+    return (member // 8 * 4 + member % 4) * 2 + member // 4 % 2
+
+
+def gathered_taps(weights):
+    lane = lax.broadcasted_iota(jnp.int32, (C, C), 0)
+    target = lax.broadcasted_iota(jnp.int32, (C, C), 1)
+    total = jnp.zeros((32, C), F32)
+    for member in range(16):
+        chosen = (lane >= 8) & (lane < 16) & (target == lane - 8 + place_of(member) * 8)
+        piece = weights[member * C : member * C + 32, 768:]
+        total = total + dot(piece, jnp.where(chosen, 1.0, 0.0).astype(BF16), NN)
+    return total
+
+
+def forward_kernel(chunks, mm, place, same, other, weights, out_w, out_w_next, aux, segs, wait, wait_next, mixed, raw, taps, part_same, part_other, t_out, u_out, s_out, m_out, q_out, before, state):
     step = pl.program_id(0)
 
     @pl.when(step == 0)
     def _():
         raw[:512, :] = dot(same[...], weights[...], NN)
         raw[512:, :] = dot(other[...], weights[...], NN)
+        taps[...] = gathered_taps(weights)
         before[...] = jnp.zeros_like(before)
         state[...] = jnp.zeros_like(state)
 
@@ -104,7 +120,7 @@
             acts = []
             for part in range(3):
                 cols = slice(384 * h + 128 * part, 384 * h + 128 * part + 128)
-                conv, _ = convolved(raw[rows, cols], prev[:, cols], taps_now[:, cols], marks)
+                conv, _ = convolved(raw[rows, cols], prev[:, cols], taps_of(taps_now, part, h), marks)
                 acts.append(conv * sigmoid(conv))
             q, k, v = acts
             q = q * lax.rsqrt(jnp.sum(q * q, -1, keepdims=True) + EPS)
@@ -152,7 +168,7 @@
     return pl.ds(pl.multiple_of(place[block] * C + start, 8), count)
 
 
-def mix_forward(place, parts, weights, taps, aux, segs, waits, mm=fine):
+def mix_forward(place, parts, weights, aux, segs, waits, mm=fine):
     chunks, steps = 4, 2
     saved = jax.ShapeDtypeStruct((2, 8, C, C), F32)
     block = pl.BlockSpec((2, chunks, C, C), lambda i, place: (0, i, 0, 0))
@@ -166,24 +182,23 @@
                 *[pl.BlockSpec((part.shape[0], D), lambda i, place: (0, 0)) for part in parts],
                 pl.BlockSpec((D, 896), lambda i, place: (0, 0)),
                 *[pl.BlockSpec((D, 128), lambda i, place, n=n: (0, 7 + n)) for n in range(2)],
-                pl.BlockSpec((4, 768), lambda i, place: (0, 0)),
                 pl.BlockSpec((chunks * C, 128), lambda i, place: (i, 0)),
                 pl.BlockSpec((1, chunks, 128), lambda i, place: (i, 0, 0)),
                 *[pl.BlockSpec(memory_space=pl.ANY) for _ in waits],
             ],
-            out_specs=[rows(256), rows(896)]
+            out_specs=[rows(256), rows(896), pl.BlockSpec((32, C), lambda i, place: (0, 0))]
             + [pl.BlockSpec((count, D), lambda i, place: (0, 0)) for count in PARTS]
             + [block] * 5,
             scratch_shapes=[pltpu.VMEM((8, 768), F32), pltpu.VMEM((2, C, C), F32)],
         ),
         out_shape=[jax.ShapeDtypeStruct((1024, 256), BF16)]
-        + [jax.ShapeDtypeStruct((1024, 896), F32)]
+        + [jax.ShapeDtypeStruct((1024, 896), F32), jax.ShapeDtypeStruct((32, C), F32)]
         + [jax.ShapeDtypeStruct((count, D), BF16) for count in PARTS]
         + [saved] * 5,
         compiler_params=pltpu.CompilerParams(vmem_limit_bytes=48 * 1024 * 1024),
         cost_estimate=pl.CostEstimate(flops=20 << 30, bytes_accessed=20 << 20, transcendentals=0),
         name="mix_forward",
-    )(place, *parts, weights, weights, weights, taps, aux, segs.reshape(steps, chunks, 128), *waits)
+    )(place, *parts, weights, weights, weights, aux, segs.reshape(steps, chunks, 128), *waits)
 
 
 def backward_kernel(chunks, mm, place, near, other, out_w, out_w_next, raw, taps, aux, segs, t_in, u_in, s_in, m_in, q_in, back, taps_grad, after, adjoint, grad):
@@ -204,6 +219,7 @@
         back[:, 768:] = jnp.zeros_like(back[:, 768:])
 
     row, col = masks()
+    taps_now = taps[...]
     taps_sum = [[jnp.zeros((1, 128), F32) for _ in range(4)] for _ in range(6)]
     items = []
     for c in range(chunks):
@@ -220,7 +236,7 @@
             for part in range(3):
                 cols = slice(384 * h + 128 * part, 384 * h + 128 * part + 128)
                 now = raw[rows, cols]
-                conv, terms = convolved(now, prev[:, cols], taps[:, cols], marks)
+                conv, terms = convolved(now, prev[:, cols], taps_of(taps_now, part, h), marks)
                 s = sigmoid(conv)
                 acts.append(conv * s)
                 slopes.append(s * (1.0 + conv * (1.0 - s)))
@@ -266,7 +282,8 @@
             d = backs[part] * slopes[part]
             cols = slice(384 * h + part * 128, 384 * h + part * 128 + 128)
             sums = taps_sum[3 * h + part]
-            total = taps[0:1, cols] * d
+            taps_here = taps_of(taps_now, part, h)
+            total = taps_here[0] * d
             sums[0] += jnp.sum(d * moved[part][0], 0, keepdims=True)
             for offset in range(1, 4):
                 sums[offset] += jnp.sum(d * moved[part][offset], 0, keepdims=True)
@@ -274,11 +291,12 @@
                 joined = jnp.concatenate([marked, after[offset - 1, :, cols]], 0)
                 after[offset - 1, :, cols] = marked[:8]
                 up = pltpu.roll(joined, C + 8 - offset, 0)[:C]
-                total = total + taps[offset : offset + 1, cols] * up
+                total = total + taps_here[offset] * up
             back[rows, cols] = total.astype(BF16)
-    for part in range(6):
+    for n in range(6):
         for offset in range(4):
-            taps_grad[offset : offset + 1, part * 128 : part * 128 + 128] += taps_sum[part][offset]
+            at = (n % 3 * 4 + offset) * 2 + n // 3
+            taps_grad[at : at + 1, :] += taps_sum[n][offset]
 
 
 def mix_backward(place, three, weights, raw, taps, aux, segs, saved, mm=fine):
@@ -294,19 +312,19 @@
             + [pl.BlockSpec((D, 128), lambda i, place, n=n: (0, 7 + n)) for n in range(2)]
             + [
                 rows(896),
-                pl.BlockSpec((4, 768), lambda i, place: (0, 0)),
+                pl.BlockSpec((32, C), lambda i, place: (0, 0)),
                 pl.BlockSpec((chunks * C, 128), lambda i, place: (steps - 1 - i, 0)),
                 pl.BlockSpec((1, chunks, 128), lambda i, place: (steps - 1 - i, 0, 0)),
             ]
             + [block] * 5,
-            out_specs=[rows(896), pl.BlockSpec((4, 768), lambda i, place: (0, 0))],
+            out_specs=[rows(896), pl.BlockSpec((32, C), lambda i, place: (0, 0))],
             scratch_shapes=[
                 pltpu.VMEM((3, 8, 768), F32),
                 pltpu.VMEM((2, C, C), F32),
                 pltpu.VMEM((1024, 256), F32),
             ],
         ),
-        out_shape=[jax.ShapeDtypeStruct((1024, 896), BF16), jax.ShapeDtypeStruct((4, 768), F32)],
+        out_shape=[jax.ShapeDtypeStruct((1024, 896), BF16), jax.ShapeDtypeStruct((32, C), F32)],
         compiler_params=pltpu.CompilerParams(vmem_limit_bytes=60 * 1024 * 1024),
         cost_estimate=pl.CostEstimate(flops=25 << 30, bytes_accessed=20 << 20, transcendentals=0),
         name="mix_backward",
@@ -450,6 +468,10 @@
     put(out, grad[...] + norm_back(value * scale, scale, scaled), HOME)
 
 
+def widen_kernel(rows, out):
+    out[...] = rows[...].astype(F32)
+
+
 def result_kernel(middle, own, up_high, up_low, down_high, down_low, out):
     put(out, middle[...] + landed(own, up_high, up_low, down_high, down_low), HOME)
 
@@ -463,7 +485,8 @@
     out[:24, 776:784] = taps[...]
     out[:, 784:792] = segs[...].astype(F32).T.astype(BF16)
     out[:, 896:1152] = out_w[...].astype(F32).T.astype(BF16)
-    gains[...] = jnp.concatenate([gain_one[...], gain_two[...]], 0)
+    for n in range(16):
+        gains[n] = jnp.concatenate([gain_one[...], gain_two[...]], 0)
     out[:, 1152:] = tokens[...]
 
 
@@ -492,22 +515,13 @@
         out[:, at + 512 : at + 768] = pack[:, at + 512 : at + 768]
 
 
-def ffn_sums_kernel(grads, weights, out, copy):
-    copy[...] = grads[...]
-    total = jnp.zeros((128, 1), F32)
-    for j in range(3):
-        here = slice(768 * j, 768 * j + 512)
-        total = total + jnp.sum(grads[:, here].astype(F32) * weights[:, here].astype(F32), 1, keepdims=True)
-    out[...] = total.reshape(1, 128)
-
-
 def ffn_unpack_kernel(pack, gain, gate, up, down):
     for n, ref in enumerate((gate, up, down)):
-        for j in range(3):
-            count = min(256, HID - 256 * j)
-            at = 768 * j + 256 * n
-            value = pack[:, at : at + 256].astype(F32).T[:count]
-            ref[256 * j : 256 * j + count, :] = value if n == 2 else value * gain[...]
+        for block in range(6):
+            count = min(128, HID - 128 * block)
+            at = 1040 + 768 * (block // 2) + 256 * n + 128 * (block % 2)
+            value = pack[at : at + 128, :].astype(F32).T[:count]
+            ref[128 * block : 128 * block + count, :] = value if n == 2 else value * gain[...]
 
 
 def mix_unpack_kernel(pack, gain, query, key, value, beta, taps, out):
@@ -515,9 +529,9 @@
         for n, ref in enumerate((query, key, value)):
             at = 384 * h + 128 * n
             ref[:, h * 128 : h * 128 + 128] = pack[at : at + 128, :].astype(F32) * gain[...]
-    beta[...] = pack[768:770, :].astype(F32) * gain[...].reshape(1, 128)
-    taps[...] = pack[770:772, :].astype(F32)
-    out[...] = pack[784:, :].astype(F32)
+    beta[...] = pack[768:784, :].astype(F32)[:2] * gain[...].reshape(1, 128)
+    taps[...] = pack[768:784, :].astype(F32)[2:10]
+    out[...] = pack[784:1040, :].astype(F32)
 
 
 def cross_kernel(same, other, own, up, down, after_high, after_low, before_high, before_low):
@@ -564,14 +578,10 @@
     )
     up, down = ahead(up), behind(down)
     after_low, before_high = ahead(after_low), behind(before_high)
-    passed, before_low = local_call(
+    after_high, before_low = local_call(
         pass_kernel, "pass_sum", [((64, D), BF16)] * 2, after_high, up, before_low, down
     )
-    return (own, ahead(passed), after_low, before_high, behind(before_low)), passed
-
-
-def gather_rows(rows):
-    return lax.all_gather(rows, TEAM, axis=0, tiled=True)
+    return own, ahead(after_high), after_low, before_high, behind(before_low)
 
 
 def sum_rows(part):
@@ -582,77 +592,85 @@
     return lax.all_gather(rows, RING, axis=0, tiled=True)
 
 
-def swap_ring(part):
-    return lax.all_to_all(part, RING, 0, 0, tiled=True)
-
-
-def total_kernel(parts, pack, out, sums):
+def total_kernel(parts, mix_weights, ffn_grads, ffn_weights, out, sums):
     total = parts[0].astype(F32)
     for n in range(1, 16):
         total = total + parts[n].astype(F32)
-    out[...] = total.astype(BF16)
-    small = pack[:, 768:896].astype(F32).T
+    out[:1040, :] = total.astype(BF16)
+    small = mix_weights[:, 768:896].astype(F32).T
     across = jnp.sum(total[768:770, :] * small[:2], 0, keepdims=True)
     rows = jnp.zeros((128, 1), F32)
     for n in range(6):
         here = slice(128 * n, 128 * n + 128)
-        rows = rows + jnp.sum(total[here, :] * pack[:, here].astype(F32), 1, keepdims=True)
-    sums[...] = across + rows.reshape(1, 128)
-
-
-def matmul(left, right, dims, kind=F32):
-    return lax.dot_general(left, right, dims, preferred_element_type=F32).astype(kind)
+        rows = rows + jnp.sum(total[here, :] * mix_weights[:, here].astype(F32), 1, keepdims=True)
+    sums[0:1, :] = across + rows.reshape(1, 128)
+    rows = jnp.zeros((128, 1), F32)
+    for n in range(18):
+        here = slice(128 * n, 128 * n + 128)
+        grad = ffn_grads[:, here]
+        out[1040 + 128 * n : 1168 + 128 * n, :] = grad
+        if n % 6 < 4:
+            rows = rows + jnp.sum(grad.astype(F32) * ffn_weights[:, here].astype(F32), 1, keepdims=True)
+    sums[1:2, :] = rows.reshape(1, 128)
 
 
 def ffn_kernel(source, *refs):
-    parts, grads, (weights, active, back, second, total) = refs[:2], refs[2:4], refs[4:]
+    parts, grads, stored, (active, back, second), (kept, weights, sems) = refs[:2], refs[2:4], refs[4], refs[5:8], refs[8:]
     step = pl.program_id(0)
-    row = 0
-    for part, grad in zip(parts, grads):
-        count = part.shape[0]
-        here = slice(row, row + count)
-        both = dot(part[...], weights[:, :512], NN)
-        grad_active = dot(grad[...], weights[:, 512:], NN)
-        gate, up = both[:, :256], both[:, 256:]
-        sigma = sigmoid(gate)
-        swish = gate * sigma
-        active[here, :] = (swish * up).astype(BF16)
-        slope = sigma * (1.0 + gate * (1.0 - sigma))
-        backs = jnp.concatenate([grad_active * up * slope, grad_active * swish], 1).astype(BF16)
-        back[here, :] = backs
-        piece = dot(backs, weights[:, :512], NT)
-
-        @pl.when(step == 0)
+
+    def copy(j):
+        return pltpu.make_async_copy(stored.at[:, pl.ds(j * 768, 768)], weights.at[j], sems.at[j])
+
+    @pl.when(step == 0)
+    def _():
+        for j in range(3):
+            copy(j).start()
+
+    for j in range(3):
+
+        @pl.when(step == j)
         def _():
-            total[here, :] = piece
-
-        @pl.when(step == 1)
-        def _():
-            total[here, :] = total[here, :] + piece
-
-        @pl.when(step == 2)
-        def _():
-            done = (total[here, :] + piece).astype(BF16)
-            for n in range(count // C):
-                second[spot(source, row // C + n), :] = done[n * C : n * C + C]
-
-        row += count
+            copy(j).wait()
+            for n, (part, grad) in enumerate(zip(parts, grads)):
+                here = slice(n * 512, n * 512 + 512)
+                both = dot(part[...], weights[j, :, :512], NN)
+                grad_active = dot(grad[...], weights[j, :, 512:], NN)
+                gate, up = both[:, :256], both[:, 256:]
+                sigma = sigmoid(gate)
+                swish = gate * sigma
+                active[here, :] = (swish * up).astype(BF16)
+                slope = sigma * (1.0 + gate * (1.0 - sigma))
+                backs = jnp.concatenate([grad_active * up * slope, grad_active * swish], 1).astype(BF16)
+                back[here, :] = backs
+                kept[here, j * 512 : j * 512 + 512] = backs
+
+    @pl.when(step == 2)
+    def _():
+        every = jnp.concatenate([weights[j, :, :512] for j in range(3)], 1)
+        for n in range(2):
+            done = dot(kept[n * 512 : n * 512 + 512, :], every, NT).astype(BF16)
+            for q in range(4):
+                second[spot(source, n * 4 + q), :] = done[q * C : q * C + C]
 
 
 def ffn(source, parts, grads, weights):
-    whole = [pl.BlockSpec(part.shape, lambda j, source: (0, 0)) for part in parts]
+    whole = [pl.BlockSpec((512, D), lambda j, source: (0, 0))] * 4
     return pl.pallas_call(
         ffn_kernel,
         grid_spec=pltpu.PrefetchScalarGridSpec(
             num_scalar_prefetch=1,
             grid=(3,),
-            in_specs=whole + whole + [pl.BlockSpec((D, 768), lambda j, source: (0, j))],
+            in_specs=whole + [pl.BlockSpec(memory_space=pl.ANY)],
             out_specs=[
                 pl.BlockSpec((1024, 256), lambda j, source: (0, j)),
                 pl.BlockSpec((1024, 512), lambda j, source: (0, j)),
                 pl.BlockSpec((1024, D), lambda j, source: (0, 0)),
             ],
-            scratch_shapes=[pltpu.VMEM((1024, D), F32)],
+            scratch_shapes=[
+                pltpu.VMEM((1024, 1536), BF16),
+                pltpu.VMEM((3, D, 768), BF16),
+                pltpu.SemaphoreType.DMA((3,)),
+            ],
         ),
         out_shape=[
             jax.ShapeDtypeStruct((1024, 768), BF16),
@@ -698,11 +716,15 @@
         outer = outer + dot(mixed[at : at + ref.shape[0], :].T, ref[...], NN)
         at += ref.shape[0]
     small = total[:, 768:].T
+    every = jnp.concatenate([taps[...], jnp.zeros((96, C), F32)], 0).astype(BF16)
+    lane = lax.broadcasted_iota(jnp.int32, (8, C), 1)
     for r in range(4):
         rows = slice(r * 128, r * 128 + 128)
         for n in range(6):
             out[r, n * 128 : n * 128 + 128, :] = total[rows, n * 128 : n * 128 + 128].astype(BF16)
-        tail = jnp.concatenate([small[:2, rows], taps[r], jnp.zeros((12, 128), F32)], 0)
+        chosen = lane == place_of(pl.program_id(0) * 4 + r) * 8 + lax.broadcasted_iota(jnp.int32, (8, C), 0)
+        picked = dot(jnp.where(chosen, 1.0, 0.0).astype(BF16), every, NT)
+        tail = jnp.concatenate([small[:2, rows], picked, jnp.zeros((6, 128), F32)], 0)
         out[r, 768:784, :] = tail.astype(BF16)
         out[r, 784:, :] = outer[:, rows].astype(BF16)
 
@@ -715,7 +737,7 @@
         in_specs=[
             pl.BlockSpec((block, 1024), lambda i: (i, 0)),
             pl.BlockSpec(back.shape, lambda i: (0, 0)),
-            pl.BlockSpec((4, 2, 128), lambda i: (i, 0, 0)),
+            pl.BlockSpec((32, C), lambda i: (0, 0)),
             *[pl.BlockSpec((part.shape[0], block), lambda i: (0, i)) for part in three],
             pl.BlockSpec(mixed.shape, lambda i: (0, 0)),
         ],
@@ -773,20 +795,22 @@
     )(active, weights, weights, weights, wait)
 
 
-def team_total(values, pair):
-    values = values.reshape(4, 2, 16)
-    here = lax.axis_index(pair)
-    mine = lax.dynamic_index_in_dim(values, here, 1, False)
-    other = lax.dynamic_index_in_dim(values, 1 - here, 1, False)
-    mine = mine + lax.ppermute(other, pair, [(0, 1), (1, 0)])
+def team_total(values):
+    values = values.reshape(2, 4, 2, 16)
+    core = lax.axis_index("c")
+    mine = lax.dynamic_index_in_dim(values, core, 2, False)
+    mine = mine + mate(lax.dynamic_index_in_dim(values, 1 - core, 2, False))
     place = lax.axis_index("z")
-
-    def block(distance):
-        return lax.dynamic_index_in_dim(mine, (place + distance) & 3, 0, False)
-
-    total = block(0)
-    for distance in range(1, 4):
-        total = total + lax.ppermute(block(distance), "z", [(n, (n + distance) % 4) for n in range(4)])
+    total = 0.0
+    for distance in range(4):
+        block = lax.dynamic_index_in_dim(mine, (place + distance) & 3, 1, False)
+        pairs = [
+            ((c * 4 + n) * 2 + y, (y * 4 + (n + distance) % 4) * 2 + c)
+            for c in range(2)
+            for n in range(4)
+            for y in range(2)
+        ]
+        total = total + lax.ppermute(block, ("c", "z", "yl"), pairs)
     return total
 
 
@@ -816,7 +840,7 @@
     mix_pack, gains = local_call(
         mix_pack_kernel,
         "mix_pack",
-        [((128, 1152 + D), BF16), ((2, 16), F32)],
+        [((128, 1152 + D), BF16), ((16, 2, 16), F32)],
         w_query,
         w_key,
         w_value,
@@ -836,10 +860,10 @@
     (ffn_pack,) = local_call(ffn_pack_kernel, "ffn_pack", [((128, 2304), BF16)], w_gate.T, w_up.T, w_down, limit=60)
     ffn_pack = trade(ffn_pack)
 
-    gains = jnp.broadcast_to(jnp.concatenate([gains, mate(gains)], 0)[None], (8, 4, 16))
-    gains = lax.all_to_all(gains, ("z", "yl"), 0, 0, tiled=True).transpose(1, 0, 2).reshape(4, 128)
-    home = gains[:2]
-    away = jnp.where(core == lax.axis_index("yl"), gains[:2], gains[2:])
+    gains = lax.all_to_all(gains, ("z", "yl", "c"), 0, 0, tiled=True).reshape(8, 2, 2, 16)
+    gains = gains.transpose(1, 2, 0, 3).reshape(2, 2, 128)
+    home = jnp.where(core == 0, gains[0], gains[1])
+    away = jnp.where(lax.axis_index("yl") == 0, gains[0], gains[1])
     (scaled_pack,) = local_call(mix_scale_kernel, "mix_scale", [((128, 1152), BF16)], mix_pack, away[0][:, None])
     mix_w = gather_ring(scaled_pack)
 
@@ -850,12 +874,10 @@
     )
     ffn_w = gather_ring(scaled_ffn)
 
-    taps = mix_w[:, 768:896].reshape(2, 2, 4, 128, 128)[:, :, :, :24, 8:16].reshape(2, 2, 4, 3, 4, 2, 8)
-    taps = taps.transpose(4, 5, 3, 0, 2, 1, 6).reshape(4, 768).astype(F32)
     marks, seg_rows = local_call(marks_kernel, "marks", [((1024, 128), F32), ((8, 128), F32)], mix_pack)
-    mixed, raw, *saved = mix_forward(place, one, mix_w, taps, marks, seg_rows, (scaled_ffn, grads[1]))
+    mixed, raw, taps, *saved = mix_forward(place, one, mix_w, marks, seg_rows, (scaled_ffn, grads[1]))
     middle, two = local_call(
-        middle_kernel, "middle", [((128, D), F32), ((128, D), BF16)], rows, *sum_team(*saved[:2])[0]
+        middle_kernel, "middle", [((128, D), F32), ((128, D), BF16)], rows, *sum_team(*saved[:2])
     )
     one_turned = turned(one, saved[0])
     two = gather_team(two)
@@ -874,53 +896,46 @@
     ring_grads = lax.psum_scatter(ffn_grads, RING, scatter_dimension=0, tiled=True)
     three = gather_team(three)
     back, taps_grad = mix_backward(place, three, mix_w, raw, taps, marks, seg_rows, saved[2:])
-    taps_grad = taps_grad.reshape(4, 2, 3, 2, 4, 2, 8).transpose(3, 5, 4, 1, 2, 0, 6).reshape(16, 2, 96)
-    taps_grad = jnp.pad(taps_grad, ((0, 0), (0, 0), (0, 32)))
     ring_parts = lax.all_to_all(in_grad(one_turned, back, taps_grad, three, mixed), RING, 0, 0, tiled=True)
-    terms, _ = sum_team(*first_parts(back, mix_w))
+    terms = sum_team(*first_parts(back, mix_w))
     (tokens_grad,) = local_call(first_kernel, "first", [((128, D), BF16)], rows, middle_grad, *terms)
-    terms, passed = sum_team(*result, waits=terms[:1])
+    (tokens_grad,) = local_call(widen_kernel, "widen", [((128, D), F32)], trade(tokens_grad))
+    terms = sum_team(*result, waits=terms[:1])
     (output,) = local_call(result_kernel, "result", [((128, D), BF16)], middle, *terms)
-    ffn_sum, ring_grads = local_call(
-        ffn_sums_kernel,
-        "ffn_sums",
-        [((1, 128), F32), ((128, 2304), BF16)],
+    output = trade(output)
+    total, sums = local_call(
+        total_kernel,
+        "ring_total",
+        [((1040 + 2304, 128), BF16), ((2, 128), F32)],
+        ring_parts,
+        scaled_pack,
         ring_grads,
         scaled_ffn,
-        waits=(passed, tokens_grad),
-    )
+        waits=(tokens_grad, output),
+    )
+    total, sums = trade(total), team_total(sums)
     grad_gate, grad_up, grad_down = local_call(
-        ffn_unpack_kernel, "ffn_unpack", [((HID, 128), F32)] * 3, trade(ring_grads), home[1][None]
-    )
-    mix_grad, sums = local_call(
-        total_kernel,
-        "ring_total",
-        [((1040, 128), BF16), ((1, 128), F32)],
-        ring_parts,
-        scaled_pack,
-        waits=(tokens_grad, ffn_sum),
-    )
-    tokens_grad = trade(tokens_grad).astype(F32)
-    output = trade(output)
+        ffn_unpack_kernel, "ffn_unpack", [((HID, 128), F32)] * 3, total, home[1][None]
+    )
     grad_query, grad_key, grad_value, grad_beta, grad_taps, grad_out = local_call(
         mix_unpack_kernel,
         "mix_unpack",
-        [((128, 256), F32)] * 3 + [((2, 128), F32), ((2, 128), F32), ((256, 128), F32)],
-        trade(mix_grad),
+        [((128, 256), F32)] * 3 + [((2, 128), F32), ((8, 128), F32), ((256, 128), F32)],
+        total,
         home[0][:, None],
     )
-    grad_taps = grad_taps[:, :96].reshape(2, 3, 4, 8).transpose(1, 2, 0, 3)
+    grad_taps = grad_taps[:, :24].reshape(8, 3, 4, 2).transpose(1, 2, 3, 0)
     return (
         output,
         tokens_grad,
-        trade(team_total(sums, "c")) / attn_gain,
+        sums[0] / attn_gain,
         grad_query,
         grad_key,
         grad_value,
         grad_beta.T,
         grad_taps,
         grad_out,
-        trade(team_total(ffn_sum, "c")) / ffn_gain,
+        sums[1] / ffn_gain,
         grad_gate.T,
         grad_up.T,
         grad_down,

time: 449 us -> 434 us (0.967)
  starting transfers between devices: 116 us -> 103 us
  waiting for transfers between devices: 115 us -> 128 us
  Pallas kernels: 165 us -> 158 us
  other arithmetic: 5.91 us -> 1.14 us
    ppermute x9 -> x6, starting transfers between devices: 39.7 us -> 30.6 us  [trade(): return lax.ppermute(value, ('c', 'yl'), [(0, 0), (1, 2), (2, 1), (3, 3)])]
    pallas_call x1, Pallas kernels: 33.7 us -> 26 us  [ffn(): pl.pallas_call(ffn_kernel, grid_spec=pltpu.PrefetchScalarGridSpec(num_sca...]
    ppermute x9 -> x6, waiting for transfers between devices: 25.9 us -> 28.1 us  [trade(): return lax.ppermute(value, ('c', 'yl'), [(0, 0), (1, 2), (2, 1), (3, 3)])]
    unnamed x75 -> x79, local copies, waits for them, and re-layouts: 20.8 us -> 21.3 us
  transfers between devices with their start and end apart: 65 -> 58, of which waited for: 30 -> 28; matrix products, arithmetic and copies ran while one was open for 2% -> 0% of each run, Pallas kernels for 28% -> 29%
where the time goes in v3:
time: 434 us; the launch traced here: 428 us
  Pallas kernels  158 us (36%)
  waiting for transfers between devices  128 us (29%)
  starting transfers between devices  103 us (24%)
  local copies, waits for them, and re-layouts  22.4 us (5%)
  between operations  14.6 us (3%)
    ppermute x17, waiting for transfers between devices, ahead(): return lax.ppermute(value, 'z', [(n, (n + 1) % 4) for n in range(4)])  56.2 us
    ppermute x17, starting transfers between devices, behind(): return lax.ppermute(value, 'z', [(n, (n - 1) % 4) for n in range(4)])  36.1 us
    pallas_call x29, Pallas kernels, local_call(): pl.pallas_call(body, grid=(1,), in_specs=[whole(part.shape) for part in o...  32.3 us
    ppermute x6, starting transfers between devices, trade(): return lax.ppermute(value, ('c', 'yl'), [(0, 0), (1, 2), (2, 1), (3, 3)])  30.6 us
    ppermute x6, waiting for transfers between devices, trade(): return lax.ppermute(value, ('c', 'yl'), [(0, 0), (1, 2), (2, 1), (3, 3)])  28.1 us
    pallas_call x1, Pallas kernels, mix_backward(): pl.pallas_call(functools.partial(backward_kernel, chunks, mm), grid_spec=...  27.6 us
    pallas_call x1, Pallas kernels, ffn(): pl.pallas_call(ffn_kernel, grid_spec=pltpu.PrefetchScalarGridSpec(num_sca...  26 us
    pallas_call x1, Pallas kernels, mix_forward(): pl.pallas_call(functools.partial(forward_kernel, chunks, mm), grid_spec=p...  25.9 us
  transfers between devices with their start and end apart: 58, of which 28 were waited for; matrix products, arithmetic and copies ran while one was open for 0% of the time, Pallas kernels for 29%

profile of v3, /device:TPU:1, one launch (start us, length us, event | category | flops | bytes accessed | tf_op | source)
XLA Modules:
  0.0 427.6 jit_solution(13310161402823461802)
XLA Ops:
  9.6 4.6 %collective-permute-start = (bf16[128,3200]{1,0:T(8,128)(2,1)}, bf16[128,3200]{1,0:T(8,128)(2,1)S(1)}, u32[]{:S(2)}, u32[]{:S(2)}) collective-permute-start(bf16[128,3200]{1,0:T(8,128)(2,1)} %get-tuple-element.88), channel_id=1, source_target_pairs={{0,0},{1,8},{8,1},{9,9},{2,2},{3,10},{10,3},{11,11},{4,4},{5,12},{... | collective-permute-start | bytes 2457608 | tf_op jit(solution)/shard_map/ppermute | solution.py:360
  14.1 5.5 %all-to-all-start = ((f32[16,2,16]{2,1,0:T(2,128)}), f32[16,2,16]{2,1,0:T(2,128)S(1)}, u32[]{:S(2)}, u32[]{:S(2)}) async-start(f32[16,2,16]{2,1,0:T(2,128)} %get-tuple-element.93), calls=%async_computation | async-start | bytes 32768 | tf_op jit(solution)/shard_map/all_to_all | solution.py:863
  19.6 8.4 %all-to-all-done = f32[16,2,16]{2,1,0:T(2,128)S(1)} async-done(((f32[16,2,16]{2,1,0:T(2,128)}), f32[16,2,16]{2,1,0:T(2,128)S(1)}, u32[]{:S(2)}, u32[]{:S(2)}) %all-to-all-start) | async-done | bytes 2080 | tf_op jit(solution)/shard_map/all_to_all | solution.py:863
  34.9 9.7 %collective-permute-done.6.refs_0_ = bf16[128,2304]{1,0:T(8,128)(2,1)S(1)} collective-permute-done((bf16[128,2304]{1,0:T(8,128)(2,1)}, bf16[128,2304]{1,0:T(8,128)(2,1)S(1)}, u32[]{:S(2)}, u32[]{:S(2)}) %collective-permute-start.6) | collective-permute-done | bytes 589856 | tf_op jit(solution)/shard_map/ppermute | solution.py:360
  50.7 7.9 %collective-permute-done.7.refs_0_.refs_1_ = bf16[128,2048]{1,0:T(8,128)(2,1)S(1)} collective-permute-done((bf16[128,2048]{1,0:T(8,128)(2,1)}, bf16[128,2048]{1,0:T(8,128)(2,1)S(1)}, u32[]{:S(2)}, u32[]{:S(2)}) %collective-permute-start.7) | collective-permute-done | bytes 524320 | tf_op jit(solution)/shard_map/ppermute | solution.py:360
  86.6 25.9 %mix_forward.1 = (bf16[1024,256]{1,0:T(8,128)(2,1)S(1)}, f32[1024,896]{1,0:T(8,128)}, f32[32,128]{1,0:T(8,128)S(1)}, bf16[512,2048]{1,0:T(8,128)(2,1)}, bf16[512...) custom-call(s32[8]{0:T(128)S(1)} %fusion.2.place, ...), custom_call_target="tpu_custom_call" | custom-call | flops 21474836480 | bytes 20971520 | tf_op jit(solution)/shard_map/mix_forward/pallas_call | solution.py:176
  143.0 4.4 %collective-permute-done.16.refs_2_ = bf16[64,2048]{1,0:T(8,128)(2,1)S(1)} collective-permute-done((bf16[64,2048]{1,0:T(8,128)(2,1)S(1)}, bf16[64,2048]{1,0:T(8,128)(2,1)S(1)}, u32[]{:S(2)}, u32[]{:S(2)}) %collective-permute-start.16) | collective-permute-done | bytes 262176 | tf_op jit(solution)/shard_map/ppermute | solution.py:368
  150.6 9.8 %collective-permute-done.21.refs_0_.refs_2_ = bf16[128,2048]{1,0:T(8,128)(2,1)S(1)} collective-permute-done((bf16[128,2048]{1,0:T(8,128)(2,1)S(1)}, bf16[128,2048]{1,0:T(8,128)(2,1)S(1)}, u32[]{:S(2)}, u32[]{:S(2)}) %collective-permute-start.21) | collective-permute-done | bytes 524320 | tf_op jit(solution)/shard_map/ppermute | solution.py:368
  175.3 26.0 %ffn.1 = (bf16[1024,768]{1,0:T(8,128)(2,1)}, bf16[1024,1536]{1,0:T(8,128)(2,1)}, bf16[1024,2048]{1,0:T(8,128)(2,1)}) custom-call(s32[8]{0:T(128)} %select_reduce_fusion.source, bf16[512,2048]{1,0:T(8,128)(2,1)} %copy-done.4, bf16[512,2048]{1,0:T(8,128)(2,1)} %collective-permute-done.24.refs_1_, bf16[512,2048]{1,0:T(8,128)(2,1)} %join.5.refs_2_, ...), custom_call_target="tpu_custom_call" | custom-call | flops 16106127360 | bytes 31457280 | tf_op jit(solution)/shard_map/ffn/pallas_call | solution.py:658
  201.5 15.3 %ffn_grad.1.refs_3_ = bf16[2048,2304]{1,0:T(8,128)(2,1)} custom-call(bf16[512,2048]{1,0:T(8,128)(2,1)} %copy-done.4, bf16[512,2048]{1,0:T(8,128)(2,1)} %collective-permute-done.24.refs_1_, bf16[512,2048]{1,0:T(8,128)(2,1)} %join.5.refs_2_, bf16[512,2048]{1,0:T(8,128)(2,1)} %collective-permute-done.12.wait_next.refs_3_, ...), custom_call_target="tpu_custom_call" | custom-call | flops 9663676416 | bytes 20971520 | tf_op jit(solution)/shard_map/ffn_grad/pallas_call | solution.py:698
  216.8 5.3 %turned.1.refs_4_.one = bf16[2048,1024]{1,0:T(8,128)(2,1)} custom-call(bf16[512,2048]{1,0:T(8,128)(2,1)} %copy-done, bf16[512,2048]{1,0:T(8,128)(2,1)} %collective-permute-done.5.other.refs_1_, bf16[512,2048]{1,0:T(8,128)(2,1)} %get-tuple-element.98.refs_0_.refs_2_), custom_call_target="tpu_custom_call" | custom-call | tf_op jit(solution)/shard_map/turned/pallas_call | solution.py:432
  222.1 7.1 %down_product.1 = (bf16[512,2048]{1,0:T(8,128)(2,1)}, bf16[512,2048]{1,0:T(8,128)(2,1)}) custom-call(bf16[1024,768]{1,0:T(8,128)(2,1)} %get-tuple-element.113.active.refs_5_, bf16[2048,2304]{1,0:T(8,128)(2,1)} %all-gather.5.cloned.1.call-done.refs_4_.first.second.third, bf16[2048,2304]{1,0:T(8,128)(2,1)} %all-gather.5.cloned.1.call-done.refs_4_.first.second.third, ...), custom_call_target="tpu_custom_call" | custom-call | flops 3221225472 | bytes 8388608 | tf_op jit(solution)/shard_map/down_product/pallas_call | solution.py:784
  229.3 10.9 %reduce-scatter.3.cloned.1.call-done.refs_2_ = bf16[128,2048]{1,0:T(8,128)(2,1)} async-done(((bf16[1024,2048]{1,0:T(8,128)(2,1)}), bf16[128,2048]{1,0:T(8,128)(2,1)}) %reduce-scatter.3.cloned.1.call-update) | async-done | bytes 524304 | tf_op jit(solution)/shard_map/reduce_scatter | solution.py:588
  247.3 9.4 %collective-permute-done.27.refs_0_.refs_2_ = bf16[128,2048]{1,0:T(8,128)(2,1)S(1)} collective-permute-done((bf16[128,2048]{1,0:T(8,128)(2,1)S(1)}, bf16[128,2048]{1,0:T(8,128)(2,1)S(1)}, u32[]{:S(2)}, u32[]{:S(2)}) %collective-permute-start.27) | collective-permute-done | bytes 524320 | tf_op jit(solution)/shard_map/ppermute | solution.py:368
  260.6 5.0 %collective-permute-done.28.refs_3_ = bf16[64,2048]{1,0:T(8,128)(2,1)S(1)} collective-permute-done((bf16[64,2048]{1,0:T(8,128)(2,1)S(1)}, bf16[64,2048]{1,0:T(8,128)(2,1)S(1)}, u32[]{:S(2)}, u32[]{:S(2)}) %collective-permute-start.28) | collective-permute-done | bytes 262176 | tf_op jit(solution)/shard_map/ppermute | solution.py:368
  274.0 27.6 %mix_backward.1 = (bf16[1024,896]{1,0:T(8,128)(2,1)}, f32[32,128]{1,0:T(8,128)}) custom-call(s32[8]{0:T(128)} %copy-done.25, bf16[512,2048]{1,0:T(8,128)(2,1)} %copy-done.5, bf16[512,2048]{1,0:T(8,128)(2,1)} %copy-done.36, bf16[2048,1152]{1,0:T(8,128)(2,1)} %all-gather.3.cloned.1.call-done.weights.out_w.out_w_next, ...), custom_call_target="tpu_custom_call" | custom-call | flops 26843545600 | bytes 20971520 | tf_op jit(solution)/shard_map/mix_backward/pallas_call | solution.py:306
  301.6 10.3 %in_grad.1 = bf16[16,1040,128]{2,1,0:T(8,128)(2,1)} custom-call(bf16[2048,1024]{1,0:T(8,128)(2,1)} %turned.1.refs_4_.one, bf16[1024,896]{1,0:T(8,128)(2,1)} %get-tuple-element.128.back, f32[32,128]{1,0:T(8,128)} %get-tuple-element.150.taps, bf16[512,2048]{1,0:T(8,128)(2,1)} %copy-done.5, bf16[512,2048]{1,0:T(8,128)(2,1)} %copy-done.36, ...), custom_call_target="tpu_custom_call" | custom-call | flops 4831838208 | bytes 8388608 | tf_op jit(solution)/shard_map/in_grad/pallas_call | solution.py:734
  311.9 7.0 %all-to-all-start.1 = ((bf16[16,1040,128]{2,1,0:T(8,128)(2,1)}), bf16[16,1040,128]{2,1,0:T(8,128)(2,1)}, u32[]{:S(2)}, u32[]{:S(2)}) async-start(bf16[16,1040,128]{2,1,0:T(8,128)(2,1)} %in_grad.1), calls=%async_computation.2 | async-start | bytes 8519680 | tf_op jit(solution)/shard_map/all_to_all | solution.py:899
  318.9 7.9 %first_parts.1 = (bf16[512,2048]{1,0:T(8,128)(2,1)}, bf16[512,2048]{1,0:T(8,128)(2,1)}) custom-call(bf16[1024,896]{1,0:T(8,128)(2,1)} %get-tuple-element.128.back, bf16[2048,1152]{1,0:T(8,128)(2,1)} %all-gather.3.cloned.1.call-done.weights.out_w.out_w_next), custom_call_target="tpu_custom_call" | custom-call | flops 3758096384 | bytes 8388608 | tf_op jit(solution)/shard_map/first_parts/pallas_call | solution.py:762
  327.3 4.7 %collective-permute-done.31.refs_1_ = bf16[512,2048]{1,0:T(8,128)(2,1)S(1)} collective-permute-done((bf16[512,2048]{1,0:T(8,128)(2,1)}, bf16[512,2048]{1,0:T(8,128)(2,1)S(1)}, u32[]{:S(2)}, u32[]{:S(2)}) %collective-permute-start.31) | collective-permute-done | bytes 2097184 | tf_op jit(solution)/shard_map/ppermute | solution.py:364
  364.8 8.3 %collective-permute-start.45 = (bf16[128,2048]{1,0:T(8,128)(2,1)S(1)}, bf16[128,2048]{1,0:T(8,128)(2,1)S(1)}, u32[]{:S(2)}, u32[]{:S(2)}) collective-permute-start(bf16[128,2048]{1,0:T(8,128)(2,1)S(1)} %first.1), channel_id=1, source_target_pairs={{0,0},{1,8},{8,1},{9,9},{2,2},{3,10},{10,3},{11,11},{4,4},{5,12},{... | collective-permute-start | bytes 1572872 | tf_op jit(solution)/shard_map/ppermute | solution.py:360
  375.6 6.6 %collective-permute-start.38 = (bf16[128,2048]{1,0:T(8,128)(2,1)S(1)}, bf16[128,2048]{1,0:T(8,128)(2,1)S(1)}, u32[]{:S(2)}, u32[]{:S(2)}) collective-permute-start(bf16[128,2048]{1,0:T(8,128)(2,1)S(1)} %result.1), channel_id=1, source_target_pairs={{0,0},{1,8},{8,1},{9,9},{2,2},{3,10},{10,3},{11,11},{4,4},{5,12},{... | collective-permute-start | bytes 1572872 | tf_op jit(solution)/shard_map/ppermute | solution.py:360
  383.2 10.5 %collective-permute-done.38.refs_5_ = bf16[128,2048]{1,0:T(8,128)(2,1)S(1)} collective-permute-done((bf16[128,2048]{1,0:T(8,128)(2,1)S(1)}, bf16[128,2048]{1,0:T(8,128)(2,1)S(1)}, u32[]{:S(2)}, u32[]{:S(2)}) %collective-permute-start.38) | collective-permute-done | bytes 524320 | tf_op jit(solution)/shard_map/ppermute | solution.py:360
  399.4 4.4 %collective-permute-start.51 = (bf16[3344,128]{1,0:T(8,128)(2,1)S(1)}, bf16[3344,128]{1,0:T(8,128)(2,1)S(1)}, u32[]{:S(2)}, u32[]{:S(2)}) collective-permute-start(bf16[3344,128]{1,0:T(8,128)(2,1)S(1)} %get-tuple-element.153), channel_id=1, source_target_pairs={{0,0},{1,8},{8,1},{9,9},{2,2},{3,10},{10,3},{11,11},{4,4},{5,12},{... | collective-permute-start | bytes 2568200 | tf_op jit(solution)/shard_map/ppermute | solution.py:360
  (228 shorter events, 170.5 us)
Async XLA Ops:
  9.6 18.6 %collective-permute-start = (bf16[128,3200]{1,0:T(8,128)(2,1)}, bf16[128,3200]{1,0:T(8,128)(2,1)S(1)}, u32[]{:S(2)}, u32[]{:S(2)}) collective-permute-start(bf16[128,3200]{1,0:T(8,128)(2,1)} %get-tuple-element.88), channel_id=1, source_target_pairs={{0,0},{1,8},{8,1},{9,9},{2,2},{3,10},{10,3},{11,11},{4,4},{5,12},{... | collective-permute-start | bytes 2457608 | tf_op jit(solution)/shard_map/ppermute | solution.py:360
  14.1 13.9 %all-to-all-start = ((f32[16,2,16]{2,1,0:T(2,128)}), f32[16,2,16]{2,1,0:T(2,128)S(1)}, u32[]{:S(2)}, u32[]{:S(2)}) async-start(f32[16,2,16]{2,1,0:T(2,128)} %get-tuple-element.93), calls=%async_computation | async-start | bytes 32768 | tf_op jit(solution)/shard_map/all_to_all | solution.py:863
  19.6 65.9 %all-gather.3.cloned.1.call-start = ((), (), s32[]{:S(2)}) async-start(), calls=%async_computation.4 | async-start | bytes 5013504 | tf_op jit(solution)/shard_map/all_gather | solution.py:592
  29.0 146.3 %all-gather.5.cloned.1.call-start = ((), (), s32[]{:S(2)}) async-start(), calls=%async_computation.5 | async-start | bytes 10027008 | tf_op jit(solution)/shard_map/all_gather | solution.py:592
  31.2 13.4 %collective-permute-start.6 = (bf16[128,2304]{1,0:T(8,128)(2,1)}, bf16[128,2304]{1,0:T(8,128)(2,1)S(1)}, u32[]{:S(2)}, u32[]{:S(2)}) collective-permute-start(bf16[128,2304]{1,0:T(8,128)(2,1)} %ffn_pack.1), channel_id=1, source_target_pairs={{0,0},{1,8},{8,1},{9,9},{2,2},{3,10},{10,3},{11,11},{4,4},{5,12},{... | collective-permute-start | bytes 1769480 | tf_op jit(solution)/shard_map/ppermute | solution.py:360
  45.6 194.6 %reduce-scatter.3.cloned.1.call-start = ((), (), s32[]{:S(2)}) async-start(), calls=%async_computation.6 | async-start | bytes 4718592 | tf_op jit(solution)/shard_map/reduce_scatter | solution.py:588
  61.6 12.2 %collective-permute-start.2 = (bf16[128,2048]{1,0:T(8,128)(2,1)S(1)}, bf16[128,2048]{1,0:T(8,128)(2,1)S(1)}, u32[]{:S(2)}, u32[]{:S(2)}) collective-permute-start(bf16[128,2048]{1,0:T(8,128)(2,1)S(1)} %get-tuple-element.90.refs_0_), channel_id=1, source_target_pairs={{0,2},{2,4},{4,6},{6,0},{1,3},{3,5},{5,7},{7,1},{8,10},{10,12},{12... | collective-permute-start | bytes 1572872 | tf_op jit(solution)/shard_map/ppermute | solution.py:368
  61.7 12.1 %collective-permute-start.1 = (bf16[128,2048]{1,0:T(8,128)(2,1)S(1)}, bf16[128,2048]{1,0:T(8,128)(2,1)S(1)}, u32[]{:S(2)}, u32[]{:S(2)}) collective-permute-start(bf16[128,2048]{1,0:T(8,128)(2,1)S(1)} %get-tuple-element.90.refs_0_), channel_id=1, source_target_pairs={{0,6},{2,0},{4,2},{6,4},{1,7},{3,1},{5,3},{7,5},{8,14},{10,8},{12,... | collective-permute-start | bytes 1572872 | tf_op jit(solution)/shard_map/ppermute | solution.py:372
  130.8 12.2 %collective-permute-start.17 = (bf16[64,2048]{1,0:T(8,128)(2,1)}, bf16[64,2048]{1,0:T(8,128)(2,1)S(1)}, u32[]{:S(2)}, u32[]{:S(2)}) collective-permute-start(bf16[64,2048]{1,0:T(8,128)(2,1)} %get-tuple-element.106), channel_id=1, source_target_pairs={{0,2},{2,4},{4,6},{6,0},{1,3},{3,5},{5,7},{7,1},{8,10},{10,12},{12... | collective-permute-start | bytes 786440 | tf_op jit(solution)/shard_map/ppermute | solution.py:368
  130.8 12.2 %collective-permute-start.18 = (bf16[64,2048]{1,0:T(8,128)(2,1)}, bf16[64,2048]{1,0:T(8,128)(2,1)S(1)}, u32[]{:S(2)}, u32[]{:S(2)}) collective-permute-start(bf16[64,2048]{1,0:T(8,128)(2,1)} %get-tuple-element.107), channel_id=1, source_target_pairs={{0,6},{2,0},{4,2},{6,4},{1,7},{3,1},{5,3},{7,5},{8,14},{10,8},{12,... | collective-permute-start | bytes 786440 | tf_op jit(solution)/shard_map/ppermute | solution.py:372
  147.9 12.6 %collective-permute-start.21 = (bf16[128,2048]{1,0:T(8,128)(2,1)S(1)}, bf16[128,2048]{1,0:T(8,128)(2,1)S(1)}, u32[]{:S(2)}, u32[]{:S(2)}) collective-permute-start(bf16[128,2048]{1,0:T(8,128)(2,1)S(1)} %get-tuple-element.110.refs_0_), channel_id=1, source_target_pairs={{0,2},{2,4},{4,6},{6,0},{1,3},{3,5},{5,7},{7,1},{8,10},{10,12},{12... | collective-permute-start | bytes 1572872 | tf_op jit(solution)/shard_map/ppermute | solution.py:368
  147.9 12.5 %collective-permute-start.20 = (bf16[128,2048]{1,0:T(8,128)(2,1)S(1)}, bf16[128,2048]{1,0:T(8,128)(2,1)S(1)}, u32[]{:S(2)}, u32[]{:S(2)}) collective-permute-start(bf16[128,2048]{1,0:T(8,128)(2,1)S(1)} %get-tuple-element.110.refs_0_), channel_id=1, source_target_pairs={{0,6},{2,0},{4,2},{6,4},{1,7},{3,1},{5,3},{7,5},{8,14},{10,8},{12,... | collective-permute-start | bytes 1572872 | tf_op jit(solution)/shard_map/ppermute | solution.py:372
  201.4 192.3 %reduce-scatter.5.cloned.1.call-start = ((), (), s32[]{:S(2)}) async-start(), calls=%async_computation.7 | async-start | bytes 10027008 | tf_op jit(solution)/shard_map/reduce_scatter | solution.py:896
  243.3 13.4 %collective-permute-start.27 = (bf16[128,2048]{1,0:T(8,128)(2,1)S(1)}, bf16[128,2048]{1,0:T(8,128)(2,1)S(1)}, u32[]{:S(2)}, u32[]{:S(2)}) collective-permute-start(bf16[128,2048]{1,0:T(8,128)(2,1)S(1)} %get-tuple-element.118.refs_0_), channel_id=1, source_target_pairs={{0,2},{2,4},{4,6},{6,0},{1,3},{3,5},{5,7},{7,1},{8,10},{10,12},{12... | collective-permute-start | bytes 1572872 | tf_op jit(solution)/shard_map/ppermute | solution.py:368
  244.2 12.6 %collective-permute-start.26 = (bf16[128,2048]{1,0:T(8,128)(2,1)S(1)}, bf16[128,2048]{1,0:T(8,128)(2,1)S(1)}, u32[]{:S(2)}, u32[]{:S(2)}) collective-permute-start(bf16[128,2048]{1,0:T(8,128)(2,1)S(1)} %get-tuple-element.118.refs_0_), channel_id=1, source_target_pairs={{0,6},{2,0},{4,2},{6,4},{1,7},{3,1},{5,3},{7,5},{8,14},{10,8},{12,... | collective-permute-start | bytes 1572872 | tf_op jit(solution)/shard_map/ppermute | solution.py:372
  311.9 81.9 %all-to-all-start.1 = ((bf16[16,1040,128]{2,1,0:T(8,128)(2,1)}), bf16[16,1040,128]{2,1,0:T(8,128)(2,1)}, u32[]{:S(2)}, u32[]{:S(2)}) async-start(bf16[16,1040,128]{2,1,0:T(8,128)(2,1)} %in_grad.1), calls=%async_computation.2 | async-start | bytes 8519680 | tf_op jit(solution)/shard_map/all_to_all | solution.py:899
  327.0 12.9 %collective-permute-start.25 = (bf16[512,2048]{1,0:T(8,128)(2,1)}, bf16[512,2048]{1,0:T(8,128)(2,1)}, u32[]{:S(2)}, u32[]{:S(2)}) collective-permute-start(bf16[512,2048]{1,0:T(8,128)(2,1)} %get-tuple-element.116), channel_id=1, source_target_pairs={{0,8},{8,0},{1,9},{9,1},{2,10},{10,2},{3,11},{11,3},{4,12},{12,4},... | collective-permute-start | bytes 6291464 | tf_op jit(solution)/shard_map/ppermute | solution.py:364
  349.6 14.4 %collective-permute-start.41 = (bf16[64,2048]{1,0:T(8,128)(2,1)S(1)}, bf16[64,2048]{1,0:T(8,128)(2,1)S(1)}, u32[]{:S(2)}, u32[]{:S(2)}) collective-permute-start(bf16[64,2048]{1,0:T(8,128)(2,1)S(1)} %get-tuple-element.146), channel_id=1, source_target_pairs={{0,2},{2,4},{4,6},{6,0},{1,3},{3,5},{5,7},{7,1},{8,10},{10,12},{12... | collective-permute-start | bytes 786440 | tf_op jit(solution)/shard_map/ppermute | solution.py:368
  352.8 20.4 %collective-permute-start.35 = (bf16[64,2048]{1,0:T(8,128)(2,1)}, bf16[64,2048]{1,0:T(8,128)(2,1)S(1)}, u32[]{:S(2)}, u32[]{:S(2)}) collective-permute-start(bf16[64,2048]{1,0:T(8,128)(2,1)} %get-tuple-element.138), channel_id=1, source_target_pairs={{0,2},{2,4},{4,6},{6,0},{1,3},{3,5},{5,7},{7,1},{8,10},{10,12},{12... | collective-permute-start | bytes 786440 | tf_op jit(solution)/shard_map/ppermute | solution.py:368
  358.4 14.8 %collective-permute-start.36 = (bf16[64,2048]{1,0:T(8,128)(2,1)}, bf16[64,2048]{1,0:T(8,128)(2,1)S(1)}, u32[]{:S(2)}, u32[]{:S(2)}) collective-permute-start(bf16[64,2048]{1,0:T(8,128)(2,1)} %get-tuple-element.139), channel_id=1, source_target_pairs={{0,6},{2,0},{4,2},{6,4},{1,7},{3,1},{5,3},{7,5},{8,14},{10,8},{12,... | collective-permute-start | bytes 786440 | tf_op jit(solution)/shard_map/ppermute | solution.py:372
  358.4 16.8 %collective-permute-start.34 = (bf16[64,2048]{1,0:T(8,128)(2,1)S(1)}, bf16[64,2048]{1,0:T(8,128)(2,1)S(1)}, u32[]{:S(2)}, u32[]{:S(2)}) collective-permute-start(bf16[64,2048]{1,0:T(8,128)(2,1)S(1)} %get-tuple-element.137), channel_id=1, source_target_pairs={{0,2},{2,4},{4,6},{6,0},{1,3},{3,5},{5,7},{7,1},{8,10},{10,12},{12... | collective-permute-start | bytes 786440 | tf_op jit(solution)/shard_map/ppermute | solution.py:368
  364.8 17.3 %collective-permute-start.45 = (bf16[128,2048]{1,0:T(8,128)(2,1)S(1)}, bf16[128,2048]{1,0:T(8,128)(2,1)S(1)}, u32[]{:S(2)}, u32[]{:S(2)}) collective-permute-start(bf16[128,2048]{1,0:T(8,128)(2,1)S(1)} %first.1), channel_id=1, source_target_pairs={{0,0},{1,8},{8,1},{9,9},{2,2},{3,10},{10,3},{11,11},{4,4},{5,12},{... | collective-permute-start | bytes 1572872 | tf_op jit(solution)/shard_map/ppermute | solution.py:360
  375.6 18.1 %collective-permute-start.38 = (bf16[128,2048]{1,0:T(8,128)(2,1)S(1)}, bf16[128,2048]{1,0:T(8,128)(2,1)S(1)}, u32[]{:S(2)}, u32[]{:S(2)}) collective-permute-start(bf16[128,2048]{1,0:T(8,128)(2,1)S(1)} %result.1), channel_id=1, source_target_pairs={{0,0},{1,8},{8,1},{9,9},{2,2},{3,10},{10,3},{11,11},{4,4},{5,12},{... | collective-permute-start | bytes 1572872 | tf_op jit(solution)/shard_map/ppermute | solution.py:360
  399.4 18.0 %collective-permute-start.51 = (bf16[3344,128]{1,0:T(8,128)(2,1)S(1)}, bf16[3344,128]{1,0:T(8,128)(2,1)S(1)}, u32[]{:S(2)}, u32[]{:S(2)}) collective-permute-start(bf16[3344,128]{1,0:T(8,128)(2,1)S(1)} %get-tuple-element.153), channel_id=1, source_target_pairs={{0,0},{1,8},{8,1},{9,9},{2,2},{3,10},{10,3},{11,11},{4,4},{5,12},{... | collective-permute-start | bytes 2568200 | tf_op jit(solution)/shard_map/ppermute | solution.py:360
  (73 other events, 773.4 us)
Sparse Core Ops, SparseCore 0:
  29.2 53.7 all-gather.2
  85.1 75.3 all-gather.4
  201.5 38.5 reduce-scatter.2
  243.5 127.4 reduce-scatter.4

commit v4 on v3

--- a/solution.py
+++ b/solution.py
@@ -169,7 +169,7 @@
 
 
 def mix_forward(place, parts, weights, aux, segs, waits, mm=fine):
-    chunks, steps = 4, 2
+    chunks, steps = 8, 1
     saved = jax.ShapeDtypeStruct((2, 8, C, C), F32)
     block = pl.BlockSpec((2, chunks, C, C), lambda i, place: (0, i, 0, 0))
     rows = lambda width: pl.BlockSpec((1024, width), lambda i, place: (0, 0))
@@ -195,7 +195,7 @@
         + [jax.ShapeDtypeStruct((1024, 896), F32), jax.ShapeDtypeStruct((32, C), F32)]
         + [jax.ShapeDtypeStruct((count, D), BF16) for count in PARTS]
         + [saved] * 5,
-        compiler_params=pltpu.CompilerParams(vmem_limit_bytes=48 * 1024 * 1024),
+        compiler_params=pltpu.CompilerParams(vmem_limit_bytes=60 * 1024 * 1024),
         cost_estimate=pl.CostEstimate(flops=20 << 30, bytes_accessed=20 << 20, transcendentals=0),
         name="mix_forward",
     )(place, *parts, weights, weights, weights, aux, segs.reshape(steps, chunks, 128), *waits)
@@ -892,6 +892,7 @@
         grad_rows,
         sum_rows(second),
         waits=(ffn_grads, one_turned, result[0]),
+        limit=60,
     )
     ring_grads = lax.psum_scatter(ffn_grads, RING, scatter_dimension=0, tiled=True)
     three = gather_team(three)
@@ -912,6 +913,7 @@
         ring_grads,
         scaled_ffn,
         waits=(tokens_grad, output),
+        limit=60,
     )
     total, sums = trade(total), team_total(sums)
     grad_gate, grad_up, grad_down = local_call(

time: 434 us -> 427 us (0.984)
  local copies, waits for them, and re-layouts: 22.4 us -> 15.1 us
    unnamed x79 -> x59, local copies, waits for them, and re-layouts: 21.3 us -> 13.3 us
  transfers between devices with their start and end apart: 58 -> 58, of which waited for: 28 -> 28; matrix products, arithmetic and copies ran while one was open for 0% -> 1% of each run, Pallas kernels for 29% -> 30%
where the time goes in v4:
time: 427 us; the launch traced here: 422 us
  Pallas kernels  162 us (38%)
  waiting for transfers between devices  127 us (30%)
  starting transfers between devices  102 us (24%)
  local copies, waits for them, and re-layouts  15.1 us (4%)
  between operations  14.5 us (3%)
    ppermute x17, waiting for transfers between devices, ahead(): return lax.ppermute(value, 'z', [(n, (n + 1) % 4) for n in range(4)])  58 us
    pallas_call x29, Pallas kernels, local_call(): pl.pallas_call(body, grid=(1,), in_specs=[whole(part.shape) for part in o...  36.1 us
    ppermute x17, starting transfers between devices, behind(): return lax.ppermute(value, 'z', [(n, (n - 1) % 4) for n in range(4)])  36 us
    ppermute x6, starting transfers between devices, trade(): return lax.ppermute(value, ('c', 'yl'), [(0, 0), (1, 2), (2, 1), (3, 3)])  29.4 us
    ppermute x6, waiting for transfers between devices, trade(): return lax.ppermute(value, ('c', 'yl'), [(0, 0), (1, 2), (2, 1), (3, 3)])  27.8 us
    pallas_call x1, Pallas kernels, mix_backward(): pl.pallas_call(functools.partial(backward_kernel, chunks, mm), grid_spec=...  27.7 us
    pallas_call x1, Pallas kernels, ffn(): pl.pallas_call(ffn_kernel, grid_spec=pltpu.PrefetchScalarGridSpec(num_sca...  26.6 us
    pallas_call x1, Pallas kernels, mix_forward(): pl.pallas_call(functools.partial(forward_kernel, chunks, mm), grid_spec=p...  25.5 us
  transfers between devices with their start and end apart: 58, of which 28 were waited for; matrix products, arithmetic and copies ran while one was open for 1% of the time, Pallas kernels for 30%

profile of v4, /device:TPU:1, one launch (start us, length us, event | category | flops | bytes accessed | tf_op | source)
XLA Modules:
  0.0 421.6 jit_solution(15994335737853013390)
XLA Ops:
  9.6 4.6 %collective-permute-start = (bf16[128,3200]{1,0:T(8,128)(2,1)}, bf16[128,3200]{1,0:T(8,128)(2,1)S(1)}, u32[]{:S(2)}, u32[]{:S(2)}) collective-permute-start(bf16[128,3200]{1,0:T(8,128)(2,1)} %get-tuple-element.88), channel_id=1, source_target_pairs={{0,0},{1,8},{8,1},{9,9},{2,2},{3,10},{10,3},{11,11},{4,4},{5,12},{... | collective-permute-start | bytes 2457608 | tf_op jit(solution)/shard_map/ppermute | solution.py:360
  14.1 5.5 %all-to-all-start = ((f32[16,2,16]{2,1,0:T(2,128)}), f32[16,2,16]{2,1,0:T(2,128)S(1)}, u32[]{:S(2)}, u32[]{:S(2)}) async-start(f32[16,2,16]{2,1,0:T(2,128)} %get-tuple-element.93), calls=%async_computation | async-start | bytes 32768 | tf_op jit(solution)/shard_map/all_to_all | solution.py:863
  19.6 8.4 %all-to-all-done = f32[16,2,16]{2,1,0:T(2,128)S(1)} async-done(((f32[16,2,16]{2,1,0:T(2,128)}), f32[16,2,16]{2,1,0:T(2,128)S(1)}, u32[]{:S(2)}, u32[]{:S(2)}) %all-to-all-start) | async-done | bytes 2080 | tf_op jit(solution)/shard_map/all_to_all | solution.py:863
  34.9 9.7 %collective-permute-done.6.refs_0_ = bf16[128,2304]{1,0:T(8,128)(2,1)S(1)} collective-permute-done((bf16[128,2304]{1,0:T(8,128)(2,1)}, bf16[128,2304]{1,0:T(8,128)(2,1)S(1)}, u32[]{:S(2)}, u32[]{:S(2)}) %collective-permute-start.6) | collective-permute-done | bytes 589856 | tf_op jit(solution)/shard_map/ppermute | solution.py:360
  50.7 7.9 %collective-permute-done.7.refs_0_.refs_1_ = bf16[128,2048]{1,0:T(8,128)(2,1)S(1)} collective-permute-done((bf16[128,2048]{1,0:T(8,128)(2,1)}, bf16[128,2048]{1,0:T(8,128)(2,1)S(1)}, u32[]{:S(2)}, u32[]{:S(2)}) %collective-permute-start.7) | collective-permute-done | bytes 524320 | tf_op jit(solution)/shard_map/ppermute | solution.py:360
  85.8 25.5 %mix_forward.1 = (bf16[1024,256]{1,0:T(8,128)(2,1)}, f32[1024,896]{1,0:T(8,128)}, f32[32,128]{1,0:T(8,128)}, bf16[512,2048]{1,0:T(8,128)(2,1)}, bf16[512,2048]{1...) custom-call(s32[8]{0:T(128)} %fusion.2.place, ...), custom_call_target="tpu_custom_call" | custom-call | flops 21474836480 | bytes 20971520 | tf_op jit(solution)/shard_map/mix_forward/pallas_call | solution.py:176
  136.3 4.7 %collective-permute-done.16.refs_2_ = bf16[64,2048]{1,0:T(8,128)(2,1)S(1)} collective-permute-done((bf16[64,2048]{1,0:T(8,128)(2,1)S(1)}, bf16[64,2048]{1,0:T(8,128)(2,1)S(1)}, u32[]{:S(2)}, u32[]{:S(2)}) %collective-permute-start.16) | collective-permute-done | bytes 262176 | tf_op jit(solution)/shard_map/ppermute | solution.py:368
  145.2 10.2 %collective-permute-done.21.refs_0_.refs_2_ = bf16[128,2048]{1,0:T(8,128)(2,1)S(1)} collective-permute-done((bf16[128,2048]{1,0:T(8,128)(2,1)S(1)}, bf16[128,2048]{1,0:T(8,128)(2,1)S(1)}, u32[]{:S(2)}, u32[]{:S(2)}) %collective-permute-start.21) | collective-permute-done | bytes 524320 | tf_op jit(solution)/shard_map/ppermute | solution.py:368
  169.9 26.6 %ffn.1 = (bf16[1024,768]{1,0:T(8,128)(2,1)}, bf16[1024,1536]{1,0:T(8,128)(2,1)}, bf16[1024,2048]{1,0:T(8,128)(2,1)}) custom-call(s32[8]{0:T(128)} %select_reduce_fusion.source, bf16[512,2048]{1,0:T(8,128)(2,1)} %copy-done.4, bf16[512,2048]{1,0:T(8,128)(2,1)} %collective-permute-done.24.refs_1_, bf16[512,2048]{1,0:T(8,128)(2,1)} %join.5.refs_2_, ...), custom_call_target="tpu_custom_call" | custom-call | flops 16106127360 | bytes 31457280 | tf_op jit(solution)/shard_map/ffn/pallas_call | solution.py:658
  196.6 15.3 %ffn_grad.1.refs_3_ = bf16[2048,2304]{1,0:T(8,128)(2,1)} custom-call(bf16[512,2048]{1,0:T(8,128)(2,1)} %copy-done.4, bf16[512,2048]{1,0:T(8,128)(2,1)} %collective-permute-done.24.refs_1_, bf16[512,2048]{1,0:T(8,128)(2,1)} %join.5.refs_2_, bf16[512,2048]{1,0:T(8,128)(2,1)} %collective-permute-done.12.wait_next.refs_3_, ...), custom_call_target="tpu_custom_call" | custom-call | flops 9663676416 | bytes 20971520 | tf_op jit(solution)/shard_map/ffn_grad/pallas_call | solution.py:698
  211.9 5.3 %turned.1.refs_4_.one = bf16[2048,1024]{1,0:T(8,128)(2,1)} custom-call(bf16[512,2048]{1,0:T(8,128)(2,1)} %copy-done, bf16[512,2048]{1,0:T(8,128)(2,1)} %collective-permute-done.5.other.refs_1_, bf16[512,2048]{1,0:T(8,128)(2,1)} %get-tuple-element.98.refs_0_.refs_2_), custom_call_target="tpu_custom_call" | custom-call | tf_op jit(solution)/shard_map/turned/pallas_call | solution.py:432
  217.2 7.1 %down_product.1 = (bf16[512,2048]{1,0:T(8,128)(2,1)}, bf16[512,2048]{1,0:T(8,128)(2,1)}) custom-call(bf16[1024,768]{1,0:T(8,128)(2,1)} %get-tuple-element.113.active.refs_5_, bf16[2048,2304]{1,0:T(8,128)(2,1)} %all-gather.5.cloned.1.call-done.refs_4_.first.second.third, bf16[2048,2304]{1,0:T(8,128)(2,1)} %all-gather.5.cloned.1.call-done.refs_4_.first.second.third, ...), custom_call_target="tpu_custom_call" | custom-call | flops 3221225472 | bytes 8388608 | tf_op jit(solution)/shard_map/down_product/pallas_call | solution.py:784
  224.3 9.8 %reduce-scatter.3.cloned.1.call-done.refs_2_ = bf16[128,2048]{1,0:T(8,128)(2,1)} async-done(((bf16[1024,2048]{1,0:T(8,128)(2,1)}), bf16[128,2048]{1,0:T(8,128)(2,1)}) %reduce-scatter.3.cloned.1.call-update) | async-done | bytes 524304 | tf_op jit(solution)/shard_map/reduce_scatter | solution.py:588
  241.1 9.6 %collective-permute-done.27.refs_0_.refs_2_ = bf16[128,2048]{1,0:T(8,128)(2,1)S(1)} collective-permute-done((bf16[128,2048]{1,0:T(8,128)(2,1)}, bf16[128,2048]{1,0:T(8,128)(2,1)S(1)}, u32[]{:S(2)}, u32[]{:S(2)}) %collective-permute-start.27) | collective-permute-done | bytes 524320 | tf_op jit(solution)/shard_map/ppermute | solution.py:368
  254.6 5.1 %collective-permute-done.28.refs_3_ = bf16[64,2048]{1,0:T(8,128)(2,1)S(1)} collective-permute-done((bf16[64,2048]{1,0:T(8,128)(2,1)S(1)}, bf16[64,2048]{1,0:T(8,128)(2,1)S(1)}, u32[]{:S(2)}, u32[]{:S(2)}) %collective-permute-start.28) | collective-permute-done | bytes 262176 | tf_op jit(solution)/shard_map/ppermute | solution.py:368
  269.1 27.7 %mix_backward.1 = (bf16[1024,896]{1,0:T(8,128)(2,1)}, f32[32,128]{1,0:T(8,128)}) custom-call(s32[8]{0:T(128)} %fusion.2.place, bf16[512,2048]{1,0:T(8,128)(2,1)} %copy-done.5, bf16[512,2048]{1,0:T(8,128)(2,1)} %copy-done.25, bf16[2048,1152]{1,0:T(8,128)(2,1)} %all-gather.3.cloned.1.call-done.weights.out_w.out_w_next, ...), custom_call_target="tpu_custom_call" | custom-call | flops 26843545600 | bytes 20971520 | tf_op jit(solution)/shard_map/mix_backward/pallas_call | solution.py:306
  296.8 10.2 %in_grad.1 = bf16[16,1040,128]{2,1,0:T(8,128)(2,1)} custom-call(bf16[2048,1024]{1,0:T(8,128)(2,1)} %turned.1.refs_4_.one, bf16[1024,896]{1,0:T(8,128)(2,1)} %get-tuple-element.128.back, f32[32,128]{1,0:T(8,128)} %get-tuple-element.150.taps, bf16[512,2048]{1,0:T(8,128)(2,1)} %copy-done.5, bf16[512,2048]{1,0:T(8,128)(2,1)} %copy-done.25, ...), custom_call_target="tpu_custom_call" | custom-call | flops 4831838208 | bytes 8388608 | tf_op jit(solution)/shard_map/in_grad/pallas_call | solution.py:734
  307.0 7.0 %all-to-all-start.1 = ((bf16[16,1040,128]{2,1,0:T(8,128)(2,1)}), bf16[16,1040,128]{2,1,0:T(8,128)(2,1)}, u32[]{:S(2)}, u32[]{:S(2)}) async-start(bf16[16,1040,128]{2,1,0:T(8,128)(2,1)} %in_grad.1), calls=%async_computation.2 | async-start | bytes 8519680 | tf_op jit(solution)/shard_map/all_to_all | solution.py:900
  314.0 8.0 %first_parts.1 = (bf16[512,2048]{1,0:T(8,128)(2,1)}, bf16[512,2048]{1,0:T(8,128)(2,1)}) custom-call(bf16[1024,896]{1,0:T(8,128)(2,1)} %get-tuple-element.128.back, bf16[2048,1152]{1,0:T(8,128)(2,1)} %all-gather.3.cloned.1.call-done.weights.out_w.out_w_next), custom_call_target="tpu_custom_call" | custom-call | flops 3758096384 | bytes 8388608 | tf_op jit(solution)/shard_map/first_parts/pallas_call | solution.py:762
  322.5 6.0 %collective-permute-done.31.refs_1_ = bf16[512,2048]{1,0:T(8,128)(2,1)} collective-permute-done((bf16[512,2048]{1,0:T(8,128)(2,1)}, bf16[512,2048]{1,0:T(8,128)(2,1)}, u32[]{:S(2)}, u32[]{:S(2)}) %collective-permute-start.31) | collective-permute-done | bytes 2097184 | tf_op jit(solution)/shard_map/ppermute | solution.py:364
  361.1 7.5 %collective-permute-start.45 = (bf16[128,2048]{1,0:T(8,128)(2,1)S(1)}, bf16[128,2048]{1,0:T(8,128)(2,1)S(1)}, u32[]{:S(2)}, u32[]{:S(2)}) collective-permute-start(bf16[128,2048]{1,0:T(8,128)(2,1)S(1)} %first.1), channel_id=1, source_target_pairs={{0,0},{1,8},{8,1},{9,9},{2,2},{3,10},{10,3},{11,11},{4,4},{5,12},{... | collective-permute-start | bytes 1572872 | tf_op jit(solution)/shard_map/ppermute | solution.py:360
  371.7 6.1 %collective-permute-start.38 = (bf16[128,2048]{1,0:T(8,128)(2,1)S(1)}, bf16[128,2048]{1,0:T(8,128)(2,1)S(1)}, u32[]{:S(2)}, u32[]{:S(2)}) collective-permute-start(bf16[128,2048]{1,0:T(8,128)(2,1)S(1)} %result.1), channel_id=1, source_target_pairs={{0,0},{1,8},{8,1},{9,9},{2,2},{3,10},{10,3},{11,11},{4,4},{5,12},{... | collective-permute-start | bytes 1572872 | tf_op jit(solution)/shard_map/ppermute | solution.py:360
  378.9 10.2 %collective-permute-done.38.refs_5_ = bf16[128,2048]{1,0:T(8,128)(2,1)S(1)} collective-permute-done((bf16[128,2048]{1,0:T(8,128)(2,1)S(1)}, bf16[128,2048]{1,0:T(8,128)(2,1)S(1)}, u32[]{:S(2)}, u32[]{:S(2)}) %collective-permute-start.38) | collective-permute-done | bytes 524320 | tf_op jit(solution)/shard_map/ppermute | solution.py:360
  394.3 4.5 %collective-permute-start.51 = (bf16[3344,128]{1,0:T(8,128)(2,1)}, bf16[3344,128]{1,0:T(8,128)(2,1)S(1)}, u32[]{:S(2)}, u32[]{:S(2)}) collective-permute-start(bf16[3344,128]{1,0:T(8,128)(2,1)} %get-tuple-element.153), channel_id=1, source_target_pairs={{0,0},{1,8},{8,1},{9,9},{2,2},{3,10},{10,3},{11,11},{4,4},{5,12},{... | collective-permute-start | bytes 2568200 | tf_op jit(solution)/shard_map/ppermute | solution.py:360
  (208 shorter events, 164.7 us)
Async XLA Ops:
  9.6 18.6 %collective-permute-start = (bf16[128,3200]{1,0:T(8,128)(2,1)}, bf16[128,3200]{1,0:T(8,128)(2,1)S(1)}, u32[]{:S(2)}, u32[]{:S(2)}) collective-permute-start(bf16[128,3200]{1,0:T(8,128)(2,1)} %get-tuple-element.88), channel_id=1, source_target_pairs={{0,0},{1,8},{8,1},{9,9},{2,2},{3,10},{10,3},{11,11},{4,4},{5,12},{... | collective-permute-start | bytes 2457608 | tf_op jit(solution)/shard_map/ppermute | solution.py:360
  14.1 13.9 %all-to-all-start = ((f32[16,2,16]{2,1,0:T(2,128)}), f32[16,2,16]{2,1,0:T(2,128)S(1)}, u32[]{:S(2)}, u32[]{:S(2)}) async-start(f32[16,2,16]{2,1,0:T(2,128)} %get-tuple-element.93), calls=%async_computation | async-start | bytes 32768 | tf_op jit(solution)/shard_map/all_to_all | solution.py:863
  19.6 66.2 %all-gather.3.cloned.1.call-start = ((), (), s32[]{:S(2)}) async-start(), calls=%async_computation.4 | async-start | bytes 5013504 | tf_op jit(solution)/shard_map/all_gather | solution.py:592
  29.0 140.9 %all-gather.5.cloned.1.call-start = ((), (), s32[]{:S(2)}) async-start(), calls=%async_computation.5 | async-start | bytes 10027008 | tf_op jit(solution)/shard_map/all_gather | solution.py:592
  31.2 13.4 %collective-permute-start.6 = (bf16[128,2304]{1,0:T(8,128)(2,1)}, bf16[128,2304]{1,0:T(8,128)(2,1)S(1)}, u32[]{:S(2)}, u32[]{:S(2)}) collective-permute-start(bf16[128,2304]{1,0:T(8,128)(2,1)} %ffn_pack.1), channel_id=1, source_target_pairs={{0,0},{1,8},{8,1},{9,9},{2,2},{3,10},{10,3},{11,11},{4,4},{5,12},{... | collective-permute-start | bytes 1769480 | tf_op jit(solution)/shard_map/ppermute | solution.py:360
  45.6 188.5 %reduce-scatter.3.cloned.1.call-start = ((), (), s32[]{:S(2)}) async-start(), calls=%async_computation.6 | async-start | bytes 4718592 | tf_op jit(solution)/shard_map/reduce_scatter | solution.py:588
  61.6 12.2 %collective-permute-start.2 = (bf16[128,2048]{1,0:T(8,128)(2,1)S(1)}, bf16[128,2048]{1,0:T(8,128)(2,1)S(1)}, u32[]{:S(2)}, u32[]{:S(2)}) collective-permute-start(bf16[128,2048]{1,0:T(8,128)(2,1)S(1)} %get-tuple-element.90.refs_0_), channel_id=1, source_target_pairs={{0,2},{2,4},{4,6},{6,0},{1,3},{3,5},{5,7},{7,1},{8,10},{10,12},{12... | collective-permute-start | bytes 1572872 | tf_op jit(solution)/shard_map/ppermute | solution.py:368
  123.9 12.4 %collective-permute-start.17 = (bf16[64,2048]{1,0:T(8,128)(2,1)}, bf16[64,2048]{1,0:T(8,128)(2,1)S(1)}, u32[]{:S(2)}, u32[]{:S(2)}) collective-permute-start(bf16[64,2048]{1,0:T(8,128)(2,1)} %get-tuple-element.106), channel_id=1, source_target_pairs={{0,2},{2,4},{4,6},{6,0},{1,3},{3,5},{5,7},{7,1},{8,10},{10,12},{12... | collective-permute-start | bytes 786440 | tf_op jit(solution)/shard_map/ppermute | solution.py:368
  123.9 12.4 %collective-permute-start.18 = (bf16[64,2048]{1,0:T(8,128)(2,1)}, bf16[64,2048]{1,0:T(8,128)(2,1)S(1)}, u32[]{:S(2)}, u32[]{:S(2)}) collective-permute-start(bf16[64,2048]{1,0:T(8,128)(2,1)} %get-tuple-element.107), channel_id=1, source_target_pairs={{0,6},{2,0},{4,2},{6,4},{1,7},{3,1},{5,3},{7,5},{8,14},{10,8},{12,... | collective-permute-start | bytes 786440 | tf_op jit(solution)/shard_map/ppermute | solution.py:372
  142.5 12.9 %collective-permute-start.21 = (bf16[128,2048]{1,0:T(8,128)(2,1)S(1)}, bf16[128,2048]{1,0:T(8,128)(2,1)S(1)}, u32[]{:S(2)}, u32[]{:S(2)}) collective-permute-start(bf16[128,2048]{1,0:T(8,128)(2,1)S(1)} %get-tuple-element.110.refs_0_), channel_id=1, source_target_pairs={{0,2},{2,4},{4,6},{6,0},{1,3},{3,5},{5,7},{7,1},{8,10},{10,12},{12... | collective-permute-start | bytes 1572872 | tf_op jit(solution)/shard_map/ppermute | solution.py:368
  142.5 12.9 %collective-permute-start.20 = (bf16[128,2048]{1,0:T(8,128)(2,1)S(1)}, bf16[128,2048]{1,0:T(8,128)(2,1)S(1)}, u32[]{:S(2)}, u32[]{:S(2)}) collective-permute-start(bf16[128,2048]{1,0:T(8,128)(2,1)S(1)} %get-tuple-element.110.refs_0_), channel_id=1, source_target_pairs={{0,6},{2,0},{4,2},{6,4},{1,7},{3,1},{5,3},{7,5},{8,14},{10,8},{12,... | collective-permute-start | bytes 1572872 | tf_op jit(solution)/shard_map/ppermute | solution.py:372
  196.5 192.6 %reduce-scatter.5.cloned.1.call-start = ((), (), s32[]{:S(2)}) async-start(), calls=%async_computation.7 | async-start | bytes 10027008 | tf_op jit(solution)/shard_map/reduce_scatter | solution.py:897
  237.3 13.4 %collective-permute-start.27 = (bf16[128,2048]{1,0:T(8,128)(2,1)}, bf16[128,2048]{1,0:T(8,128)(2,1)S(1)}, u32[]{:S(2)}, u32[]{:S(2)}) collective-permute-start(bf16[128,2048]{1,0:T(8,128)(2,1)} %get-tuple-element.118.refs_0_), channel_id=1, source_target_pairs={{0,2},{2,4},{4,6},{6,0},{1,3},{3,5},{5,7},{7,1},{8,10},{10,12},{12... | collective-permute-start | bytes 1572872 | tf_op jit(solution)/shard_map/ppermute | solution.py:368
  238.1 12.6 %collective-permute-start.26 = (bf16[128,2048]{1,0:T(8,128)(2,1)}, bf16[128,2048]{1,0:T(8,128)(2,1)S(1)}, u32[]{:S(2)}, u32[]{:S(2)}) collective-permute-start(bf16[128,2048]{1,0:T(8,128)(2,1)} %get-tuple-element.118.refs_0_), channel_id=1, source_target_pairs={{0,6},{2,0},{4,2},{6,4},{1,7},{3,1},{5,3},{7,5},{8,14},{10,8},{12,... | collective-permute-start | bytes 1572872 | tf_op jit(solution)/shard_map/ppermute | solution.py:372
  307.0 82.1 %all-to-all-start.1 = ((bf16[16,1040,128]{2,1,0:T(8,128)(2,1)}), bf16[16,1040,128]{2,1,0:T(8,128)(2,1)}, u32[]{:S(2)}, u32[]{:S(2)}) async-start(bf16[16,1040,128]{2,1,0:T(8,128)(2,1)} %in_grad.1), calls=%async_computation.2 | async-start | bytes 8519680 | tf_op jit(solution)/shard_map/all_to_all | solution.py:900
  322.4 12.8 %collective-permute-start.25 = (bf16[512,2048]{1,0:T(8,128)(2,1)}, bf16[512,2048]{1,0:T(8,128)(2,1)S(1)}, u32[]{:S(2)}, u32[]{:S(2)}) collective-permute-start(bf16[512,2048]{1,0:T(8,128)(2,1)} %get-tuple-element.116), channel_id=1, source_target_pairs={{0,8},{8,0},{1,9},{9,1},{2,10},{10,2},{3,11},{11,3},{4,12},{12,4},... | collective-permute-start | bytes 6291464 | tf_op jit(solution)/shard_map/ppermute | solution.py:364
  333.2 12.8 %collective-permute-start.40 = (bf16[64,2048]{1,0:T(8,128)(2,1)}, bf16[64,2048]{1,0:T(8,128)(2,1)S(1)}, u32[]{:S(2)}, u32[]{:S(2)}) collective-permute-start(bf16[64,2048]{1,0:T(8,128)(2,1)} %get-tuple-element.145), channel_id=1, source_target_pairs={{0,6},{2,0},{4,2},{6,4},{1,7},{3,1},{5,3},{7,5},{8,14},{10,8},{12,... | collective-permute-start | bytes 786440 | tf_op jit(solution)/shard_map/ppermute | solution.py:372
  346.1 14.2 %collective-permute-start.41 = (bf16[64,2048]{1,0:T(8,128)(2,1)S(1)}, bf16[64,2048]{1,0:T(8,128)(2,1)S(1)}, u32[]{:S(2)}, u32[]{:S(2)}) collective-permute-start(bf16[64,2048]{1,0:T(8,128)(2,1)S(1)} %get-tuple-element.146), channel_id=1, source_target_pairs={{0,2},{2,4},{4,6},{6,0},{1,3},{3,5},{5,7},{7,1},{8,10},{10,12},{12... | collective-permute-start | bytes 786440 | tf_op jit(solution)/shard_map/ppermute | solution.py:368
  349.0 19.5 %collective-permute-start.35 = (bf16[64,2048]{1,0:T(8,128)(2,1)}, bf16[64,2048]{1,0:T(8,128)(2,1)S(1)}, u32[]{:S(2)}, u32[]{:S(2)}) collective-permute-start(bf16[64,2048]{1,0:T(8,128)(2,1)} %get-tuple-element.138), channel_id=1, source_target_pairs={{0,2},{2,4},{4,6},{6,0},{1,3},{3,5},{5,7},{7,1},{8,10},{10,12},{12... | collective-permute-start | bytes 786440 | tf_op jit(solution)/shard_map/ppermute | solution.py:368
  354.7 13.9 %collective-permute-start.36 = (bf16[64,2048]{1,0:T(8,128)(2,1)}, bf16[64,2048]{1,0:T(8,128)(2,1)S(1)}, u32[]{:S(2)}, u32[]{:S(2)}) collective-permute-start(bf16[64,2048]{1,0:T(8,128)(2,1)} %get-tuple-element.139), channel_id=1, source_target_pairs={{0,6},{2,0},{4,2},{6,4},{1,7},{3,1},{5,3},{7,5},{8,14},{10,8},{12,... | collective-permute-start | bytes 786440 | tf_op jit(solution)/shard_map/ppermute | solution.py:372
  354.7 16.7 %collective-permute-start.34 = (bf16[64,2048]{1,0:T(8,128)(2,1)S(1)}, bf16[64,2048]{1,0:T(8,128)(2,1)S(1)}, u32[]{:S(2)}, u32[]{:S(2)}) collective-permute-start(bf16[64,2048]{1,0:T(8,128)(2,1)S(1)} %get-tuple-element.137), channel_id=1, source_target_pairs={{0,2},{2,4},{4,6},{6,0},{1,3},{3,5},{5,7},{7,1},{8,10},{10,12},{12... | collective-permute-start | bytes 786440 | tf_op jit(solution)/shard_map/ppermute | solution.py:368
  361.1 16.8 %collective-permute-start.45 = (bf16[128,2048]{1,0:T(8,128)(2,1)S(1)}, bf16[128,2048]{1,0:T(8,128)(2,1)S(1)}, u32[]{:S(2)}, u32[]{:S(2)}) collective-permute-start(bf16[128,2048]{1,0:T(8,128)(2,1)S(1)} %first.1), channel_id=1, source_target_pairs={{0,0},{1,8},{8,1},{9,9},{2,2},{3,10},{10,3},{11,11},{4,4},{5,12},{... | collective-permute-start | bytes 1572872 | tf_op jit(solution)/shard_map/ppermute | solution.py:360
  371.7 17.4 %collective-permute-start.38 = (bf16[128,2048]{1,0:T(8,128)(2,1)S(1)}, bf16[128,2048]{1,0:T(8,128)(2,1)S(1)}, u32[]{:S(2)}, u32[]{:S(2)}) collective-permute-start(bf16[128,2048]{1,0:T(8,128)(2,1)S(1)} %result.1), channel_id=1, source_target_pairs={{0,0},{1,8},{8,1},{9,9},{2,2},{3,10},{10,3},{11,11},{4,4},{5,12},{... | collective-permute-start | bytes 1572872 | tf_op jit(solution)/shard_map/ppermute | solution.py:360
  394.3 17.1 %collective-permute-start.51 = (bf16[3344,128]{1,0:T(8,128)(2,1)}, bf16[3344,128]{1,0:T(8,128)(2,1)S(1)}, u32[]{:S(2)}, u32[]{:S(2)}) collective-permute-start(bf16[3344,128]{1,0:T(8,128)(2,1)} %get-tuple-element.153), channel_id=1, source_target_pairs={{0,0},{1,8},{8,1},{9,9},{2,2},{3,10},{10,3},{11,11},{4,4},{5,12},{... | collective-permute-start | bytes 2568200 | tf_op jit(solution)/shard_map/ppermute | solution.py:360
  (63 other events, 535.1 us)
Sparse Core Ops, SparseCore 0:
  29.2 53.7 all-gather.2
  85.1 75.1 all-gather.4
  196.6 37.4 reduce-scatter.2
  237.5 128.8 reduce-scatter.4
